TPU v7x, 32 devices: a whole 2x2x4 slice. The times are simulated.
32 devices in a mesh: row: 8 (over y, x, core), col: 4 (over z).
Axes of the slice: x: 2, y: 2, z: 4, core: 2. Of those that a mesh axis runs over, the one named last changes fastest.
Arguments:
- mask_logits: float32 [1024, 512], P('row', 'col'), may hold values from -6 to 6
- target: float32 [1024, 512], P('row', 'col'), may hold values from 0 to 1
- weight: float32 [1024, 512], P('row', 'col'), may hold values from 0.004 to 10, as said below
- kernels: float32 [2, 12288], P(None, ('row', 'col')), may hold values from -3 to 3
Outputs:
- new_logits: float32 [1024, 512], P('row', 'col')
- loss_value: float32 [], replicated
Inputs may be any that keep to these rules, and one draw needn't show every extreme that they name: `weight`: positive loss weights.
All inputs are finite; a program needn't handle non-finite values.
Results may differ from a plain program's by a relative error of at most 0.0003.
Values sent between devices are 32-bit elements; how exact they have to be, the bound alone decides.
No kernel may reach another device: no remote copies, remote signals or barrier semaphores. Data moves between devices by JAX's collectives and lax.ppermute only.
A program may use at most 64 MiB of HBM per device.

v0:
```python
import math

import jax
import jax.numpy as jnp
from jax import lax
from jax.sharding import PartitionSpec as P

HALO = 64
KERNELS = 6
BAND = 32
CONDITIONS = 2


SHARPNESS = 6.0
THRESHOLD = 0.75
STEP = 0.5
EPSILON = 1e-06
DOSES = (1.0, 1.15)


def padded_2(block, sides, width):
    for axis, dim in sides:
        count = lax.axis_size(axis)
        forward = [(i, i + 1) for i in range(count - 1)]
        backward = [(target, source) for source, target in forward]
        low = lax.ppermute(
            lax.slice_in_dim(block, block.shape[dim] - width, None, axis=dim), axis, forward
        )
        high = lax.ppermute(lax.slice_in_dim(block, 0, width, axis=dim), axis, backward)
        block = jnp.concatenate([low, block, high], axis=dim)
    return block


def matmul(first, second):
    return jnp.matmul(
        first, second, precision=lax.Precision.HIGHEST, preferred_element_type=jnp.float32
    )


def cmatmul(first_re, first_im, second_re, second_im):
    return (
        matmul(first_re, second_re) - matmul(first_im, second_im),
        matmul(first_re, second_im) + matmul(first_im, second_re),
    )


def dft_rows(band, pad_width):
    freq = jnp.arange(band, dtype=jnp.int32) - band // 2
    place = jnp.arange(pad_width, dtype=jnp.int32)
    turns = (freq[:, None] * place[None, :] % pad_width).astype(jnp.float32) * (
        2.0 * math.pi / pad_width
    )
    factor = 1.0 / math.sqrt(pad_width)
    return (jnp.cos(turns) * factor, -jnp.sin(turns) * factor)


def synthesize(spec_re, spec_im, wave_re, wave_im):
    left_re, left_im = cmatmul(wave_re.T, -wave_im.T, spec_re, spec_im)
    return cmatmul(left_re, left_im, wave_re, -wave_im)


def analyse(cell_re, cell_im, wave_re, wave_im):
    left_re, left_im = cmatmul(wave_re, wave_im, cell_re, cell_im)
    return cmatmul(left_re, left_im, wave_re.T, wave_im.T)


def tile_terms(padded_tile, kernel_re, kernel_im, wave_re, wave_im, dose, margin):
    mask_tile, target_tile, weight_tile = (padded_tile[0], padded_tile[1], padded_tile[2])
    pad_width = mask_tile.shape[0]
    core_width = pad_width - 2 * margin
    four_re, four_im = cmatmul(
        matmul(wave_re, mask_tile), matmul(wave_im, mask_tile), wave_re.T, wave_im.T
    )
    prod_re = four_re[None] * kernel_re - four_im[None] * kernel_im
    prod_im = four_re[None] * kernel_im + four_im[None] * kernel_re
    fields_re, fields_im = synthesize(prod_re, prod_im, wave_re, wave_im)
    intensity = jnp.sum(fields_re * fields_re + fields_im * fields_im, axis=0)
    resist = jax.nn.sigmoid(SHARPNESS * (dose * intensity - THRESHOLD))
    error_map = resist - target_tile
    inner = (weight_tile * error_map * error_map)[
        margin : margin + core_width, margin : margin + core_width
    ]
    tile_loss = jnp.sum(inner)
    slope_map = 2.0 * SHARPNESS * dose * weight_tile * error_map * resist * (1.0 - resist)
    back_re, back_im = analyse(
        slope_map[None] * fields_re, slope_map[None] * fields_im, wave_re, wave_im
    )
    sum_re = jnp.sum(kernel_re * back_re + kernel_im * back_im, axis=0)
    sum_im = jnp.sum(kernel_re * back_im - kernel_im * back_re, axis=0)
    core_re = wave_re[:, margin : margin + core_width]
    core_im = wave_im[:, margin : margin + core_width]
    left_re, left_im = cmatmul(core_re.T, -core_im.T, sum_re, sum_im)
    real_part = matmul(left_re, core_re) + matmul(left_im, core_im)
    return (2.0 * real_part, tile_loss)


def shards(mask_logits, target, weight, kernels):
    mask_cells = jax.nn.sigmoid(mask_logits)
    stacked = jnp.stack([mask_cells, target, weight])
    padded = padded_2(stacked, (("row", 1), ("col", 2)), HALO)
    core_width = mask_logits.shape[0]
    tile_count = mask_logits.shape[1] // core_width
    pad_width = core_width + 2 * HALO
    wave_re, wave_im = dft_rows(BAND, pad_width)
    whole_bank = lax.all_gather(kernels, ("row", "col"), axis=1, tiled=True)
    tile_grads = [jnp.zeros((core_width, core_width), jnp.float32)]
    loss_global = jnp.float32(0.0)
    for condition in range(CONDITIONS):
        flat_bank = whole_bank[condition]
        spectra = flat_bank.reshape(2, KERNELS, BAND, BAND)
        condition_loss = jnp.float32(0.0)
        part_grad, part_loss = tile_terms(
            padded, spectra[0], spectra[1], wave_re, wave_im, DOSES[condition], HALO
        )
        tile_grads[0] = tile_grads[0] + part_grad
        condition_loss = part_loss
        loss_global = loss_global + lax.psum(condition_loss, ("row", "col"))
    grad_cells = tile_grads[0] * mask_cells * (1.0 - mask_cells)
    square_local = jnp.sum(grad_cells * grad_cells)
    square_global = lax.psum(square_local, ("row", "col"))
    cell_count = lax.axis_size("row") * core_width * lax.axis_size("col") * core_width * tile_count
    loss_value = loss_global / cell_count
    norm_value = jnp.sqrt(square_global / cell_count + EPSILON)
    return (mask_logits - STEP * grad_cells / norm_value, loss_value)


def solution(mesh):
    placed = (P("row", "col"), P("row", "col"), P("row", "col"), P(None, ("row", "col")))
    return jax.shard_map(
        shards, mesh=mesh, in_specs=placed, out_specs=(P("row", "col"), P()), check_vma=False
    )
```

profile of v0, /device:TPU:0, one launch (start us, length us, event | category | flops | bytes accessed | tf_op | source)
XLA Modules:
  0.0 186.7 jit_solution(1945341854920983822)
XLA Ops:
  0.7 0.9 fusion.144
  1.6 0.9 pad_maximum_fusion.2
  2.5 1.3 collective-permute-start.1
  3.8 3.0 %collective-permute-start = (f32[3,64,128]{2,1,0:T(8,128)S(1)}, f32[3,64,128]{2,1,0:T(8,128)S(1)}, u32[]{:S(2)}, u32[]{:S(2)}) collective-permute-start(f32[3,64,128]{2,1,0:T(8,128)S(1)} %get-tuple-element.24), channel_id=1, source_target_pairs={{0,4},{4,8},{8,12},{12,16},{16,20},{20,24},{24,28},{1,5},{5,9},{9,... | collective-permute-start | bytes 294920 | tf_op jit(solution)/shard_map/ppermute | solution.py:26
  6.8 70.2 %all_gather.3 = f32[2,12288]{1,0:T(2,128)S(1)} all-gather(f32[2,384]{1,0:T(2,128)} %param.7), channel_id=1, replica_groups=mesh['row'=8,'col'=4] {'row','col'}, dimensions={1}, use_global_device_ids=true | all-gather | bytes 101376 | tf_op jit(solution)/shard_map/all_gather | solution.py:105
  77.9 1.3 collective-permute-start.3
  79.2 4.6 %collective-permute-start.2 = (f32[3,256,64]{2,1,0:T(8,128)S(1)}, f32[3,256,64]{2,1,0:T(8,128)S(1)}, u32[]{:S(2)}, u32[]{:S(2)}) collective-permute-start(f32[3,256,64]{2,1,0:T(8,128)S(1)} %get-tuple-element.18), channel_id=1, source_target_pairs={{0,1},{1,2},{2,3},{4,5},{5,6},{6,7},{8,9},{9,10},{10,11},{12,13},{... | collective-permute-start | bytes 589832 | tf_op jit(solution)/shard_map/ppermute | solution.py:26
  83.8 0.8 negate_multiply_fusion
  84.6 3.0 %collective-permute-done.3 = f32[3,256,64]{2,1,0:T(8,128)S(1)} collective-permute-done((f32[3,256,64]{2,1,0:T(8,128)S(1)}, f32[3,256,64]{2,1,0:T(8,128)S(1)}, u32[]{:S(2)}, u32[]{:S(2)}) %collective-permute-start.3) | collective-permute-done | bytes 196640 | tf_op jit(solution)/shard_map/ppermute | solution.py:29
  87.6 1.5 collective-permute-done.2
  92.2 0.7 multiply_add_fusion
  93.0 0.5 fusion.136
  93.6 0.5 fusion.140
  94.2 0.5 fusion.141
  94.7 0.5 fusion.134
  95.2 1.6 fusion.70
  96.8 2.5 %fusion.68 = f32[6,256,256]{2,1,0:T(8,128)S(1)} fusion(f32[256,6,32]{0,2,1:T(8,128)S(1)} %bitcast.208, f32[256,6,32]{0,2,1:T(8,128)} %bitcast.206, s32[32]{0:T(128)S(1)} %iota_add_fusion), kind=kOutput, calls=%fused_computation.84 | convolution fusion | flops 151183360 | bytes 1966208 | tf_op jit(solution)/shard_map/dot_general | solution.py:35
  99.3 1.6 copy.11
  100.9 2.1 %fusion.132 = f32[256,192]{0,1} fusion(f32[32,192]{0,1:T(8,128)} %bitcast.215, s32[32]{0:T(128)S(1)} %iota_add_fusion), kind=kOutput, calls=%fused_computation.174 | convolution fusion | flops 19013632 | bytes 221312
  103.0 2.1 %fusion.139 = f32[256,192]{0,1} fusion(f32[32,192]{0,1:T(8,128)} %bitcast.216, s32[32]{0:T(128)S(1)} %iota_add_fusion), kind=kOutput, calls=%fused_computation.178 | convolution fusion | flops 18997248 | bytes 221312
  105.0 1.6 copy.10
  106.7 1.4 fusion.138
  108.1 1.4 fusion.130
  109.5 2.5 %fusion.64 = f32[6,256,256]{2,1,0:T(8,128)S(1)} fusion(f32[256,6,32]{0,2,1:T(8,128)S(1)} %bitcast.209, f32[256,6,32]{0,2,1:T(8,128)} %bitcast.203, s32[32]{0:T(128)S(1)} %iota_add_fusion), kind=kOutput, calls=%fused_computation.80 | convolution fusion | flops 151166976 | bytes 1966208 | tf_op jit(solution)/shard_map/dot_general | solution.py:35
  112.0 1.6 fusion.62
  113.6 1.8 convolution_subtract_fusion.1
  115.4 1.7 add_reduce_fusion.1
  117.1 1.6 convolution_subtract_fusion
  118.7 1.7 add_reduce_fusion
  120.6 1.2 fusion.10
  121.9 1.2 fusion.8
  123.1 1.3 fusion.19
  124.4 0.5 fusion.97
  125.4 1.2 fusion.2
  126.7 1.5 fusion
  128.1 1.3 fusion.31
  129.4 0.5 fusion.92
  129.9 0.5 fusion.108
  130.6 1.2 fusion.25
  131.9 0.5 convolution_add_fusion.3
  132.4 0.5 subtract_reduce_fusion.1
  134.7 1.2 fusion.37
  135.9 0.5 convolution_add_fusion.2
  136.5 0.5 subtract_reduce_fusion
  139.0 0.7 fusion.81
  141.0 0.9 multiply_reduce_fusion
  141.9 41.6 %all-reduce = (f32[]{:T(128)}, f32[]{:T(128)}) all-reduce(f32[]{:T(128)} %get-tuple-element.34, f32[]{:T(128)S(6)} %add.285), channel_id=1, replica_groups=mesh['row'=8,'col'=4] {'row','col'}, use_global_device_ids=true, to_apply=%region_7.8 | all-reduce | flops 2 | bytes 16 | tf_op jit(solution)/shard_map/psum | solution.py:120
  184.9 0.6 divide_subtract_fusion
  (70 shorter events, 8.6 us)
Async XLA Ops:
  0.6 77.1 %copy-start.13 = (f32[128,128]{1,0:T(8,128)S(1)}, f32[128,128]{1,0:T(8,128)}, u32[]{:S(2)}) copy-start(f32[128,128]{1,0:T(8,128)} %param.6) | copy-start | bytes 196612
  0.6 77.1 %copy-start.14 = (f32[128,128]{1,0:T(8,128)S(1)}, f32[128,128]{1,0:T(8,128)}, u32[]{:S(2)}) copy-start(f32[128,128]{1,0:T(8,128)} %param.5) | copy-start | bytes 196612
  2.5 75.2 %collective-permute-start.1 = (f32[3,64,128]{2,1,0:T(8,128)S(1)}, f32[3,64,128]{2,1,0:T(8,128)S(1)}, u32[]{:S(2)}, u32[]{:S(2)}) collective-permute-start(f32[3,64,128]{2,1,0:T(8,128)S(1)} %get-tuple-element.25), channel_id=1, source_target_pairs={{4,0},{8,4},{12,8},{16,12},{20,16},{24,20},{28,24},{5,1},{9,5},{13... | collective-permute-start | bytes 294920 | tf_op jit(solution)/shard_map/ppermute | solution.py:29
  3.8 73.9 %collective-permute-start = (f32[3,64,128]{2,1,0:T(8,128)S(1)}, f32[3,64,128]{2,1,0:T(8,128)S(1)}, u32[]{:S(2)}, u32[]{:S(2)}) collective-permute-start(f32[3,64,128]{2,1,0:T(8,128)S(1)} %get-tuple-element.24), channel_id=1, source_target_pairs={{0,4},{4,8},{8,12},{12,16},{16,20},{20,24},{24,28},{1,5},{5,9},{9,... | collective-permute-start | bytes 294920 | tf_op jit(solution)/shard_map/ppermute | solution.py:26
  77.4 14.8 %copy-start.9 = (f32[6,32,32]{2,1,0:T(8,128)}, f32[6,32,32]{2,1,0:T(8,128)S(1)}, u32[]{:S(2)}) copy-start(f32[6,32,32]{2,1,0:T(8,128)S(1)} %squeeze.26) | copy-start | bytes 73732
  77.5 14.7 %copy-start.11 = (f32[6,32,32]{2,1,0:T(8,128)}, f32[6,32,32]{2,1,0:T(8,128)S(1)}, u32[]{:S(2)}) copy-start(f32[6,32,32]{2,1,0:T(8,128)S(1)} %squeeze.24) | copy-start | bytes 73732
  77.5 14.7 %copy-start.5 = (f32[6,32,32]{2,1,0:T(8,128)}, f32[6,32,32]{2,1,0:T(8,128)S(1)}, u32[]{:S(2)}) copy-start(f32[6,32,32]{2,1,0:T(8,128)S(1)} %squeeze.27) | copy-start | bytes 73732
  77.6 14.6 %copy-start.7 = (f32[6,32,32]{2,1,0:T(8,128)}, f32[6,32,32]{2,1,0:T(8,128)S(1)}, u32[]{:S(2)}) copy-start(f32[6,32,32]{2,1,0:T(8,128)S(1)} %squeeze.28) | copy-start | bytes 73732
  77.9 9.7 %collective-permute-start.3 = (f32[3,256,64]{2,1,0:T(8,128)S(1)}, f32[3,256,64]{2,1,0:T(8,128)S(1)}, u32[]{:S(2)}, u32[]{:S(2)}) collective-permute-start(f32[3,256,64]{2,1,0:T(8,128)S(1)} %get-tuple-element.19), channel_id=1, source_target_pairs={{1,0},{2,1},{3,2},{5,4},{6,5},{7,6},{9,8},{10,9},{11,10},{13,12},{... | collective-permute-start | bytes 589832 | tf_op jit(solution)/shard_map/ppermute | solution.py:29
  79.2 9.8 %collective-permute-start.2 = (f32[3,256,64]{2,1,0:T(8,128)S(1)}, f32[3,256,64]{2,1,0:T(8,128)S(1)}, u32[]{:S(2)}, u32[]{:S(2)}) collective-permute-start(f32[3,256,64]{2,1,0:T(8,128)S(1)} %get-tuple-element.18), channel_id=1, source_target_pairs={{0,1},{1,2},{2,3},{4,5},{5,6},{6,7},{8,9},{9,10},{10,11},{12,13},{... | collective-permute-start | bytes 589832 | tf_op jit(solution)/shard_map/ppermute | solution.py:26
  89.4 0.9 copy-start
  93.5 1.6 copy-start.4
  106.7 5.4 %copy-start.3 = (f32[256,192]{0,1:S(1)}, f32[256,192]{0,1}, u32[]{:S(2)}) copy-start(f32[256,192]{0,1} %fusion.132) | copy-start | bytes 589828
  115.4 1.7 copy-start.2
  118.7 1.7 copy-start.1
  130.6 1.8 copy-start.10
  130.6 1.8 copy-start.12
  130.6 2.3 %copy-start.15 = (f32[32,256]{1,0:T(8,128)S(1)}, f32[32,256]{1,0:T(8,128)}, u32[]{:S(2)}) copy-start(f32[32,256]{1,0:T(8,128)} %get-tuple-element.29) | copy-start | bytes 98308
  130.6 3.1 %copy-start.16 = (f32[32,256]{1,0:T(8,128)S(1)}, f32[32,256]{1,0:T(8,128)}, u32[]{:S(2)}) copy-start(f32[32,256]{1,0:T(8,128)} %get-tuple-element.28) | copy-start | bytes 98308
  133.6 2.8 %copy-start.6 = (f32[6,32,32]{2,1,0:T(8,128)S(1)}, f32[6,32,32]{2,1,0:T(8,128)}, u32[]{:S(2)}) copy-start(f32[6,32,32]{2,1,0:T(8,128)} %copy-done.5) | copy-start | bytes 73732
  133.7 2.8 %copy-start.8 = (f32[6,32,32]{2,1,0:T(8,128)S(1)}, f32[6,32,32]{2,1,0:T(8,128)}, u32[]{:S(2)}) copy-start(f32[6,32,32]{2,1,0:T(8,128)} %copy-done.7) | copy-start | bytes 73732
  135.9 5.1 %copy-start.17 = (f32[128,128]{1,0:T(8,128)S(1)}, f32[128,128]{1,0:T(8,128)}, u32[]{:S(2)}) copy-start(f32[128,128]{1,0:T(8,128)} %param.4) | copy-start | bytes 196612
where the time goes:
time: 187 us
  blocking collectives  112 us (60%)
  matrix products  44.8 us (24%)
  starting transfers between devices  10.2 us (5%)
  other arithmetic  5.5 us (3%)
  between operations  5.15 us (3%)
  local copies, waits for them, and re-layouts  4.7 us (3%)
  waiting for transfers between devices  4.42 us (2%)
    all_gather x1, blocking collectives, shards(): whole_bank = lax.all_gather(kernels, ('row', 'col'), axis=1, tiled=True)  70.2 us
    psum x1, blocking collectives, shards(): square_global = lax.psum(square_local, ('row', 'col'))  41.6 us
    dot_general x42, matrix products, matmul(): jnp.matmul(first, second, precision=lax.Precision.HIGHEST, preferred_elem...  35.8 us
    unnamed x8, matrix products  8.99 us
    ppermute x2, starting transfers between devices, padded_2(): lax.ppermute(lax.slice_in_dim(block, block.shape[dim] - width, None, axis...  7.61 us
  transfers between devices with their start and end apart: 4, of which 2 were waited for; matrix products, arithmetic and copies ran while one was open for 1% of the time, Pallas kernels for 0%

commit v1 on v0

v1 whole, which is shorter than its diff:
```python
import math

import jax
import jax.numpy as jnp
import numpy as np
from jax import lax
from jax.experimental import pallas as pl
from jax.experimental.pallas import tpu as pltpu
from jax.sharding import PartitionSpec as P

HALO = 64
KERNELS = 6
BAND = 32
CONDITIONS = 2

SHARPNESS = 6.0
THRESHOLD = 0.75
STEP = 0.5
EPSILON = 1e-06
DOSES = (1.0, 1.15)

LANES = 128
VMEM = pl.BlockSpec(memory_space=pltpu.VMEM)


def dot(first, second):
    return lax.dot_general(
        first,
        second,
        (((1,), (0,)), ((), ())),
        precision=lax.Precision.HIGHEST,
        preferred_element_type=jnp.float32,
    )


def tables(pad_width, margin):
    freq = np.arange(BAND) - BAND // 2
    place = np.arange(pad_width)
    turns = (freq[:, None] * place[None, :] % pad_width) * (2.0 * math.pi / pad_width)
    wave_re = np.cos(turns) / math.sqrt(pad_width)
    wave_im = -np.sin(turns) / math.sqrt(pad_width)
    grid = 2 * BAND
    stride = pad_width // grid
    fold = LANES // BAND
    rows = np.arange(BAND).reshape(BAND // fold, fold).T.reshape(-1)
    row_re, row_im = wave_re[rows], wave_im[rows]
    coarse_re, coarse_im = wave_re[:, ::stride], wave_im[:, ::stride]
    crow_re, crow_im = row_re[:, ::stride], row_im[:, ::stride]
    core = slice(margin, pad_width - margin)
    steps = (place[:, None] - stride * np.arange(grid)[None, :]) % pad_width
    diffs = np.arange(1, BAND)
    between = (
        1.0
        + 2.0
        * np.cos(2.0 * math.pi / pad_width * (steps[..., None] * diffs % pad_width)).sum(-1)
    ) / grid

    def cat(*blocks):
        return np.concatenate(blocks, axis=1)

    analyse_cols = cat(wave_re.T, wave_im.T, -wave_im.T, wave_re.T)
    analyse_rows = np.concatenate([row_re, row_im], axis=0)
    field_cols = np.concatenate(
        [
            cat(coarse_re, -coarse_im, -coarse_im, -coarse_re),
            cat(coarse_im, coarse_re, coarse_re, -coarse_im),
        ]
        * 2,
        axis=0,
    )
    field_rows = cat(crow_re.T, crow_im.T)
    up_rows = between
    up_cols = np.concatenate([between.T, between.T], axis=0)
    down_cols = cat(between, between)
    down_rows = between.T
    c_re, c_im = coarse_re.T, coarse_im.T
    back_cols = np.concatenate(
        [
            cat(c_re, c_im, c_im, -c_re, -c_im, c_re, c_re, c_im),
            cat(-c_im, c_re, c_re, c_im, -c_re, -c_im, -c_im, c_re),
        ],
        axis=0,
    )
    back_rows = cat(crow_re, crow_im)
    core_re, core_im = wave_re[:, core], wave_im[:, core]
    core_cols = np.concatenate([cat(core_re, -core_im), cat(core_im, core_re)] * 2, axis=0)
    core_rows = 2.0 * cat(row_re[:, core].T, row_im[:, core].T)
    return [
        jnp.asarray(t, jnp.float32)
        for t in (
            analyse_cols,
            analyse_rows,
            field_cols,
            field_rows,
            up_rows,
            up_cols,
            down_cols,
            down_rows,
            back_cols,
            back_rows,
            core_cols,
            core_rows,
        )
    ]


def pack_columns(logits_ref, target_ref, weight_ref, a_ref, b_ref):
    half = HALO
    odd = lax.rem(lax.axis_index("col"), 2) == 1
    values = [ref[...] for ref in (logits_ref, target_ref, weight_ref)]
    turned = [pltpu.roll(value, half, 1) for value in values]
    low = lax.broadcasted_iota(jnp.int32, values[0].shape, 1) < half
    rows = values[0].shape[0]
    to_right = [
        jnp.where(low, turned[0], values[1]),
        jnp.where(low[: rows // 2], turned[2][: rows // 2], values[2][rows // 2 :]),
    ]
    to_left = [
        jnp.where(low, values[0], turned[1]),
        jnp.where(low[: rows // 2], values[2][: rows // 2], turned[2][rows // 2 :]),
    ]
    a_ref[:rows] = jnp.where(odd, to_left[0], to_right[0])
    a_ref[rows:] = jnp.where(odd, to_left[1], to_right[1])
    b_ref[:rows] = jnp.where(odd, to_right[0], to_left[0])
    b_ref[rows:] = jnp.where(odd, to_right[1], to_left[1])


def widen(logits_ref, target_ref, weight_ref, a_ref, b_ref, centre_ref, up_ref, down_ref):
    half = HALO
    odd = lax.rem(lax.axis_index("col"), 2) == 1
    odd_row = lax.rem(lax.axis_index("row"), 2) == 1
    values = [ref[...] for ref in (logits_ref, target_ref, weight_ref)]
    rows = values[0].shape[0]
    low = lax.broadcasted_iota(jnp.int32, values[0].shape, 1) < half
    got_a, got_b = a_ref[...], b_ref[...]
    left = jnp.where(odd, got_a, got_b)
    right = jnp.where(odd, got_b, got_a)
    left_turned, right_turned = pltpu.roll(left, half, 1), pltpu.roll(right, half, 1)

    def two(first, second):
        return jnp.concatenate([first, second], axis=0)

    lefts = [left[:rows], left_turned[:rows], two(left[rows:], left_turned[rows:])]
    rights = [right_turned[:rows], right[:rows], two(right_turned[rows:], right[rows:])]
    for index, value in enumerate(values):
        turned = pltpu.roll(value, half, 1)
        wide = jnp.concatenate(
            [jnp.where(low, lefts[index], turned), jnp.where(low, turned, rights[index])], axis=1
        )
        centre_ref[index] = wide
        up_ref[index] = jnp.where(odd_row, wide[:half], wide[half:])
        down_ref[index] = jnp.where(odd_row, wide[half:], wide[:half])


def step_kernel(
    order,
    bank_ref,
    centre_ref,
    up_ref,
    down_ref,
    analyse_cols,
    analyse_rows,
    field_cols,
    field_rows,
    up_rows,
    up_cols,
    down_cols,
    down_rows,
    back_cols,
    back_rows,
    core_cols,
    core_rows,
    grad_ref,
    sums_ref,
    flat_ref,
):
    odd_row = lax.rem(lax.axis_index("row"), 2) == 1
    grid = 2 * BAND
    fold = LANES // BAND
    per = BAND // fold

    def padded(index):
        first, second = up_ref[index], down_ref[index]
        return jnp.concatenate(
            [
                jnp.where(odd_row, first, second),
                centre_ref[index],
                jnp.where(odd_row, second, first),
            ],
            axis=0,
        )

    weight = padded(2)
    mask = jnp.where(weight > 0.0, jax.nn.sigmoid(padded(0)), 0.0)
    target = padded(1)
    pad_width = mask.shape[0]
    core = slice(HALO, pad_width - HALO)

    for row, (device, piece) in enumerate(order):
        both = bank_ref[device, :, piece * LANES : (piece + 1) * LANES]
        for condition in range(CONDITIONS):
            flat_ref[condition, row : row + 1, :] = both[condition : condition + 1]

    lane = lax.broadcasted_iota(jnp.int32, (per, LANES), 1)

    def spread(condition, kernel):
        real = flat_ref[condition, pl.ds(kernel * per, per), :]
        imag = flat_ref[condition, pl.ds((KERNELS + kernel) * per, per), :]
        reals = [real] + [pltpu.roll(real, BAND * s, 1) for s in range(1, fold)]
        imags = [imag] + [pltpu.roll(imag, BAND * s, 1) for s in range(1, fold)]
        rows = []
        for j in range(fold):
            first, second = reals[-j % fold], reals[(1 - j) % fold]
            third, fourth = imags[(2 - j) % fold], imags[(3 - j) % fold]
            rows.append(
                jnp.where(
                    lane < 2 * BAND,
                    jnp.where(lane < BAND, first, second),
                    jnp.where(lane < 3 * BAND, third, fourth),
                )
            )
        return jnp.concatenate(rows, axis=0)

    pairs = [(c, k) for c in range(CONDITIONS) for k in range(KERNELS)]
    spectra = [spread(c, k) for c, k in pairs]

    half = dot(mask, analyse_cols[...])
    both = dot(analyse_rows[...], half)
    wide_lane = lax.broadcasted_iota(jnp.int32, (BAND, LANES), 1)
    turned = pltpu.roll(both[BAND:], LANES // 2, 1)
    spectrum = both[:BAND] + jnp.where(wide_lane < LANES // 2, turned, -turned)

    products = jnp.concatenate([s * spectrum for s in spectra], axis=0)
    halves = dot(products, field_cols[...])
    fields = []
    squares = [0.0] * CONDITIONS
    for index, (condition, _) in enumerate(pairs):
        rows = halves[index * BAND : (index + 1) * BAND]
        stacked = jnp.concatenate([rows[:, :LANES], rows[:, LANES:]], axis=0)
        field = dot(field_rows[...], stacked)
        fields.append(field)
        squares[condition] = squares[condition] + field * field

    tall = dot(up_rows[...], jnp.concatenate(squares, axis=1))
    tall = jnp.concatenate(
        [tall[:, c * LANES : (c + 1) * LANES] for c in range(CONDITIONS)], axis=0
    )
    intensities = dot(tall, up_cols[...])

    slopes = []
    loss = 0.0
    for condition, dose in enumerate(DOSES):
        intensity = intensities[condition * pad_width : (condition + 1) * pad_width]
        resist = jax.nn.sigmoid(SHARPNESS * (dose * intensity - THRESHOLD))
        error = resist - target
        scaled = weight * error
        loss = loss + (scaled * error)[core, core]
        slopes.append((2.0 * SHARPNESS * dose) * scaled * (resist * (1.0 - resist)))
    narrow = dot(jnp.concatenate(slopes, axis=0), down_cols[...])
    narrow = jnp.concatenate(
        [narrow[c * pad_width : (c + 1) * pad_width] for c in range(CONDITIONS)], axis=1
    )
    coarse = dot(down_rows[...], narrow)

    weighted = jnp.concatenate(
        [
            field * coarse[:, condition * LANES : (condition + 1) * LANES]
            for field, (condition, _) in zip(fields, pairs, strict=True)
        ],
        axis=0,
    )
    backs = dot(weighted, back_cols[...])
    total = 0.0
    for index in range(len(pairs)):
        rows = backs[index * grid : (index + 1) * grid]
        stacked = jnp.concatenate([rows[:, :LANES], rows[:, LANES:]], axis=0)
        total = total + spectra[index] * dot(back_rows[...], stacked)

    across = dot(total, core_cols[...])
    core_width = across.shape[1] // 2
    stacked = jnp.concatenate([across[:, :core_width], across[:, core_width:]], axis=0)
    gradient = dot(core_rows[...], stacked)
    own = mask[core, core]
    cells = gradient * own * (1.0 - own)
    grad_ref[...] = cells
    square = jnp.sum(jnp.sum(cells * cells, axis=0, keepdims=True), axis=1, keepdims=True)
    loss = jnp.sum(jnp.sum(loss, axis=0, keepdims=True), axis=1, keepdims=True)
    sums_ref[0:1, :] = jnp.broadcast_to(square, (1, LANES))
    sums_ref[1:2, :] = jnp.broadcast_to(loss, (1, LANES))


def axis_rounds(axis):
    count = lax.axis_size(axis)
    bits = [1 << b for b in range(count.bit_length() - 1)]
    return bits[1:] + bits[:1] if axis == "row" else bits


def swap(value, axis, bit):
    count = lax.axis_size(axis)
    return lax.ppermute(value, axis, [(i, i ^ bit) for i in range(count)])


def gather_bank(kernels):
    held = kernels[None]
    crossed = []
    for axis in ("col", "row"):
        for bit in axis_rounds(axis):
            got = swap(held, axis, bit)
            high = (lax.axis_index(axis) & bit) != 0
            held = jnp.concatenate(
                [jnp.where(high, got, held), jnp.where(high, held, got)], axis=0
            )
            crossed.append((axis, bit))
    rows, cols = lax.axis_size("row"), lax.axis_size("col")
    place = {}
    for row in range(rows):
        for col in range(cols):
            index = 0
            for level, (axis, bit) in enumerate(crossed):
                own = row if axis == "row" else col
                index += (1 << level) * ((own & bit) != 0)
            place[row * cols + col] = index
    return held, place


def pair_swap(value, axis, first):
    count = lax.axis_size(axis)
    pairs = []
    for low in range(first, count - 1, 2):
        pairs += [(low, low + 1), (low + 1, low)]
    return lax.ppermute(value, axis, pairs)


def total_sum(value):
    for axis in ("row", "col"):
        for bit in axis_rounds(axis):
            value = value + swap(value, axis, bit)
    return value


def shards(mask_logits, target, weight, kernels):
    core_width = mask_logits.shape[0]
    pad_width = core_width + 2 * HALO
    rows, cols = lax.axis_size("row"), lax.axis_size("col")
    f32 = jnp.float32

    bank, place = gather_bank(kernels)
    pieces = kernels.shape[1] // LANES
    if kernels.shape[1] % LANES:
        whole = bank[np.array([place[device] for device in range(rows * cols)])]
        bank = jnp.swapaxes(whole, 0, 1).reshape(1, CONDITIONS, -1)
        place, pieces = {0: 0}, bank.shape[2] // LANES
    order = [(place[device], piece) for device in sorted(place) for piece in range(pieces)]

    packed = jax.ShapeDtypeStruct((core_width * 3 // 2, core_width), f32)
    slab_a, slab_b = pl.pallas_call(
        pack_columns, out_shape=(packed, packed), in_specs=[VMEM] * 3, out_specs=(VMEM,) * 2
    )(mask_logits, target, weight)
    got_a, got_b = pair_swap(slab_a, "col", 0), pair_swap(slab_b, "col", 1)
    slab = jax.ShapeDtypeStruct((3, HALO, pad_width), f32)
    centre, up, down = pl.pallas_call(
        widen,
        out_shape=(jax.ShapeDtypeStruct((3, core_width, pad_width), f32), slab, slab),
        in_specs=[VMEM] * 5,
        out_specs=(VMEM,) * 3,
    )(mask_logits, target, weight, got_a, got_b)
    up, down = pair_swap(up, "row", 0), pair_swap(down, "row", 1)

    consts = tables(pad_width, HALO)
    grad_cells, sums = pl.pallas_call(
        lambda *refs: step_kernel(order, *refs),
        out_shape=(
            jax.ShapeDtypeStruct((core_width, core_width), f32),
            jax.ShapeDtypeStruct((2, LANES), f32),
        ),
        in_specs=[VMEM] * (4 + len(consts)),
        out_specs=(VMEM,) * 2,
        scratch_shapes=[pltpu.VMEM((CONDITIONS, len(order), LANES), f32)],
        compiler_params=pltpu.CompilerParams(vmem_limit_bytes=32 * 1024 * 1024),
    )(bank, centre, up, down, *consts)

    sums = total_sum(sums)
    cell_count = rows * cols * core_width * core_width
    norm = jnp.sqrt(sums[0:1] / cell_count + EPSILON)
    return (mask_logits - STEP * grad_cells / norm, sums[1, 0] / cell_count)


def solution(mesh):
    placed = (P("row", "col"), P("row", "col"), P("row", "col"), P(None, ("row", "col")))
    return jax.shard_map(
        shards, mesh=mesh, in_specs=placed, out_specs=(P("row", "col"), P()), check_vma=False
    )
```

time: 187 us -> 66.5 us (0.36)
  blocking collectives: 112 us -> 0 us
  matrix products: 44.8 us -> 0 us
  starting transfers between devices: 10.2 us -> 31.2 us
  Pallas kernels: 0 us -> 11.5 us
  waiting for transfers between devices: 4.42 us -> 15.7 us
  other arithmetic: 5.5 us -> 1.54 us
  between operations: 5.15 us -> 2.66 us
    all_gather x1 -> x0, blocking collectives: 70.2 us -> none  [shards(): whole_bank = lax.all_gather(kernels, ('row', 'col'), axis=1, tiled=True)]
    psum x1 -> x0, blocking collectives: 41.6 us -> none  [shards(): square_global = lax.psum(square_local, ('row', 'col'))]
    dot_general x42 -> x0, matrix products: 35.8 us -> none  [matmul(): jnp.matmul(first, second, precision=lax.Precision.HIGHEST, preferred_elem...]
    ppermute x4 -> x14, starting transfers between devices: 10.2 us -> 31.2 us  [the longest x10 28.1 us: swap(): return lax.ppermute(value, axis, [(i, i ^ bit) for i in range(count)])]
    pallas_call x0 -> x3, Pallas kernels: none -> 11.5 us  [the longest x1 7.63 us: shards(): pl.pallas_call(lambda *refs: step_kernel(order, *refs), out_shape=(jax.Sh...]
    ppermute x4 -> x14, waiting for transfers between devices: 4.42 us -> 15.7 us  [the longest x10 12.6 us: swap(): return lax.ppermute(value, axis, [(i, i ^ bit) for i in range(count)])]
    unnamed x8 -> x0, matrix products: 8.99 us -> none
    unnamed x36 -> x32, local copies, waits for them, and re-layouts: 0.55 us -> 2.99 us
  transfers between devices with their start and end apart: 4 -> 14, of which waited for: 2 -> 10; matrix products, arithmetic and copies ran while one was open for 1% -> 0% of each run, Pallas kernels for 0% -> 6%
where the time goes in v1:
time: 66.5 us; the launch traced here: 66.1 us
  starting transfers between devices  31.2 us (47%)
  waiting for transfers between devices  15.7 us (24%)
  Pallas kernels  11.5 us (17%)
  local copies, waits for them, and re-layouts  3.51 us (5%)
  between operations  2.66 us (4%)
  other arithmetic  1.54 us (2%)
    ppermute x10, starting transfers between devices, swap(): return lax.ppermute(value, axis, [(i, i ^ bit) for i in range(count)])  28.1 us
    ppermute x10, waiting for transfers between devices, swap(): return lax.ppermute(value, axis, [(i, i ^ bit) for i in range(count)])  12.6 us
    pallas_call x1, Pallas kernels, shards(): pl.pallas_call(lambda *refs: step_kernel(order, *refs), out_shape=(jax.Sh...  7.63 us
    ppermute x4, waiting for transfers between devices, pair_swap(): return lax.ppermute(value, axis, pairs)  3.16 us
    ppermute x4, starting transfers between devices, pair_swap(): return lax.ppermute(value, axis, pairs)  3.03 us
    unnamed x32, local copies, waits for them, and re-layouts  2.99 us
    pallas_call x1, Pallas kernels, shards(): pl.pallas_call(widen, out_shape=(jax.ShapeDtypeStruct((3, core_width, pad...  2.15 us
    pallas_call x1, Pallas kernels, shards(): pl.pallas_call(pack_columns, out_shape=(packed, packed), in_specs=[VMEM]...  1.74 us
  transfers between devices with their start and end apart: 14, of which 10 were waited for; matrix products, arithmetic and copies ran while one was open for 0% of the time, Pallas kernels for 6%

profile of v1, /device:TPU:0, one launch (start us, length us, event | category | flops | bytes accessed | tf_op | source)
XLA Modules:
  0.0 66.1 jit_solution(5941419741406822149)
XLA Ops:
  0.6 0.0 copy-start.12
  0.6 0.0 copy-start.11
  0.7 3.1 %collective-permute-start = (f32[1,2,384]{2,1,0:T(2,128)}, f32[1,2,384]{2,1,0:T(2,128)S(1)}, u32[]{:S(2)}, u32[]{:S(2)}) collective-permute-start(f32[1,2,384]{2,1,0:T(2,128)} %bitcast.6), channel_id=1, source_target_pairs={{0,1},{1,0},{2,3},{3,2},{4,5},{5,4},{6,7},{7,6},{8,9},{9,8},{10,11... | collective-permute-start | bytes 9224 | tf_op jit(solution)/shard_map/ppermute | solution.py:300
  3.7 1.8 %collective-permute-done = f32[1,2,384]{2,1,0:T(2,128)S(1)} collective-permute-done((f32[1,2,384]{2,1,0:T(2,128)}, f32[1,2,384]{2,1,0:T(2,128)S(1)}, u32[]{:S(2)}, u32[]{:S(2)}) %collective-permute-start) | collective-permute-done | bytes 3104 | tf_op jit(solution)/shard_map/ppermute | solution.py:300
  5.5 0.7 %broadcast_select_fusion.9 = (f32[1,2,384]{2,1,0:T(2,128)S(1)}, f32[1,2,384]{2,1,0:T(2,128)S(1)}) fusion(f32[1,2,384]{2,1,0:T(2,128)S(1)} %collective-permute-done, pred[]{:T(512)S(6)} %ne.19, f32[2,384]{1,0:T(2,128)} %param.19), kind=kLoop, calls=%fused_computation.15 | loop fusion | flops 1536 | bytes 12289 | tf_op jit(solution)/shard_map/jit(_where)/select_n | solution.py:311
  6.2 3.1 %collective-permute-start.1 = (f32[2,2,384]{2,1,0:T(2,128)S(1)}, f32[2,2,384]{2,1,0:T(2,128)S(1)}, u32[]{:S(2)}, u32[]{:S(2)}) collective-permute-start(f32[2,2,384]{2,1,0:T(2,128)S(1)} %pad_maximum_fusion.4), channel_id=1, source_target_pairs={{0,2},{1,3},{2,0},{3,1},{4,6},{5,7},{6,4},{7,5},{8,10},{9,11},{10,... | collective-permute-start | bytes 18440 | tf_op jit(solution)/shard_map/ppermute | solution.py:300
  9.3 1.6 %collective-permute-done.1 = f32[2,2,384]{2,1,0:T(2,128)S(1)} collective-permute-done((f32[2,2,384]{2,1,0:T(2,128)S(1)}, f32[2,2,384]{2,1,0:T(2,128)S(1)}, u32[]{:S(2)}, u32[]{:S(2)}) %collective-permute-start.1) | collective-permute-done | bytes 6176 | tf_op jit(solution)/shard_map/ppermute | solution.py:300
  10.9 0.0 copy-start.7
  11.0 1.9 %collective-permute-start.2 = (f32[4,2,384]{2,1,0:T(2,128)S(1)}, f32[4,2,384]{2,1,0:T(2,128)S(1)}, u32[]{:S(2)}, u32[]{:S(2)}) collective-permute-start(f32[4,2,384]{2,1,0:T(2,128)S(1)} %pad_maximum_fusion.3), channel_id=1, source_target_pairs={{0,8},{4,12},{8,0},{12,4},{16,24},{20,28},{24,16},{28,20},{1,9},{5... | collective-permute-start | bytes 36872 | tf_op jit(solution)/shard_map/ppermute | solution.py:300
  12.9 1.9 %collective-permute-done.2 = f32[4,2,384]{2,1,0:T(2,128)S(1)} collective-permute-done((f32[4,2,384]{2,1,0:T(2,128)S(1)}, f32[4,2,384]{2,1,0:T(2,128)S(1)}, u32[]{:S(2)}, u32[]{:S(2)}) %collective-permute-start.2) | collective-permute-done | bytes 12320 | tf_op jit(solution)/shard_map/ppermute | solution.py:300
  14.8 1.9 %collective-permute-start.3 = (f32[8,2,384]{2,1,0:T(2,128)S(1)}, f32[8,2,384]{2,1,0:T(2,128)S(1)}, u32[]{:S(2)}, u32[]{:S(2)}) collective-permute-start(f32[8,2,384]{2,1,0:T(2,128)S(1)} %pad_maximum_fusion.2), channel_id=1, source_target_pairs={{0,16},{4,20},{8,24},{12,28},{16,0},{20,4},{24,8},{28,12},{1,17},{... | collective-permute-start | bytes 73736 | tf_op jit(solution)/shard_map/ppermute | solution.py:300
  16.7 1.7 %shard_map.167 = (f32[192,128]{1,0:T(8,128)}, f32[192,128]{1,0:T(8,128)}) custom-call(f32[128,128]{1,0:T(8,128)} %logits_ref.3, f32[128,128]{1,0:T(8,128)} %target_ref.3, f32[128,128]{1,0:T(8,128)} %weight_ref.3), custom_call_target="tpu_custom_call" | custom-call | tf_op jit(solution)/shard_map/pallas_call | solution.py:356
  18.4 1.6 %collective-permute-start.5 = (f32[192,128]{1,0:T(8,128)}, f32[192,128]{1,0:T(8,128)S(1)}, u32[]{:S(2)}, u32[]{:S(2)}) collective-permute-start(f32[192,128]{1,0:T(8,128)} %get-tuple-element.9), channel_id=1, source_target_pairs={{0,1},{1,0},{2,3},{3,2},{4,5},{5,4},{6,7},{7,6},{8,9},{9,8},{10,11... | collective-permute-start | bytes 294920 | tf_op jit(solution)/shard_map/ppermute | solution.py:331
  20.0 0.7 collective-permute-start.6
  20.7 0.0 collective-permute-done.3
  20.7 0.0 copy-start.4
  20.8 0.1 collective-permute-start.4
  20.8 2.4 %collective-permute-done.5.a_ref = f32[192,128]{1,0:T(8,128)S(1)} collective-permute-done((f32[192,128]{1,0:T(8,128)}, f32[192,128]{1,0:T(8,128)S(1)}, u32[]{:S(2)}, u32[]{:S(2)}) %collective-permute-start.5) | collective-permute-done | bytes 98336 | tf_op jit(solution)/shard_map/ppermute | solution.py:331
  23.3 0.0 collective-permute-done.6.b_ref
  23.3 0.6 copy-done.14
  23.9 0.6 copy-done.15
  24.5 2.1 %shard_map.168 = (f32[3,128,256]{2,1,0:T(8,128)}, f32[3,64,256]{2,1,0:T(8,128)}, f32[3,64,256]{2,1,0:T(8,128)}) custom-call(f32[128,128]{1,0:T(8,128)} %logits_ref.3, f32[128,128]{1,0:T(8,128)} %target_ref.3, f32[128,128]{1,0:T(8,128)} %weight_ref.3, f32[192,128]{1,0:T(8,128)} %copy-done.14, f32[192,128]{1,0:T(8,128)} %copy-done.15), custom_call_target="tpu_custom_call" | custom-call | tf_op jit(solution)/shard_map/pallas_call | solution.py:361
  26.7 0.0 collective-permute-start.7
  26.7 0.8 %collective-permute-start.8 = (f32[3,64,256]{2,1,0:T(8,128)}, f32[3,64,256]{2,1,0:T(8,128)S(1)}, u32[]{:S(2)}, u32[]{:S(2)}) collective-permute-start(f32[3,64,256]{2,1,0:T(8,128)} %get-tuple-element.13), channel_id=1, source_target_pairs={{4,8},{8,4},{12,16},{16,12},{20,24},{24,20},{5,9},{9,5},{13,17},{1... | collective-permute-start | bytes 589832 | tf_op jit(solution)/shard_map/ppermute | solution.py:331
  27.5 0.0 collective-permute-done.4
  27.6 0.7 %collective-permute-done.7.refs_2_ = f32[3,64,256]{2,1,0:T(8,128)S(1)} collective-permute-done((f32[3,64,256]{2,1,0:T(8,128)}, f32[3,64,256]{2,1,0:T(8,128)S(1)}, u32[]{:S(2)}, u32[]{:S(2)}) %collective-permute-start.7) | collective-permute-done | bytes 196640 | tf_op jit(solution)/shard_map/ppermute | solution.py:331
  28.3 0.0 collective-permute-done.8.refs_3_
  28.3 0.0 copy-done.8
  28.4 0.0 copy-done.7
  28.4 0.0 copy-done.5
  28.4 0.0 copy-done.6
  28.4 0.0 copy-done.4
  28.4 0.0 copy-start.9
  28.4 0.8 %copy-done.9 = f32[64,256]{1,0:T(8,128)S(1)} copy-done((f32[64,256]{1,0:T(8,128)S(1)}, f32[64,256]{1,0:T(8,128)}, u32[]{:S(2)}) %copy-start.9) | copy-done | bytes 65560
  29.3 0.8 %copy-done.10 = f32[64,256]{1,0:T(8,128)S(1)} copy-done((f32[64,256]{1,0:T(8,128)S(1)}, f32[64,256]{1,0:T(8,128)}, u32[]{:S(2)}) %copy-start.10) | copy-done | bytes 65560
  30.1 7.6 %shard_map.169 = (f32[128,128]{1,0:T(8,128)S(1)}, f32[2,128]{1,0:T(2,128)S(1)}) custom-call(f32[32,2,384]{2,1,0:T(2,128)S(1)} %pad_maximum_fusion.refs_0_, f32[3,128,256]{2,1,0:T(8,128)S(1)} %copy-done, f32[3,64,256]{2,1,0:T(8,128)S(1)} %collective-permute-done.7.refs_2_, f32[3,64,256]{2,1,0:T(8,128)S(1)} %collective-permute-done.8.refs_3_, ...), custom_call_target="tpu_custom_call" | custom-call | tf_op jit(solution)/shard_map/pallas_call | solution.py:370
  37.8 7.2 %collective-permute-start.9 = (f32[2,128]{1,0:T(2,128)S(1)}, f32[2,128]{1,0:T(2,128)S(1)}, u32[]{:S(2)}, u32[]{:S(2)}) collective-permute-start(f32[2,128]{1,0:T(2,128)S(1)} %get-tuple-element.15), channel_id=1, source_target_pairs={{0,8},{4,12},{8,0},{12,4},{16,24},{20,28},{24,16},{28,20},{1,9},{5... | collective-permute-start | bytes 3080 | tf_op jit(solution)/shard_map/ppermute | solution.py:300
  44.9 1.5 %collective-permute-done.9 = f32[2,128]{1,0:T(2,128)S(1)} collective-permute-done((f32[2,128]{1,0:T(2,128)S(1)}, f32[2,128]{1,0:T(2,128)S(1)}, u32[]{:S(2)}, u32[]{:S(2)}) %collective-permute-start.9) | collective-permute-done | bytes 1056 | tf_op jit(solution)/shard_map/ppermute | solution.py:300
  46.5 3.0 %collective-permute-start.10 = (f32[2,128]{1,0:T(2,128)S(1)}, f32[2,128]{1,0:T(2,128)S(1)}, u32[]{:S(2)}, u32[]{:S(2)}) collective-permute-start(f32[2,128]{1,0:T(2,128)S(1)} %add.21), channel_id=1, source_target_pairs={{0,16},{4,20},{8,24},{12,28},{16,0},{20,4},{24,8},{28,12},{1,17},{... | collective-permute-start | bytes 3080 | tf_op jit(solution)/shard_map/ppermute | solution.py:300
  49.5 1.5 %collective-permute-done.10 = f32[2,128]{1,0:T(2,128)S(1)} collective-permute-done((f32[2,128]{1,0:T(2,128)S(1)}, f32[2,128]{1,0:T(2,128)S(1)}, u32[]{:S(2)}, u32[]{:S(2)}) %collective-permute-start.10) | collective-permute-done | bytes 1056 | tf_op jit(solution)/shard_map/ppermute | solution.py:300
  51.1 0.0 collective-permute-start.11
  51.1 1.1 %collective-permute-done.11 = f32[2,128]{1,0:T(2,128)S(1)} collective-permute-done((f32[2,128]{1,0:T(2,128)S(1)}, f32[2,128]{1,0:T(2,128)S(1)}, u32[]{:S(2)}, u32[]{:S(2)}) %collective-permute-start.11) | collective-permute-done | bytes 1056 | tf_op jit(solution)/shard_map/ppermute | solution.py:300
  52.2 4.4 %collective-permute-start.12 = (f32[2,128]{1,0:T(2,128)S(1)}, f32[2,128]{1,0:T(2,128)S(1)}, u32[]{:S(2)}, u32[]{:S(2)}) collective-permute-start(f32[2,128]{1,0:T(2,128)S(1)} %add.23), channel_id=1, source_target_pairs={{0,1},{1,0},{2,3},{3,2},{4,5},{5,4},{6,7},{7,6},{8,9},{9,8},{10,11... | collective-permute-start | bytes 3080 | tf_op jit(solution)/shard_map/ppermute | solution.py:300
  56.6 1.5 %collective-permute-done.12 = f32[2,128]{1,0:T(2,128)S(1)} collective-permute-done((f32[2,128]{1,0:T(2,128)S(1)}, f32[2,128]{1,0:T(2,128)S(1)}, u32[]{:S(2)}, u32[]{:S(2)}) %collective-permute-start.12) | collective-permute-done | bytes 1056 | tf_op jit(solution)/shard_map/ppermute | solution.py:300
  58.1 3.5 %collective-permute-start.13 = (f32[2,128]{1,0:T(2,128)S(1)}, f32[2,128]{1,0:T(2,128)S(1)}, u32[]{:S(2)}, u32[]{:S(2)}) collective-permute-start(f32[2,128]{1,0:T(2,128)S(1)} %add.24), channel_id=1, source_target_pairs={{0,2},{1,3},{2,0},{3,1},{4,6},{5,7},{6,4},{7,5},{8,10},{9,11},{10,... | collective-permute-start | bytes 3080 | tf_op jit(solution)/shard_map/ppermute | solution.py:300
  61.6 1.5 %collective-permute-done.13 = f32[2,128]{1,0:T(2,128)S(1)} collective-permute-done((f32[2,128]{1,0:T(2,128)S(1)}, f32[2,128]{1,0:T(2,128)S(1)}, u32[]{:S(2)}, u32[]{:S(2)}) %collective-permute-start.13) | collective-permute-done | bytes 1056 | tf_op jit(solution)/shard_map/ppermute | solution.py:300
  63.2 0.5 slice.7
  64.4 0.6 divide_subtract_fusion
  (33 shorter events, 0.2 us)
Async XLA Ops:
  0.6 27.7 %copy-start.12 = (f32[32,128]{1,0:T(8,128)S(1)}, f32[32,128]{1,0:T(8,128)}, u32[]{:S(2)}) copy-start(f32[32,128]{1,0:T(8,128)} %constant.61.clone.refs_13_) | copy-start | bytes 49156
  0.6 27.7 %copy-start.11 = (f32[64,64]{1,0:T(8,128)S(1)}, f32[64,64]{1,0:T(8,128)}, u32[]{:S(2)}) copy-start(f32[64,64]{1,0:T(8,128)} %constant.55.clone.refs_7_) | copy-start | bytes 49156
  0.7 4.9 %collective-permute-start = (f32[1,2,384]{2,1,0:T(2,128)}, f32[1,2,384]{2,1,0:T(2,128)S(1)}, u32[]{:S(2)}, u32[]{:S(2)}) collective-permute-start(f32[1,2,384]{2,1,0:T(2,128)} %bitcast.6), channel_id=1, source_target_pairs={{0,1},{1,0},{2,3},{3,2},{4,5},{5,4},{6,7},{7,6},{8,9},{9,8},{10,11... | collective-permute-start | bytes 9224 | tf_op jit(solution)/shard_map/ppermute | solution.py:300
  6.2 22.1 %copy-start.8 = (f32[128,64]{1,0:T(8,128)S(1)}, f32[128,64]{1,0:T(8,128)}, u32[]{:S(2)}) copy-start(f32[128,64]{1,0:T(8,128)} %constant.63.clone.refs_15_) | copy-start | bytes 98308
  6.2 4.7 %collective-permute-start.1 = (f32[2,2,384]{2,1,0:T(2,128)S(1)}, f32[2,2,384]{2,1,0:T(2,128)S(1)}, u32[]{:S(2)}, u32[]{:S(2)}) collective-permute-start(f32[2,2,384]{2,1,0:T(2,128)S(1)} %pad_maximum_fusion.4), channel_id=1, source_target_pairs={{0,2},{1,3},{2,0},{3,1},{4,6},{5,7},{6,4},{7,5},{8,10},{9,11},{10,... | collective-permute-start | bytes 18440 | tf_op jit(solution)/shard_map/ppermute | solution.py:300
  10.9 17.4 %copy-start.7 = (f32[256,128]{1,0:T(8,128)S(1)}, f32[256,128]{1,0:T(8,128)}, u32[]{:S(2)}) copy-start(f32[256,128]{1,0:T(8,128)} %constant.52.clone.refs_4_) | copy-start | bytes 393220
  11.0 3.8 %collective-permute-start.2 = (f32[4,2,384]{2,1,0:T(2,128)S(1)}, f32[4,2,384]{2,1,0:T(2,128)S(1)}, u32[]{:S(2)}, u32[]{:S(2)}) collective-permute-start(f32[4,2,384]{2,1,0:T(2,128)S(1)} %pad_maximum_fusion.3), channel_id=1, source_target_pairs={{0,8},{4,12},{8,0},{12,4},{16,24},{20,28},{24,16},{28,20},{1,9},{5... | collective-permute-start | bytes 36872 | tf_op jit(solution)/shard_map/ppermute | solution.py:300
  14.8 5.9 %collective-permute-start.3 = (f32[8,2,384]{2,1,0:T(2,128)S(1)}, f32[8,2,384]{2,1,0:T(2,128)S(1)}, u32[]{:S(2)}, u32[]{:S(2)}) collective-permute-start(f32[8,2,384]{2,1,0:T(2,128)S(1)} %pad_maximum_fusion.2), channel_id=1, source_target_pairs={{0,16},{4,20},{8,24},{12,28},{16,0},{20,4},{24,8},{28,12},{1,17},{... | collective-permute-start | bytes 73736 | tf_op jit(solution)/shard_map/ppermute | solution.py:300
  16.7 11.7 %copy-start.5 = (f32[256,64]{1,0:T(8,128)S(1)}, f32[256,64]{1,0:T(8,128)}, u32[]{:S(2)}) copy-start(f32[256,64]{1,0:T(8,128)} %constant.56.clone.refs_8_) | copy-start | bytes 196612
  16.7 11.7 %copy-start.6 = (f32[128,256]{1,0:T(8,128)S(1)}, f32[128,256]{1,0:T(8,128)}, u32[]{:S(2)}) copy-start(f32[128,256]{1,0:T(8,128)} %constant.54.clone.refs_6_) | copy-start | bytes 393220
  18.4 4.8 %collective-permute-start.5 = (f32[192,128]{1,0:T(8,128)}, f32[192,128]{1,0:T(8,128)S(1)}, u32[]{:S(2)}, u32[]{:S(2)}) collective-permute-start(f32[192,128]{1,0:T(8,128)} %get-tuple-element.9), channel_id=1, source_target_pairs={{0,1},{1,0},{2,3},{3,2},{4,5},{5,4},{6,7},{7,6},{8,9},{9,8},{10,11... | collective-permute-start | bytes 294920 | tf_op jit(solution)/shard_map/ppermute | solution.py:331
  20.0 3.3 %collective-permute-start.6 = (f32[192,128]{1,0:T(8,128)}, f32[192,128]{1,0:T(8,128)S(1)}, u32[]{:S(2)}, u32[]{:S(2)}) collective-permute-start(f32[192,128]{1,0:T(8,128)} %get-tuple-element.10), channel_id=1, source_target_pairs={{1,2},{2,1},{5,6},{6,5},{9,10},{10,9},{13,14},{14,13},{17,18},{18,... | collective-permute-start | bytes 294920 | tf_op jit(solution)/shard_map/ppermute | solution.py:331
  20.7 7.7 %copy-start.4 = (f32[128,256]{1,0:T(8,128)S(1)}, f32[128,256]{1,0:T(8,128)}, u32[]{:S(2)}) copy-start(f32[128,256]{1,0:T(8,128)} %constant.57.clone.refs_9_) | copy-start | bytes 393220
  20.8 6.7 %collective-permute-start.4 = (f32[16,2,384]{2,1,0:T(2,128)S(1)}, f32[16,2,384]{2,1,0:T(2,128)S(1)}, u32[]{:S(2)}, u32[]{:S(2)}) collective-permute-start(f32[16,2,384]{2,1,0:T(2,128)S(1)} %pad_maximum_fusion.1), channel_id=1, source_target_pairs={{0,4},{4,0},{8,12},{12,8},{16,20},{20,16},{24,28},{28,24},{1,5},{5... | collective-permute-start | bytes 147464 | tf_op jit(solution)/shard_map/ppermute | solution.py:300
  23.3 0.6 copy-start.14
  23.9 0.6 copy-start.15
  24.5 3.9 %copy-start.1 = (f32[128,256]{1,0:T(8,128)S(1)}, f32[128,256]{1,0:T(8,128)}, u32[]{:S(2)}) copy-start(f32[128,256]{1,0:T(8,128)} %constant.62.clone.refs_14_) | copy-start | bytes 393220
  24.5 3.9 %copy-start.2 = (f32[128,256]{1,0:T(8,128)S(1)}, f32[128,256]{1,0:T(8,128)}, u32[]{:S(2)}) copy-start(f32[128,256]{1,0:T(8,128)} %constant.60.clone.refs_12_) | copy-start | bytes 393220
  24.5 3.9 %copy-start.3 = (f32[256,128]{1,0:T(8,128)S(1)}, f32[256,128]{1,0:T(8,128)}, u32[]{:S(2)}) copy-start(f32[256,128]{1,0:T(8,128)} %constant.58.clone.refs_10_) | copy-start | bytes 393220
  26.7 1.7 %copy-start = (f32[3,128,256]{2,1,0:T(8,128)S(1)}, f32[3,128,256]{2,1,0:T(8,128)}, u32[]{:S(2)}) copy-start(f32[3,128,256]{2,1,0:T(8,128)} %get-tuple-element.11.refs_1_) | copy-start | bytes 1179652
  26.7 1.7 %collective-permute-start.7 = (f32[3,64,256]{2,1,0:T(8,128)}, f32[3,64,256]{2,1,0:T(8,128)S(1)}, u32[]{:S(2)}, u32[]{:S(2)}) collective-permute-start(f32[3,64,256]{2,1,0:T(8,128)} %get-tuple-element.12), channel_id=1, source_target_pairs={{0,4},{4,0},{8,12},{12,8},{16,20},{20,16},{24,28},{28,24},{1,5},{5... | collective-permute-start | bytes 589832 | tf_op jit(solution)/shard_map/ppermute | solution.py:331
  26.7 1.7 %collective-permute-start.8 = (f32[3,64,256]{2,1,0:T(8,128)}, f32[3,64,256]{2,1,0:T(8,128)S(1)}, u32[]{:S(2)}, u32[]{:S(2)}) collective-permute-start(f32[3,64,256]{2,1,0:T(8,128)} %get-tuple-element.13), channel_id=1, source_target_pairs={{4,8},{8,4},{12,16},{16,12},{20,24},{24,20},{5,9},{9,5},{13,17},{1... | collective-permute-start | bytes 589832 | tf_op jit(solution)/shard_map/ppermute | solution.py:331
  28.4 0.8 %copy-start.9 = (f32[64,256]{1,0:T(8,128)S(1)}, f32[64,256]{1,0:T(8,128)}, u32[]{:S(2)}) copy-start(f32[64,256]{1,0:T(8,128)} %constant.59.clone.refs_11_) | copy-start | bytes 196612
  29.3 0.8 %copy-start.10 = (f32[64,256]{1,0:T(8,128)S(1)}, f32[64,256]{1,0:T(8,128)}, u32[]{:S(2)}) copy-start(f32[64,256]{1,0:T(8,128)} %constant.53.clone.refs_5_) | copy-start | bytes 196612
  30.1 34.2 %copy-start.13 = (f32[128,128]{1,0:T(8,128)S(1)}, f32[128,128]{1,0:T(8,128)}, u32[]{:S(2)}) copy-start(f32[128,128]{1,0:T(8,128)} %logits_ref.3) | copy-start | bytes 196612
  37.8 8.7 %collective-permute-start.9 = (f32[2,128]{1,0:T(2,128)S(1)}, f32[2,128]{1,0:T(2,128)S(1)}, u32[]{:S(2)}, u32[]{:S(2)}) collective-permute-start(f32[2,128]{1,0:T(2,128)S(1)} %get-tuple-element.15), channel_id=1, source_target_pairs={{0,8},{4,12},{8,0},{12,4},{16,24},{20,28},{24,16},{28,20},{1,9},{5... | collective-permute-start | bytes 3080 | tf_op jit(solution)/shard_map/ppermute | solution.py:300
  46.5 4.6 %collective-permute-start.10 = (f32[2,128]{1,0:T(2,128)S(1)}, f32[2,128]{1,0:T(2,128)S(1)}, u32[]{:S(2)}, u32[]{:S(2)}) collective-permute-start(f32[2,128]{1,0:T(2,128)S(1)} %add.21), channel_id=1, source_target_pairs={{0,16},{4,20},{8,24},{12,28},{16,0},{20,4},{24,8},{28,12},{1,17},{... | collective-permute-start | bytes 3080 | tf_op jit(solution)/shard_map/ppermute | solution.py:300
  51.1 1.1 %collective-permute-start.11 = (f32[2,128]{1,0:T(2,128)S(1)}, f32[2,128]{1,0:T(2,128)S(1)}, u32[]{:S(2)}, u32[]{:S(2)}) collective-permute-start(f32[2,128]{1,0:T(2,128)S(1)} %add.22), channel_id=1, source_target_pairs={{0,4},{4,0},{8,12},{12,8},{16,20},{20,16},{24,28},{28,24},{1,5},{5... | collective-permute-start | bytes 3080 | tf_op jit(solution)/shard_map/ppermute | solution.py:300
  52.2 5.9 %collective-permute-start.12 = (f32[2,128]{1,0:T(2,128)S(1)}, f32[2,128]{1,0:T(2,128)S(1)}, u32[]{:S(2)}, u32[]{:S(2)}) collective-permute-start(f32[2,128]{1,0:T(2,128)S(1)} %add.23), channel_id=1, source_target_pairs={{0,1},{1,0},{2,3},{3,2},{4,5},{5,4},{6,7},{7,6},{8,9},{9,8},{10,11... | collective-permute-start | bytes 3080 | tf_op jit(solution)/shard_map/ppermute | solution.py:300
  58.1 5.0 %collective-permute-start.13 = (f32[2,128]{1,0:T(2,128)S(1)}, f32[2,128]{1,0:T(2,128)S(1)}, u32[]{:S(2)}, u32[]{:S(2)}) collective-permute-start(f32[2,128]{1,0:T(2,128)S(1)} %add.24), channel_id=1, source_target_pairs={{0,2},{1,3},{2,0},{3,1},{4,6},{5,7},{6,4},{7,5},{8,10},{9,11},{10,... | collective-permute-start | bytes 3080 | tf_op jit(solution)/shard_map/ppermute | solution.py:300

commit v2 on v1

--- a/solution.py
+++ b/solution.py
@@ -1,3 +1,4 @@
+import functools
 import math
 
 import jax
@@ -85,29 +86,48 @@
     core_re, core_im = wave_re[:, core], wave_im[:, core]
     core_cols = np.concatenate([cat(core_re, -core_im), cat(core_im, core_re)] * 2, axis=0)
     core_rows = 2.0 * cat(row_re[:, core].T, row_im[:, core].T)
-    return [
-        jnp.asarray(t, jnp.float32)
-        for t in (
-            analyse_cols,
-            analyse_rows,
-            field_cols,
-            field_rows,
-            up_rows,
-            up_cols,
-            down_cols,
-            down_rows,
-            back_cols,
-            back_rows,
-            core_cols,
-            core_rows,
-        )
+    parts = [
+        ("field_cols", field_cols),
+        ("up_cols", up_cols),
+        ("back_cols", back_cols),
+        ("core_cols", core_cols),
+        ("analyse_rows", analyse_rows),
+        ("down_rows", down_rows),
     ]
-
-
-def pack_columns(logits_ref, target_ref, weight_ref, a_ref, b_ref):
+    side = [
+        [("analyse_cols", analyse_cols), ("up_rows", up_rows)],
+        [
+            ("down_cols", down_cols),
+            ("core_rows", core_rows),
+            ("field_rows", field_rows),
+            ("back_rows", back_rows),
+        ],
+    ]
+    place, rows = {}, []
+    start = 0
+    for name, part in parts:
+        place[name] = (start, 0, part.shape)
+        rows.append(part)
+        start += part.shape[0]
+    columns = []
+    for left, stack in zip((0, LANES), side, strict=True):
+        top = start
+        column = []
+        for name, part in stack:
+            place[name] = (top, left, part.shape)
+            column.append(np.pad(part, ((0, 0), (0, LANES - part.shape[1]))))
+            top += part.shape[0]
+        columns.append(np.concatenate(column, axis=0))
+    height = max(column.shape[0] for column in columns)
+    columns = [np.pad(c, ((0, height - c.shape[0]), (0, 0))) for c in columns]
+    rows.append(np.concatenate(columns, axis=1))
+    return jnp.asarray(np.concatenate(rows, axis=0), jnp.float32), place
+
+
+def pack_columns(own_ref, a_ref, b_ref):
     half = HALO
     odd = lax.rem(lax.axis_index("col"), 2) == 1
-    values = [ref[...] for ref in (logits_ref, target_ref, weight_ref)]
+    values = [own_ref[index] for index in range(3)]
     turned = [pltpu.roll(value, half, 1) for value in values]
     low = lax.broadcasted_iota(jnp.int32, values[0].shape, 1) < half
     rows = values[0].shape[0]
@@ -125,11 +145,12 @@
     b_ref[rows:] = jnp.where(odd, to_right[1], to_left[1])
 
 
-def widen(logits_ref, target_ref, weight_ref, a_ref, b_ref, centre_ref, up_ref, down_ref):
+def widen(own_ref, a_ref, b_ref, shards_ref, centre_ref, up_ref, down_ref, bank_ref):
+    bank_ref[...] = shards_ref[...]
     half = HALO
     odd = lax.rem(lax.axis_index("col"), 2) == 1
     odd_row = lax.rem(lax.axis_index("row"), 2) == 1
-    values = [ref[...] for ref in (logits_ref, target_ref, weight_ref)]
+    values = [own_ref[index] for index in range(3)]
     rows = values[0].shape[0]
     low = lax.broadcasted_iota(jnp.int32, values[0].shape, 1) < half
     got_a, got_b = a_ref[...], b_ref[...]
@@ -154,45 +175,40 @@
 
 def step_kernel(
     order,
+    place,
     bank_ref,
     centre_ref,
     up_ref,
     down_ref,
-    analyse_cols,
-    analyse_rows,
-    field_cols,
-    field_rows,
-    up_rows,
-    up_cols,
-    down_cols,
-    down_rows,
-    back_cols,
-    back_rows,
-    core_cols,
-    core_rows,
+    table_ref,
     grad_ref,
     sums_ref,
     flat_ref,
 ):
-    odd_row = lax.rem(lax.axis_index("row"), 2) == 1
+    row_place = lax.axis_index("row")
+    odd_row = lax.rem(row_place, 2) == 1
+    at_top, at_bottom = row_place == 0, row_place == lax.axis_size("row") - 1
     grid = 2 * BAND
     fold = LANES // BAND
     per = BAND // fold
 
+    def table(name):
+        top, left, shape = place[name]
+        return table_ref[top : top + shape[0], left : left + shape[1]]
+
     def padded(index):
         first, second = up_ref[index], down_ref[index]
-        return jnp.concatenate(
-            [
-                jnp.where(odd_row, first, second),
-                centre_ref[index],
-                jnp.where(odd_row, second, first),
-            ],
-            axis=0,
-        )
-
-    weight = padded(2)
+        above = jnp.where(odd_row, first, second)
+        below = jnp.where(odd_row, second, first)
+        return jnp.concatenate([above, centre_ref[index], below], axis=0)
+
+    cell_row = lax.broadcasted_iota(jnp.int32, (centre_ref.shape[1] + 2 * HALO, 1), 0)
+    first_row = jnp.where(at_top, HALO, 0)
+    last_row = jnp.where(at_bottom, cell_row.shape[0] - HALO, cell_row.shape[0])
+    inside = jnp.logical_and(cell_row >= first_row, cell_row < last_row)
+    weight = jnp.where(inside, padded(2), 0.0)
     mask = jnp.where(weight > 0.0, jax.nn.sigmoid(padded(0)), 0.0)
-    target = padded(1)
+    target = jnp.where(inside, padded(1), 0.0)
     pad_width = mask.shape[0]
     core = slice(HALO, pad_width - HALO)
 
@@ -224,28 +240,28 @@
     pairs = [(c, k) for c in range(CONDITIONS) for k in range(KERNELS)]
     spectra = [spread(c, k) for c, k in pairs]
 
-    half = dot(mask, analyse_cols[...])
-    both = dot(analyse_rows[...], half)
+    half = dot(mask, table("analyse_cols"))
+    both = dot(table("analyse_rows"), half)
     wide_lane = lax.broadcasted_iota(jnp.int32, (BAND, LANES), 1)
     turned = pltpu.roll(both[BAND:], LANES // 2, 1)
     spectrum = both[:BAND] + jnp.where(wide_lane < LANES // 2, turned, -turned)
 
     products = jnp.concatenate([s * spectrum for s in spectra], axis=0)
-    halves = dot(products, field_cols[...])
+    halves = dot(products, table("field_cols"))
     fields = []
     squares = [0.0] * CONDITIONS
     for index, (condition, _) in enumerate(pairs):
         rows = halves[index * BAND : (index + 1) * BAND]
         stacked = jnp.concatenate([rows[:, :LANES], rows[:, LANES:]], axis=0)
-        field = dot(field_rows[...], stacked)
+        field = dot(table("field_rows"), stacked)
         fields.append(field)
         squares[condition] = squares[condition] + field * field
 
-    tall = dot(up_rows[...], jnp.concatenate(squares, axis=1))
+    tall = dot(table("up_rows"), jnp.concatenate(squares, axis=1))
     tall = jnp.concatenate(
         [tall[:, c * LANES : (c + 1) * LANES] for c in range(CONDITIONS)], axis=0
     )
-    intensities = dot(tall, up_cols[...])
+    intensities = dot(tall, table("up_cols"))
 
     slopes = []
     loss = 0.0
@@ -256,11 +272,11 @@
         scaled = weight * error
         loss = loss + (scaled * error)[core, core]
         slopes.append((2.0 * SHARPNESS * dose) * scaled * (resist * (1.0 - resist)))
-    narrow = dot(jnp.concatenate(slopes, axis=0), down_cols[...])
+    narrow = dot(jnp.concatenate(slopes, axis=0), table("down_cols"))
     narrow = jnp.concatenate(
         [narrow[c * pad_width : (c + 1) * pad_width] for c in range(CONDITIONS)], axis=1
     )
-    coarse = dot(down_rows[...], narrow)
+    coarse = dot(table("down_rows"), narrow)
 
     weighted = jnp.concatenate(
         [
@@ -269,30 +285,30 @@
         ],
         axis=0,
     )
-    backs = dot(weighted, back_cols[...])
+    backs = dot(weighted, table("back_cols"))
     total = 0.0
     for index in range(len(pairs)):
         rows = backs[index * grid : (index + 1) * grid]
         stacked = jnp.concatenate([rows[:, :LANES], rows[:, LANES:]], axis=0)
-        total = total + spectra[index] * dot(back_rows[...], stacked)
-
-    across = dot(total, core_cols[...])
+        total = total + spectra[index] * dot(table("back_rows"), stacked)
+
+    across = dot(total, table("core_cols"))
     core_width = across.shape[1] // 2
     stacked = jnp.concatenate([across[:, :core_width], across[:, core_width:]], axis=0)
-    gradient = dot(core_rows[...], stacked)
+    gradient = dot(table("core_rows"), stacked)
     own = mask[core, core]
     cells = gradient * own * (1.0 - own)
     grad_ref[...] = cells
     square = jnp.sum(jnp.sum(cells * cells, axis=0, keepdims=True), axis=1, keepdims=True)
     loss = jnp.sum(jnp.sum(loss, axis=0, keepdims=True), axis=1, keepdims=True)
-    sums_ref[0:1, :] = jnp.broadcast_to(square, (1, LANES))
-    sums_ref[1:2, :] = jnp.broadcast_to(loss, (1, LANES))
-
-
-def axis_rounds(axis):
-    count = lax.axis_size(axis)
-    bits = [1 << b for b in range(count.bit_length() - 1)]
-    return bits[1:] + bits[:1] if axis == "row" else bits
+    sums = jnp.concatenate([square, loss], axis=0)
+    sums_ref[...] = jnp.broadcast_to(sums[None], sums_ref.shape)
+
+
+def rounds():
+    row = [("row", 1 << b) for b in range(lax.axis_size("row").bit_length() - 1)]
+    col = [("col", 1 << b) for b in range(lax.axis_size("col").bit_length() - 1)]
+    return col[:1] + row[1:2] + col[1:] + row[2:] + row[:1]
 
 
 def swap(value, axis, bit):
@@ -300,42 +316,29 @@
     return lax.ppermute(value, axis, [(i, i ^ bit) for i in range(count)])
 
 
-def gather_bank(kernels):
-    held = kernels[None]
-    crossed = []
-    for axis in ("col", "row"):
-        for bit in axis_rounds(axis):
-            got = swap(held, axis, bit)
-            high = (lax.axis_index(axis) & bit) != 0
-            held = jnp.concatenate(
-                [jnp.where(high, got, held), jnp.where(high, held, got)], axis=0
-            )
-            crossed.append((axis, bit))
-    rows, cols = lax.axis_size("row"), lax.axis_size("col")
-    place = {}
-    for row in range(rows):
-        for col in range(cols):
-            index = 0
-            for level, (axis, bit) in enumerate(crossed):
-                own = row if axis == "row" else col
-                index += (1 << level) * ((own & bit) != 0)
-            place[row * cols + col] = index
-    return held, place
-
-
-def pair_swap(value, axis, first):
+def small(megabytes):
+    return pltpu.CompilerParams(vmem_limit_bytes=megabytes * 1024 * 1024)
+
+
+def to_all(value):
+    return lax.all_to_all(value, ("row", "col"), 0, 0)
+
+
+def pair_swap(value, axis, first, wrap=False):
     count = lax.axis_size(axis)
     pairs = []
     for low in range(first, count - 1, 2):
         pairs += [(low, low + 1), (low + 1, low)]
+    if wrap and first and count % 2 == 0:
+        pairs += [(0, count - 1), (count - 1, 0)]
     return lax.ppermute(value, axis, pairs)
 
 
-def total_sum(value):
-    for axis in ("row", "col"):
-        for bit in axis_rounds(axis):
-            value = value + swap(value, axis, bit)
-    return value
+def finish(cell_count, own_ref, cells_ref, sums_ref, logits_ref, loss_ref):
+    total = jnp.sum(sums_ref[...], axis=0) / cell_count
+    scale = STEP / jnp.sqrt(total[0:1] + EPSILON)
+    logits_ref[...] = own_ref[0] - cells_ref[...] * scale
+    loss_ref[...] = total[1:2, 0:1]
 
 
 def shards(mask_logits, target, weight, kernels):
@@ -344,45 +347,59 @@
     rows, cols = lax.axis_size("row"), lax.axis_size("col")
     f32 = jnp.float32
 
-    bank, place = gather_bank(kernels)
+    def struct(*shape):
+        return jax.ShapeDtypeStruct(shape, f32)
+
+    packed = struct(core_width * 3 // 2, core_width)
+    own = jnp.stack([mask_logits, target, weight])
+    slab_a, slab_b = pl.pallas_call(
+        pack_columns,
+        out_shape=(packed, packed),
+        in_specs=[VMEM],
+        out_specs=(VMEM,) * 2,
+        compiler_params=small(4),
+    )(own)
+    bank = jnp.broadcast_to(kernels[None], (rows * cols,) + kernels.shape)
+    got_a, got_b = pair_swap(slab_a, "col", 0), pair_swap(slab_b, "col", 1)
+    slab = struct(3, HALO, pad_width)
+    centre, up, down, bank = pl.pallas_call(
+        widen,
+        out_shape=(struct(3, core_width, pad_width), slab, slab, struct(*bank.shape)),
+        in_specs=[VMEM] * 4,
+        out_specs=(VMEM,) * 4,
+        compiler_params=small(8),
+    )(own, got_a, got_b, bank)
+    up, down = pair_swap(up, "row", 0), pair_swap(down, "row", 1, wrap=True)
+    bank = to_all(bank)
     pieces = kernels.shape[1] // LANES
     if kernels.shape[1] % LANES:
-        whole = bank[np.array([place[device] for device in range(rows * cols)])]
-        bank = jnp.swapaxes(whole, 0, 1).reshape(1, CONDITIONS, -1)
-        place, pieces = {0: 0}, bank.shape[2] // LANES
-    order = [(place[device], piece) for device in sorted(place) for piece in range(pieces)]
-
-    packed = jax.ShapeDtypeStruct((core_width * 3 // 2, core_width), f32)
-    slab_a, slab_b = pl.pallas_call(
-        pack_columns, out_shape=(packed, packed), in_specs=[VMEM] * 3, out_specs=(VMEM,) * 2
-    )(mask_logits, target, weight)
-    got_a, got_b = pair_swap(slab_a, "col", 0), pair_swap(slab_b, "col", 1)
-    slab = jax.ShapeDtypeStruct((3, HALO, pad_width), f32)
-    centre, up, down = pl.pallas_call(
-        widen,
-        out_shape=(jax.ShapeDtypeStruct((3, core_width, pad_width), f32), slab, slab),
+        bank = jnp.swapaxes(bank, 0, 1).reshape(1, CONDITIONS, -1)
+        pieces = bank.shape[2] // LANES
+    order = [(device, piece) for device in range(bank.shape[0]) for piece in range(pieces)]
+
+    consts, place = tables(pad_width, HALO)
+    grad_cells, sums = pl.pallas_call(
+        functools.partial(step_kernel, order, place),
+        out_shape=(
+            struct(core_width, core_width),
+            struct(rows * cols, 2, LANES),
+        ),
         in_specs=[VMEM] * 5,
-        out_specs=(VMEM,) * 3,
-    )(mask_logits, target, weight, got_a, got_b)
-    up, down = pair_swap(up, "row", 0), pair_swap(down, "row", 1)
-
-    consts = tables(pad_width, HALO)
-    grad_cells, sums = pl.pallas_call(
-        lambda *refs: step_kernel(order, *refs),
-        out_shape=(
-            jax.ShapeDtypeStruct((core_width, core_width), f32),
-            jax.ShapeDtypeStruct((2, LANES), f32),
-        ),
-        in_specs=[VMEM] * (4 + len(consts)),
         out_specs=(VMEM,) * 2,
         scratch_shapes=[pltpu.VMEM((CONDITIONS, len(order), LANES), f32)],
-        compiler_params=pltpu.CompilerParams(vmem_limit_bytes=32 * 1024 * 1024),
-    )(bank, centre, up, down, *consts)
-
-    sums = total_sum(sums)
+        compiler_params=pltpu.CompilerParams(vmem_limit_bytes=16 * 1024 * 1024),
+    )(bank, centre, up, down, consts)
+
+    sums = to_all(sums)
     cell_count = rows * cols * core_width * core_width
-    norm = jnp.sqrt(sums[0:1] / cell_count + EPSILON)
-    return (mask_logits - STEP * grad_cells / norm, sums[1, 0] / cell_count)
+    new_logits, loss = pl.pallas_call(
+        functools.partial(finish, cell_count),
+        out_shape=(struct(core_width, core_width), struct(1, 1)),
+        in_specs=[VMEM] * 3,
+        out_specs=(VMEM,) * 2,
+        compiler_params=small(4),
+    )(own, grad_cells, sums)
+    return (new_logits, loss[0, 0])
 
 
 def solution(mesh):

time: 66.5 us -> 43.2 us (0.65)
  starting transfers between devices: 31.2 us -> 6.61 us
  blocking collectives: 0 us -> 23.1 us
  waiting for transfers between devices: 15.7 us -> 2.14 us
  local copies, waits for them, and re-layouts: 3.51 us -> 0.72 us
  Pallas kernels: 11.5 us -> 8.73 us
  between operations: 2.66 us -> 0.68 us
    ppermute x10 -> x0, starting transfers between devices: 28.1 us -> none  [swap(): return lax.ppermute(value, axis, [(i, i ^ bit) for i in range(count)])]
    all_to_all x0 -> x2, blocking collectives: none -> 23.1 us  [to_all(): return lax.all_to_all(value, ('row', 'col'), 0, 0)]
    ppermute x10 -> x0, waiting for transfers between devices: 12.6 us -> none  [swap(): return lax.ppermute(value, axis, [(i, i ^ bit) for i in range(count)])]
    ppermute x4, starting transfers between devices: 3.03 us -> 6.61 us  [pair_swap(): return lax.ppermute(value, axis, pairs)]
    unnamed x32 -> x2, local copies, waits for them, and re-layouts: 2.99 us -> 0.01 us
    pallas_call x3 -> x4, Pallas kernels: 11.5 us -> 8.73 us  [the longest x1 7.74 us: shards(): pl.pallas_call(functools.partial(step_kernel, order, place), out_shape=(s...]
    ppermute x4, waiting for transfers between devices: 3.16 us -> 2.14 us  [pair_swap(): return lax.ppermute(value, axis, pairs)]
    another operation x0 -> x1, other arithmetic: none -> 1.01 us  [shards(): own = jnp.stack([mask_logits, target, weight])]
  transfers between devices with their start and end apart: 14 -> 4, of which waited for: 10 -> 1; matrix products, arithmetic and copies ran while one was open for 0% -> 0% of each run, Pallas kernels for 6% -> 0%
where the time goes in v2:
time: 43.2 us; the launch traced here: 43 us
  blocking collectives  23.1 us (53%)
  Pallas kernels  8.73 us (20%)
  starting transfers between devices  6.61 us (15%)
  waiting for transfers between devices  2.14 us (5%)
  other arithmetic  1.01 us (2%)
  local copies, waits for them, and re-layouts  0.72 us (2%)
  between operations  0.68 us (2%)
    all_to_all x2, blocking collectives, to_all(): return lax.all_to_all(value, ('row', 'col'), 0, 0)  23.1 us
    pallas_call x1, Pallas kernels, shards(): pl.pallas_call(functools.partial(step_kernel, order, place), out_shape=(s...  7.74 us
    ppermute x4, starting transfers between devices, pair_swap(): return lax.ppermute(value, axis, pairs)  6.61 us
    ppermute x4, waiting for transfers between devices, pair_swap(): return lax.ppermute(value, axis, pairs)  2.14 us
    another operation x1, other arithmetic, shards(): own = jnp.stack([mask_logits, target, weight])  1.01 us
  transfers between devices with their start and end apart: 4, of which 1 were waited for; matrix products, arithmetic and copies ran while one was open for 0% of the time, Pallas kernels for 0%

profile of v2, /device:TPU:0, one launch (start us, length us, event | category | flops | bytes accessed | tf_op | source)
XLA Modules:
  0.0 43.0 jit_solution(13299075656908814895)
XLA Ops:
  0.6 0.0 copy-start
  0.6 1.0 %pad_maximum_fusion.own_ref = f32[3,128,128]{2,1,0:T(8,128)S(1)} fusion(f32[1,128,128]{2,1,0:T(8,128)} %bitcast.4, f32[1,128,128]{2,1,0:T(8,128)} %bitcast.5, f32[1,128,128]{2,1,0:T(8,128)} %bitcast.6), kind=kLoop, calls=%fused_computation | loop fusion | flops 98304 | bytes 393216 | tf_op jit(solution)/shard_map/stack | solution.py:354
  1.7 0.1 shard_map.68
  1.8 3.1 %collective-permute-start = (f32[192,128]{1,0:T(8,128)S(1)}, f32[192,128]{1,0:T(8,128)S(1)}, u32[]{:S(2)}, u32[]{:S(2)}) collective-permute-start(f32[192,128]{1,0:T(8,128)S(1)} %get-tuple-element.12), channel_id=1, source_target_pairs={{0,1},{1,0},{2,3},{3,2},{4,5},{5,4},{6,7},{7,6},{8,9},{9,8},{10,11... | collective-permute-start | bytes 294920 | tf_op jit(solution)/shard_map/ppermute | solution.py:334
  4.9 0.7 %collective-permute-start.1 = (f32[192,128]{1,0:T(8,128)S(1)}, f32[192,128]{1,0:T(8,128)S(1)}, u32[]{:S(2)}, u32[]{:S(2)}) collective-permute-start(f32[192,128]{1,0:T(8,128)S(1)} %get-tuple-element.13), channel_id=1, source_target_pairs={{1,2},{2,1},{5,6},{6,5},{9,10},{10,9},{13,14},{14,13},{17,18},{18,... | collective-permute-start | bytes 294920 | tf_op jit(solution)/shard_map/ppermute | solution.py:334
  5.5 2.1 %collective-permute-done.a_ref = f32[192,128]{1,0:T(8,128)S(1)} collective-permute-done((f32[192,128]{1,0:T(8,128)S(1)}, f32[192,128]{1,0:T(8,128)S(1)}, u32[]{:S(2)}, u32[]{:S(2)}) %collective-permute-start) | collective-permute-done | bytes 98336 | tf_op jit(solution)/shard_map/ppermute | solution.py:334
  7.7 0.0 collective-permute-done.1.b_ref
  7.7 0.7 %broadcast_in_dim.2.shards_ref = f32[32,2,384]{2,1,0:T(2,128)S(1)} broadcast(f32[2,384]{1,0:T(2,128)} %param.8), dimensions={1,2} | broadcast | bytes 101376 | tf_op jit(solution)/shard_map/broadcast_in_dim | solution.py:362
  8.4 0.2 shard_map.69
  8.6 0.1 collective-permute-start.2
  8.7 2.8 %collective-permute-start.3 = (f32[3,64,256]{2,1,0:T(8,128)S(1)}, f32[3,64,256]{2,1,0:T(8,128)S(1)}, u32[]{:S(2)}, u32[]{:S(2)}) collective-permute-start(f32[3,64,256]{2,1,0:T(8,128)S(1)} %get-tuple-element.17), channel_id=1, source_target_pairs={{4,8},{8,4},{12,16},{16,12},{20,24},{24,20},{0,28},{28,0},{5,9},{9... | collective-permute-start | bytes 589832 | tf_op jit(solution)/shard_map/ppermute | solution.py:334
  11.4 14.1 %all_to_all.10.bank_ref = f32[32,2,384]{2,1,0:T(2,128)S(1)} all-to-all(f32[32,2,384]{2,1,0:T(2,128)S(1)} %get-tuple-element.14), channel_id=1, replica_groups=mesh['row'=8,'col'=4] {'row','col'}, dimensions={0} | all-to-all | bytes 196608 | tf_op jit(solution)/shard_map/all_to_all | solution.py:324
  25.6 0.0 collective-permute-done.2.up_ref
  25.6 0.0 collective-permute-done.3.down_ref
  25.6 0.0 copy-done
  25.6 7.7 %shard_map.70 = (f32[128,128]{1,0:T(8,128)S(1)}, f32[32,2,128]{2,1,0:T(2,128)S(1)}) custom-call(f32[32,2,384]{2,1,0:T(2,128)S(1)} %all_to_all.10.bank_ref, f32[3,128,256]{2,1,0:T(8,128)S(1)} %get-tuple-element.15.centre_ref, f32[3,64,256]{2,1,0:T(8,128)S(1)} %collective-permute-done.2.up_ref, f32[3,64,256]{2,1,0:T(8,128)S(1)} %collective-permute-done.3.down_ref, ...), custom_call_target="tpu_custom_call" | custom-call | tf_op jit(solution)/shard_map/pallas_call | solution.py:381
  33.3 9.0 %all_to_all.11.sums_ref = f32[32,2,128]{2,1,0:T(2,128)S(1)} all-to-all(f32[32,2,128]{2,1,0:T(2,128)S(1)} %get-tuple-element.19), channel_id=1, replica_groups=mesh['row'=8,'col'=4] {'row','col'}, dimensions={0} | all-to-all | bytes 65536 | tf_op jit(solution)/shard_map/all_to_all | solution.py:324
  42.3 0.7 %shard_map.71 = (f32[128,128]{1,0:T(8,128)}, f32[1,1]{1,0:T(1,128)}) custom-call(f32[3,128,128]{2,1,0:T(8,128)S(1)} %pad_maximum_fusion.own_ref, f32[128,128]{1,0:T(8,128)S(1)} %get-tuple-element.18.cells_ref, f32[32,2,128]{2,1,0:T(2,128)S(1)} %all_to_all.11.sums_ref), custom_call_target="tpu_custom_call" | custom-call | tf_op jit(solution)/shard_map/pallas_call | solution.py:395
Async XLA Ops:
  0.6 25.0 %copy-start = (f32[1152,256]{1,0:T(8,128)S(1)}, f32[1152,256]{1,0:T(8,128)}, u32[]{:S(2)}) copy-start(f32[1152,256]{1,0:T(8,128)} %constant.2.clone.table_ref) | copy-start | bytes 3538948
  1.8 5.9 %collective-permute-start = (f32[192,128]{1,0:T(8,128)S(1)}, f32[192,128]{1,0:T(8,128)S(1)}, u32[]{:S(2)}, u32[]{:S(2)}) collective-permute-start(f32[192,128]{1,0:T(8,128)S(1)} %get-tuple-element.12), channel_id=1, source_target_pairs={{0,1},{1,0},{2,3},{3,2},{4,5},{5,4},{6,7},{7,6},{8,9},{9,8},{10,11... | collective-permute-start | bytes 294920 | tf_op jit(solution)/shard_map/ppermute | solution.py:334
  4.9 2.8 %collective-permute-start.1 = (f32[192,128]{1,0:T(8,128)S(1)}, f32[192,128]{1,0:T(8,128)S(1)}, u32[]{:S(2)}, u32[]{:S(2)}) collective-permute-start(f32[192,128]{1,0:T(8,128)S(1)} %get-tuple-element.13), channel_id=1, source_target_pairs={{1,2},{2,1},{5,6},{6,5},{9,10},{10,9},{13,14},{14,13},{17,18},{18,... | collective-permute-start | bytes 294920 | tf_op jit(solution)/shard_map/ppermute | solution.py:334
  8.6 17.0 %collective-permute-start.2 = (f32[3,64,256]{2,1,0:T(8,128)S(1)}, f32[3,64,256]{2,1,0:T(8,128)S(1)}, u32[]{:S(2)}, u32[]{:S(2)}) collective-permute-start(f32[3,64,256]{2,1,0:T(8,128)S(1)} %get-tuple-element.16), channel_id=1, source_target_pairs={{0,4},{4,0},{8,12},{12,8},{16,20},{20,16},{24,28},{28,24},{1,5},{5... | collective-permute-start | bytes 589832 | tf_op jit(solution)/shard_map/ppermute | solution.py:334
  8.7 16.9 %collective-permute-start.3 = (f32[3,64,256]{2,1,0:T(8,128)S(1)}, f32[3,64,256]{2,1,0:T(8,128)S(1)}, u32[]{:S(2)}, u32[]{:S(2)}) collective-permute-start(f32[3,64,256]{2,1,0:T(8,128)S(1)} %get-tuple-element.17), channel_id=1, source_target_pairs={{4,8},{8,4},{12,16},{16,12},{20,24},{24,20},{0,28},{28,0},{5,9},{9... | collective-permute-start | bytes 589832 | tf_op jit(solution)/shard_map/ppermute | solution.py:334

commit v3 on v2

--- a/solution.py
+++ b/solution.py
@@ -26,12 +26,27 @@
 
 def dot(first, second):
     return lax.dot_general(
-        first,
-        second,
-        (((1,), (0,)), ((), ())),
-        precision=lax.Precision.HIGHEST,
-        preferred_element_type=jnp.float32,
-    )
+        first, second, (((1,), (0,)), ((), ())), preferred_element_type=jnp.float32
+    )
+
+
+def split(value, count):
+    parts = []
+    for index in range(count):
+        part = value.astype(jnp.bfloat16)
+        parts.append(part)
+        if index + 1 < count:
+            value = value - part.astype(jnp.float32)
+    return parts
+
+
+def split_table(table, count):
+    parts = []
+    for _ in range(count):
+        part = table.astype(np.float32).astype(jnp.bfloat16)
+        parts.append(part)
+        table = table - part.astype(np.float64)
+    return parts
 
 
 def tables(pad_width, margin):
@@ -48,80 +63,56 @@
     coarse_re, coarse_im = wave_re[:, ::stride], wave_im[:, ::stride]
     crow_re, crow_im = row_re[:, ::stride], row_im[:, ::stride]
     core = slice(margin, pad_width - margin)
+    core_re, core_im = wave_re[:, core], wave_im[:, core]
     steps = (place[:, None] - stride * np.arange(grid)[None, :]) % pad_width
     diffs = np.arange(1, BAND)
-    between = (
-        1.0
-        + 2.0
-        * np.cos(2.0 * math.pi / pad_width * (steps[..., None] * diffs % pad_width)).sum(-1)
-    ) / grid
-
-    def cat(*blocks):
+    phases = (steps[..., None] * diffs % pad_width) * (2.0 * math.pi / pad_width)
+    between = (1.0 + 2.0 * np.cos(phases).sum(-1)) / grid
+
+    def beside(*blocks):
         return np.concatenate(blocks, axis=1)
 
-    analyse_cols = cat(wave_re.T, wave_im.T, -wave_im.T, wave_re.T)
-    analyse_rows = np.concatenate([row_re, row_im], axis=0)
-    field_cols = np.concatenate(
-        [
-            cat(coarse_re, -coarse_im, -coarse_im, -coarse_re),
-            cat(coarse_im, coarse_re, coarse_re, -coarse_im),
-        ]
-        * 2,
-        axis=0,
-    )
-    field_rows = cat(crow_re.T, crow_im.T)
-    up_rows = between
-    up_cols = np.concatenate([between.T, between.T], axis=0)
-    down_cols = cat(between, between)
-    down_rows = between.T
+    def below(*blocks):
+        return np.concatenate(blocks, axis=0)
+
+    found = {}
+    h, l = split_table(beside(wave_re.T, wave_im.T, -wave_im.T, wave_re.T), 2)
+    found["analyse_cols"] = beside(h, l)
+    found["analyse_rows"] = below(*split_table(below(row_re, row_im), 3))
+    from_re = beside(coarse_re, -coarse_im, -coarse_im, -coarse_re)
+    from_im = beside(coarse_im, coarse_re, coarse_re, -coarse_im)
+    h, m, l = split_table(below(from_re, from_im, from_re, from_im), 3)
+    found["field_cols"] = below(h, h, m, m, h, l)
+    h, m, l = split_table(beside(crow_re.T, crow_im.T), 3)
+    found["field_rows"] = beside(h, h, h, m, m, l)
+    h, m, l = split_table(between, 3)
+    found["up_rows"] = beside(h, h, h, m, m, l)
+    found["up_cols"] = below(h.T, h.T, h.T, m.T, m.T, l.T)
+    found["down_cols"] = beside(h, h, m, m)
+    found["down_rows"] = below(h.T, m.T)
+    h, l = split_table(below(crow_re, crow_im), 2)
+    found["back_rows"] = beside(h, h, l)
     c_re, c_im = coarse_re.T, coarse_im.T
-    back_cols = np.concatenate(
-        [
-            cat(c_re, c_im, c_im, -c_re, -c_im, c_re, c_re, c_im),
-            cat(-c_im, c_re, c_re, c_im, -c_re, -c_im, -c_im, c_re),
-        ],
-        axis=0,
-    )
-    back_rows = cat(crow_re, crow_im)
-    core_re, core_im = wave_re[:, core], wave_im[:, core]
-    core_cols = np.concatenate([cat(core_re, -core_im), cat(core_im, core_re)] * 2, axis=0)
-    core_rows = 2.0 * cat(row_re[:, core].T, row_im[:, core].T)
-    parts = [
-        ("field_cols", field_cols),
-        ("up_cols", up_cols),
-        ("back_cols", back_cols),
-        ("core_cols", core_cols),
-        ("analyse_rows", analyse_rows),
-        ("down_rows", down_rows),
-    ]
-    side = [
-        [("analyse_cols", analyse_cols), ("up_rows", up_rows)],
-        [
-            ("down_cols", down_cols),
-            ("core_rows", core_rows),
-            ("field_rows", field_rows),
-            ("back_rows", back_rows),
-        ],
-    ]
-    place, rows = {}, []
-    start = 0
-    for name, part in parts:
-        place[name] = (start, 0, part.shape)
-        rows.append(part)
-        start += part.shape[0]
-    columns = []
-    for left, stack in zip((0, LANES), side, strict=True):
-        top = start
-        column = []
-        for name, part in stack:
-            place[name] = (top, left, part.shape)
-            column.append(np.pad(part, ((0, 0), (0, LANES - part.shape[1]))))
-            top += part.shape[0]
-        columns.append(np.concatenate(column, axis=0))
-    height = max(column.shape[0] for column in columns)
-    columns = [np.pad(c, ((0, height - c.shape[0]), (0, 0))) for c in columns]
-    rows.append(np.concatenate(columns, axis=1))
-    return jnp.asarray(np.concatenate(rows, axis=0), jnp.float32), place
+    h, l = split_table(
+        below(beside(c_re, c_im, c_im, -c_re), beside(-c_im, c_re, c_re, c_im)), 2
+    )
+    found["back_cols"] = below(h, h, l)
+    from_re, from_im = beside(core_re, -core_im), beside(core_im, core_re)
+    h, l = split_table(below(from_re, from_im, from_re, from_im), 2)
+    found["core_cols"] = below(h, h, l)
+    h, l = split_table(2.0 * beside(row_re[:, core].T, row_im[:, core].T), 2)
+    found["core_rows"] = beside(h, h, l)
+
+    arrays, where = [], {}
+    for index, width in enumerate((2 * LANES, 3 * LANES)):
+        start, stack = 0, []
+        for name, table in found.items():
+            if (table.shape[1] > 2 * LANES) == (index == 1):
+                where[name] = (index, start, table.shape)
+                stack.append(np.pad(table, ((0, 0), (0, width - table.shape[1]))))
+                start += table.shape[0]
+        arrays.append(jnp.asarray(np.concatenate(stack, axis=0)))
+    return arrays, where
 
 
 def pack_columns(own_ref, a_ref, b_ref):
@@ -180,7 +171,8 @@
     centre_ref,
     up_ref,
     down_ref,
-    table_ref,
+    narrow_ref,
+    wide_ref,
     grad_ref,
     sums_ref,
     flat_ref,
@@ -192,9 +184,16 @@
     fold = LANES // BAND
     per = BAND // fold
 
-    def table(name):
-        top, left, shape = place[name]
-        return table_ref[top : top + shape[0], left : left + shape[1]]
+    def table(name, first=0, count=None):
+        index, top, shape = place[name]
+        top, count = top + first, shape[0] - first if count is None else count
+        return (narrow_ref, wide_ref)[index][top : top + count, : shape[1]]
+
+    def beside(*blocks):
+        return jnp.concatenate(blocks, axis=1)
+
+    def below(*blocks):
+        return jnp.concatenate(blocks, axis=0)
 
     def padded(index):
         first, second = up_ref[index], down_ref[index]
@@ -240,62 +239,90 @@
     pairs = [(c, k) for c in range(CONDITIONS) for k in range(KERNELS)]
     spectra = [spread(c, k) for c, k in pairs]
 
-    half = dot(mask, table("analyse_cols"))
-    both = dot(table("analyse_rows"), half)
-    wide_lane = lax.broadcasted_iota(jnp.int32, (BAND, LANES), 1)
+    h, l = split(mask, 2)
+    both = dot(h, table("analyse_cols"))
+    half = both[:, :LANES] + both[:, LANES:] + dot(l, table("analyse_cols")[:, :LANES])
+    h, m, l = split(half, 3)
+    both = dot(table("analyse_rows", 0, 2 * grid), beside(h, m))
+    rest = dot(table("analyse_rows", 2 * grid), h) + dot(table("analyse_rows", 0, grid), l)
+    both = both[:grid, :LANES] + (both[:grid, LANES:] + both[grid:, :LANES]) + (both[grid:, LANES:] + rest)
+    low = lax.broadcasted_iota(jnp.int32, (1, LANES), 1) < LANES // 2
     turned = pltpu.roll(both[BAND:], LANES // 2, 1)
-    spectrum = both[:BAND] + jnp.where(wide_lane < LANES // 2, turned, -turned)
-
-    products = jnp.concatenate([s * spectrum for s in spectra], axis=0)
-    halves = dot(products, table("field_cols"))
+    spectrum = both[:BAND] + jnp.where(low, turned, -turned)
+
+    products = below(*[s * spectrum for s in spectra])
+    h, m, l = split(products, 3)
+    size = 2 * LANES
+    halves = (
+        dot(beside(h, m), table("field_cols", 0, size))
+        + dot(beside(h, m), table("field_cols", size, size))
+        + dot(beside(l, h), table("field_cols", 2 * size, size))
+    )
+    halves = split(halves, 3)
     fields = []
-    squares = [0.0] * CONDITIONS
-    for index, (condition, _) in enumerate(pairs):
-        rows = halves[index * BAND : (index + 1) * BAND]
-        stacked = jnp.concatenate([rows[:, :LANES], rows[:, LANES:]], axis=0)
-        field = dot(table("field_rows"), stacked)
+    square = 0.0
+    for kernel in range(KERNELS):
+        parts = []
+        for part in halves:
+            stacked = []
+            for condition in range(CONDITIONS):
+                first = (condition * KERNELS + kernel) * BAND
+                rows = part[first : first + BAND]
+                stacked.append(below(rows[:, :LANES], rows[:, LANES:]))
+            parts.append(beside(*stacked))
+        h, m, l = parts
+        field = dot(table("field_rows"), below(h, m, l, h, m, h))
         fields.append(field)
-        squares[condition] = squares[condition] + field * field
-
-    tall = dot(table("up_rows"), jnp.concatenate(squares, axis=1))
-    tall = jnp.concatenate(
-        [tall[:, c * LANES : (c + 1) * LANES] for c in range(CONDITIONS)], axis=0
-    )
-    intensities = dot(tall, table("up_cols"))
+        square = square + field * field
+
+    square = below(*[square[:, c * LANES : (c + 1) * LANES] for c in range(CONDITIONS)])
+    square = square + pltpu.roll(square, LANES // 2, 1)
+    h, m, l = [part.astype(jnp.float32) for part in split(square, 3)]
+    mixed = [jnp.where(low, h, m), jnp.where(low, l, h), jnp.where(low, m, h)]
+    tall = dot(beside(*[part.astype(jnp.bfloat16) for part in mixed]), table("up_cols"))
+    tall = split(tall, 3)
 
     slopes = []
     loss = 0.0
     for condition, dose in enumerate(DOSES):
-        intensity = intensities[condition * pad_width : (condition + 1) * pad_width]
+        h, m, l = [part[condition * grid : (condition + 1) * grid] for part in tall]
+        intensity = dot(table("up_rows"), below(h, m, l, h, m, h))
         resist = jax.nn.sigmoid(SHARPNESS * (dose * intensity - THRESHOLD))
         error = resist - target
         scaled = weight * error
         loss = loss + (scaled * error)[core, core]
         slopes.append((2.0 * SHARPNESS * dose) * scaled * (resist * (1.0 - resist)))
-    narrow = dot(jnp.concatenate(slopes, axis=0), table("down_cols"))
-    narrow = jnp.concatenate(
-        [narrow[c * pad_width : (c + 1) * pad_width] for c in range(CONDITIONS)], axis=1
-    )
-    coarse = dot(table("down_rows"), narrow)
-
-    weighted = jnp.concatenate(
-        [
-            field * coarse[:, condition * LANES : (condition + 1) * LANES]
-            for field, (condition, _) in zip(fields, pairs, strict=True)
-        ],
-        axis=0,
-    )
-    backs = dot(weighted, table("back_cols"))
+    h, l = split(below(*slopes), 2)
+    both = dot(h, table("down_cols"))
+    narrow = both[:, :LANES] + (both[:, LANES:] + dot(l, table("down_cols")[:, :LANES]))
+    narrow = beside(*[narrow[c * pad_width : (c + 1) * pad_width] for c in range(CONDITIONS)])
+    h, l = split(narrow, 2)
+    both = dot(table("down_rows"), h)
+    coarse = both[:grid] + (both[grid:] + dot(table("down_rows", 0, grid), l))
+
+    backs = [[], []]
+    for field in fields:
+        h, l = split(field * coarse, 2)
+        back = dot(table("back_rows"), below(h, l, h))
+        for condition in range(CONDITIONS):
+            block = back[:, condition * LANES : (condition + 1) * LANES]
+            turned = pltpu.roll(block[BAND:], LANES // 2, 1)
+            backs[condition].append(block[:BAND] + jnp.where(low, -turned, turned))
+    h, l = split(below(*backs[0], *backs[1]), 2)
+    backs = dot(beside(h, l), table("back_cols", 0, 2 * LANES)) + dot(
+        h, table("back_cols", 2 * LANES)
+    )
     total = 0.0
-    for index in range(len(pairs)):
-        rows = backs[index * grid : (index + 1) * grid]
-        stacked = jnp.concatenate([rows[:, :LANES], rows[:, LANES:]], axis=0)
-        total = total + spectra[index] * dot(table("back_rows"), stacked)
-
-    across = dot(total, table("core_cols"))
+    for index, spectrum in enumerate(spectra):
+        total = total + spectrum * backs[index * BAND : (index + 1) * BAND]
+
+    h, l = split(total, 2)
+    across = dot(beside(h, l), table("core_cols", 0, 2 * LANES)) + dot(
+        h, table("core_cols", 2 * LANES)
+    )
     core_width = across.shape[1] // 2
-    stacked = jnp.concatenate([across[:, :core_width], across[:, core_width:]], axis=0)
-    gradient = dot(table("core_rows"), stacked)
+    h, l = split(below(across[:, :core_width], across[:, core_width:]), 2)
+    gradient = dot(table("core_rows"), below(h, l, h))
     own = mask[core, core]
     cells = gradient * own * (1.0 - own)
     grad_ref[...] = cells
@@ -303,17 +330,6 @@
     loss = jnp.sum(jnp.sum(loss, axis=0, keepdims=True), axis=1, keepdims=True)
     sums = jnp.concatenate([square, loss], axis=0)
     sums_ref[...] = jnp.broadcast_to(sums[None], sums_ref.shape)
-
-
-def rounds():
-    row = [("row", 1 << b) for b in range(lax.axis_size("row").bit_length() - 1)]
-    col = [("col", 1 << b) for b in range(lax.axis_size("col").bit_length() - 1)]
-    return col[:1] + row[1:2] + col[1:] + row[2:] + row[:1]
-
-
-def swap(value, axis, bit):
-    count = lax.axis_size(axis)
-    return lax.ppermute(value, axis, [(i, i ^ bit) for i in range(count)])
 
 
 def small(megabytes):
@@ -384,11 +400,11 @@
             struct(core_width, core_width),
             struct(rows * cols, 2, LANES),
         ),
-        in_specs=[VMEM] * 5,
+        in_specs=[VMEM] * 6,
         out_specs=(VMEM,) * 2,
         scratch_shapes=[pltpu.VMEM((CONDITIONS, len(order), LANES), f32)],
         compiler_params=pltpu.CompilerParams(vmem_limit_bytes=16 * 1024 * 1024),
-    )(bank, centre, up, down, consts)
+    )(bank, centre, up, down, *consts)
 
     sums = to_all(sums)
     cell_count = rows * cols * core_width * core_width

time: 43.2 us -> 40.2 us (0.931)
  Pallas kernels: 8.73 us -> 4.35 us
  local copies, waits for them, and re-layouts: 0.72 us -> 2.1 us
    pallas_call x1, Pallas kernels: 7.74 us -> 3.36 us  [shards(): pl.pallas_call(functools.partial(step_kernel, order, place), out_shape=(s...]
    unnamed x2 -> x4, local copies, waits for them, and re-layouts: 0.01 us -> 1.39 us
where the time goes in v3:
time: 40.2 us; the launch traced here: 40 us
  blocking collectives  23.1 us (57%)
  starting transfers between devices  6.61 us (16%)
  Pallas kernels  4.35 us (11%)
  waiting for transfers between devices  2.14 us (5%)
  local copies, waits for them, and re-layouts  2.1 us (5%)
  other arithmetic  0.96 us (2%)
  between operations  0.69 us (2%)
    all_to_all x2, blocking collectives, to_all(): return lax.all_to_all(value, ('row', 'col'), 0, 0)  23.1 us
    ppermute x4, starting transfers between devices, pair_swap(): return lax.ppermute(value, axis, pairs)  6.61 us
    pallas_call x1, Pallas kernels, shards(): pl.pallas_call(functools.partial(step_kernel, order, place), out_shape=(s...  3.36 us
    ppermute x4, waiting for transfers between devices, pair_swap(): return lax.ppermute(value, axis, pairs)  2.14 us
    unnamed x4, local copies, waits for them, and re-layouts  1.39 us
    another operation x1, other arithmetic, shards(): own = jnp.stack([mask_logits, target, weight])  0.96 us
  transfers between devices with their start and end apart: 4, of which 1 were waited for; matrix products, arithmetic and copies ran while one was open for 0% of the time, Pallas kernels for 0%

profile of v3, /device:TPU:0, one launch (start us, length us, event | category | flops | bytes accessed | tf_op | source)
XLA Modules:
  0.0 40.0 jit_solution(5424827835102232599)
XLA Ops:
  0.6 0.0 copy-start.1
  0.6 1.0 %pad_maximum_fusion.own_ref = f32[3,128,128]{2,1,0:T(8,128)S(1)} fusion(f32[1,128,128]{2,1,0:T(8,128)} %bitcast.4, f32[1,128,128]{2,1,0:T(8,128)} %bitcast.5, f32[1,128,128]{2,1,0:T(8,128)} %bitcast.6), kind=kLoop, calls=%fused_computation | loop fusion | flops 98304 | bytes 393216 | tf_op jit(solution)/shard_map/stack | solution.py:370
  1.6 0.1 shard_map.77
  1.7 3.1 %collective-permute-start = (f32[192,128]{1,0:T(8,128)S(1)}, f32[192,128]{1,0:T(8,128)S(1)}, u32[]{:S(2)}, u32[]{:S(2)}) collective-permute-start(f32[192,128]{1,0:T(8,128)S(1)} %get-tuple-element.12), channel_id=1, source_target_pairs={{0,1},{1,0},{2,3},{3,2},{4,5},{5,4},{6,7},{7,6},{8,9},{9,8},{10,11... | collective-permute-start | bytes 294920 | tf_op jit(solution)/shard_map/ppermute | solution.py:350
  4.8 0.7 %collective-permute-start.1 = (f32[192,128]{1,0:T(8,128)S(1)}, f32[192,128]{1,0:T(8,128)S(1)}, u32[]{:S(2)}, u32[]{:S(2)}) collective-permute-start(f32[192,128]{1,0:T(8,128)S(1)} %get-tuple-element.13), channel_id=1, source_target_pairs={{1,2},{2,1},{5,6},{6,5},{9,10},{10,9},{13,14},{14,13},{17,18},{18,... | collective-permute-start | bytes 294920 | tf_op jit(solution)/shard_map/ppermute | solution.py:350
  5.5 2.1 %collective-permute-done.a_ref = f32[192,128]{1,0:T(8,128)S(1)} collective-permute-done((f32[192,128]{1,0:T(8,128)S(1)}, f32[192,128]{1,0:T(8,128)S(1)}, u32[]{:S(2)}, u32[]{:S(2)}) %collective-permute-start) | collective-permute-done | bytes 98336 | tf_op jit(solution)/shard_map/ppermute | solution.py:350
  7.6 0.0 collective-permute-done.1.b_ref
  7.6 0.7 %broadcast_in_dim.2.shards_ref = f32[32,2,384]{2,1,0:T(2,128)S(1)} broadcast(f32[2,384]{1,0:T(2,128)} %param.9), dimensions={1,2} | broadcast | bytes 101376 | tf_op jit(solution)/shard_map/broadcast_in_dim | solution.py:378
  8.3 0.2 shard_map.78
  8.5 0.1 collective-permute-start.2
  8.6 2.8 %collective-permute-start.3 = (f32[3,64,256]{2,1,0:T(8,128)S(1)}, f32[3,64,256]{2,1,0:T(8,128)S(1)}, u32[]{:S(2)}, u32[]{:S(2)}) collective-permute-start(f32[3,64,256]{2,1,0:T(8,128)S(1)} %get-tuple-element.17), channel_id=1, source_target_pairs={{4,8},{8,4},{12,16},{16,12},{20,24},{24,20},{0,28},{28,0},{5,9},{9... | collective-permute-start | bytes 589832 | tf_op jit(solution)/shard_map/ppermute | solution.py:350
  11.4 14.1 %all_to_all.10.bank_ref = f32[32,2,384]{2,1,0:T(2,128)S(1)} all-to-all(f32[32,2,384]{2,1,0:T(2,128)S(1)} %get-tuple-element.14), channel_id=1, replica_groups=mesh['row'=8,'col'=4] {'row','col'}, dimensions={0} | all-to-all | bytes 196608 | tf_op jit(solution)/shard_map/all_to_all | solution.py:340
  25.5 0.0 collective-permute-done.2.up_ref
  25.5 0.0 collective-permute-done.3.down_ref
  25.5 0.0 copy-done.1
  25.6 0.0 copy-start
  25.6 1.4 %copy-done = bf16[2944,256]{1,0:T(8,128)(2,1)S(1)} copy-done((bf16[2944,256]{1,0:T(8,128)(2,1)S(1)}, bf16[2944,256]{1,0:T(8,128)(2,1)}, u32[]{:S(2)}) %copy-start) | copy-done | bytes 1507352
  26.9 3.4 %shard_map.79 = (f32[128,128]{1,0:T(8,128)S(1)}, f32[32,2,128]{2,1,0:T(2,128)S(1)}) custom-call(f32[32,2,384]{2,1,0:T(2,128)S(1)} %all_to_all.10.bank_ref, f32[3,128,256]{2,1,0:T(8,128)S(1)} %get-tuple-element.15.centre_ref, f32[3,64,256]{2,1,0:T(8,128)S(1)} %collective-permute-done.2.up_ref, f32[3,64,256]{2,1,0:T(8,128)S(1)} %collective-permute-done.3.down_ref, ...), custom_call_target="tpu_custom_call" | custom-call | tf_op jit(solution)/shard_map/pallas_call | solution.py:397
  30.3 9.0 %all_to_all.11.sums_ref = f32[32,2,128]{2,1,0:T(2,128)S(1)} all-to-all(f32[32,2,128]{2,1,0:T(2,128)S(1)} %get-tuple-element.19), channel_id=1, replica_groups=mesh['row'=8,'col'=4] {'row','col'}, dimensions={0} | all-to-all | bytes 65536 | tf_op jit(solution)/shard_map/all_to_all | solution.py:340
  39.3 0.7 %shard_map.80 = (f32[128,128]{1,0:T(8,128)}, f32[1,1]{1,0:T(1,128)}) custom-call(f32[3,128,128]{2,1,0:T(8,128)S(1)} %pad_maximum_fusion.own_ref, f32[128,128]{1,0:T(8,128)S(1)} %get-tuple-element.18.cells_ref, f32[32,2,128]{2,1,0:T(2,128)S(1)} %all_to_all.11.sums_ref), custom_call_target="tpu_custom_call" | custom-call | tf_op jit(solution)/shard_map/pallas_call | solution.py:411
Async XLA Ops:
  0.6 24.9 %copy-start.1 = (bf16[320,384]{1,0:T(8,128)(2,1)S(1)}, bf16[320,384]{1,0:T(8,128)(2,1)}, u32[]{:S(2)}) copy-start(bf16[320,384]{1,0:T(8,128)(2,1)} %constant.5.clone.wide_ref) | copy-start | bytes 737284
  1.7 5.9 %collective-permute-start = (f32[192,128]{1,0:T(8,128)S(1)}, f32[192,128]{1,0:T(8,128)S(1)}, u32[]{:S(2)}, u32[]{:S(2)}) collective-permute-start(f32[192,128]{1,0:T(8,128)S(1)} %get-tuple-element.12), channel_id=1, source_target_pairs={{0,1},{1,0},{2,3},{3,2},{4,5},{5,4},{6,7},{7,6},{8,9},{9,8},{10,11... | collective-permute-start | bytes 294920 | tf_op jit(solution)/shard_map/ppermute | solution.py:350
  4.8 2.8 %collective-permute-start.1 = (f32[192,128]{1,0:T(8,128)S(1)}, f32[192,128]{1,0:T(8,128)S(1)}, u32[]{:S(2)}, u32[]{:S(2)}) collective-permute-start(f32[192,128]{1,0:T(8,128)S(1)} %get-tuple-element.13), channel_id=1, source_target_pairs={{1,2},{2,1},{5,6},{6,5},{9,10},{10,9},{13,14},{14,13},{17,18},{18,... | collective-permute-start | bytes 294920 | tf_op jit(solution)/shard_map/ppermute | solution.py:350
  8.5 17.0 %collective-permute-start.2 = (f32[3,64,256]{2,1,0:T(8,128)S(1)}, f32[3,64,256]{2,1,0:T(8,128)S(1)}, u32[]{:S(2)}, u32[]{:S(2)}) collective-permute-start(f32[3,64,256]{2,1,0:T(8,128)S(1)} %get-tuple-element.16), channel_id=1, source_target_pairs={{0,4},{4,0},{8,12},{12,8},{16,20},{20,16},{24,28},{28,24},{1,5},{5... | collective-permute-start | bytes 589832 | tf_op jit(solution)/shard_map/ppermute | solution.py:350
  8.6 16.9 %collective-permute-start.3 = (f32[3,64,256]{2,1,0:T(8,128)S(1)}, f32[3,64,256]{2,1,0:T(8,128)S(1)}, u32[]{:S(2)}, u32[]{:S(2)}) collective-permute-start(f32[3,64,256]{2,1,0:T(8,128)S(1)} %get-tuple-element.17), channel_id=1, source_target_pairs={{4,8},{8,4},{12,16},{16,12},{20,24},{24,20},{0,28},{28,0},{5,9},{9... | collective-permute-start | bytes 589832 | tf_op jit(solution)/shard_map/ppermute | solution.py:350
  25.6 1.4 %copy-start = (bf16[2944,256]{1,0:T(8,128)(2,1)S(1)}, bf16[2944,256]{1,0:T(8,128)(2,1)}, u32[]{:S(2)}) copy-start(bf16[2944,256]{1,0:T(8,128)(2,1)} %constant.4.clone.narrow_ref) | copy-start | bytes 4521988

commit v4 on v3

--- a/solution.py
+++ b/solution.py
@@ -82,12 +82,12 @@
     from_re = beside(coarse_re, -coarse_im, -coarse_im, -coarse_re)
     from_im = beside(coarse_im, coarse_re, coarse_re, -coarse_im)
     h, m, l = split_table(below(from_re, from_im, from_re, from_im), 3)
-    found["field_cols"] = below(h, h, m, m, h, l)
+    found["field_cols"] = below(h, m, l)
     h, m, l = split_table(beside(crow_re.T, crow_im.T), 3)
     found["field_rows"] = beside(h, h, h, m, m, l)
     h, m, l = split_table(between, 3)
     found["up_rows"] = beside(h, h, h, m, m, l)
-    found["up_cols"] = below(h.T, h.T, h.T, m.T, m.T, l.T)
+    found["up_cols"] = below(h.T, m.T, l.T)
     found["down_cols"] = beside(h, h, m, m)
     found["down_rows"] = below(h.T, m.T)
     h, l = split_table(below(crow_re, crow_im), 2)
@@ -96,26 +96,38 @@
     h, l = split_table(
         below(beside(c_re, c_im, c_im, -c_re), beside(-c_im, c_re, c_re, c_im)), 2
     )
-    found["back_cols"] = below(h, h, l)
+    found["back_cols"] = below(h, l)
     from_re, from_im = beside(core_re, -core_im), beside(core_im, core_re)
     h, l = split_table(below(from_re, from_im, from_re, from_im), 2)
-    found["core_cols"] = below(h, h, l)
+    found["core_cols"] = below(h, l)
     h, l = split_table(2.0 * beside(row_re[:, core].T, row_im[:, core].T), 2)
     found["core_rows"] = beside(h, h, l)
 
-    arrays, where = [], {}
-    for index, width in enumerate((2 * LANES, 3 * LANES)):
-        start, stack = 0, []
-        for name, table in found.items():
-            if (table.shape[1] > 2 * LANES) == (index == 1):
-                where[name] = (index, start, table.shape)
-                stack.append(np.pad(table, ((0, 0), (0, width - table.shape[1]))))
-                start += table.shape[0]
-        arrays.append(jnp.asarray(np.concatenate(stack, axis=0)))
-    return arrays, where
-
-
-def pack_columns(own_ref, a_ref, b_ref):
+    pieces = []
+    for name, table in found.items():
+        for first in range(0, table.shape[1], 2 * LANES):
+            pieces.append(((name, first // (2 * LANES)), table[:, first : first + 2 * LANES]))
+    where, tops, blocks = {}, [0, 0], []
+    for key, piece in sorted(pieces, key=lambda p: (p[1].shape[1] <= LANES, -p[1].shape[0])):
+        thin = piece.shape[1] <= LANES
+        side = int(thin and tops[1] < tops[0])
+        where[key] = (tops[side], side * LANES, piece.shape)
+        blocks.append((where[key], piece))
+        tops[side] += piece.shape[0]
+        if not thin:
+            tops[1] = tops[0]
+    whole = np.zeros((max(tops), 2 * LANES), jnp.bfloat16)
+    for (top, left, shape), piece in blocks:
+        whole[top : top + shape[0], left : left + shape[1]] = piece
+    return jnp.asarray(whole), where
+
+
+def pack(own_ref, a_ref, b_ref, up_ref, down_ref):
+    odd_row = lax.rem(lax.axis_index("row"), 2) == 1
+    for index in range(3):
+        first, second = own_ref[index, :HALO], own_ref[index, HALO:]
+        up_ref[index] = jnp.where(odd_row, first, second)
+        down_ref[index] = jnp.where(odd_row, second, first)
     half = HALO
     odd = lax.rem(lax.axis_index("col"), 2) == 1
     values = [own_ref[index] for index in range(3)]
@@ -136,8 +148,11 @@
     b_ref[rows:] = jnp.where(odd, to_right[1], to_left[1])
 
 
-def widen(own_ref, a_ref, b_ref, shards_ref, centre_ref, up_ref, down_ref, bank_ref):
-    bank_ref[...] = shards_ref[...]
+def spread(shard_ref, out_ref):
+    out_ref[...] = jnp.broadcast_to(shard_ref[...][None], out_ref.shape)
+
+
+def widen(own_ref, a_ref, b_ref, _, __, centre_ref, up_ref, down_ref):
     half = HALO
     odd = lax.rem(lax.axis_index("col"), 2) == 1
     odd_row = lax.rem(lax.axis_index("row"), 2) == 1
@@ -145,8 +160,9 @@
     rows = values[0].shape[0]
     low = lax.broadcasted_iota(jnp.int32, values[0].shape, 1) < half
     got_a, got_b = a_ref[...], b_ref[...]
-    left = jnp.where(odd, got_a, got_b)
-    right = jnp.where(odd, got_b, got_a)
+    col, cols = lax.axis_index("col"), lax.axis_size("col")
+    left = jnp.where(col == 0, 0.0, jnp.where(odd, got_a, got_b))
+    right = jnp.where(col == cols - 1, 0.0, jnp.where(odd, got_b, got_a))
     left_turned, right_turned = pltpu.roll(left, half, 1), pltpu.roll(right, half, 1)
 
     def two(first, second):
@@ -160,8 +176,9 @@
             [jnp.where(low, lefts[index], turned), jnp.where(low, turned, rights[index])], axis=1
         )
         centre_ref[index] = wide
-        up_ref[index] = jnp.where(odd_row, wide[:half], wide[half:])
-        down_ref[index] = jnp.where(odd_row, wide[half:], wide[:half])
+        margin = jnp.where(low, wide[:, :LANES], wide[:, LANES:])
+        up_ref[index] = jnp.where(odd_row, margin[:half], margin[half:])
+        down_ref[index] = jnp.where(odd_row, margin[half:], margin[:half])
 
 
 def step_kernel(
@@ -171,8 +188,9 @@
     centre_ref,
     up_ref,
     down_ref,
-    narrow_ref,
-    wide_ref,
+    up_margin_ref,
+    down_margin_ref,
+    table_ref,
     grad_ref,
     sums_ref,
     flat_ref,
@@ -184,10 +202,17 @@
     fold = LANES // BAND
     per = BAND // fold
 
-    def table(name, first=0, count=None):
-        index, top, shape = place[name]
+    def table(name, first=0, count=None, part=0):
+        top, left, shape = place[name, part]
         top, count = top + first, shape[0] - first if count is None else count
-        return (narrow_ref, wide_ref)[index][top : top + count, : shape[1]]
+        return table_ref[top : top + count, left : left + shape[1]]
+
+    def three(name, h, l):
+        th, tl = table(name, 0, LANES), table(name, LANES)
+        return dot(beside(h, l), below(th, th)) + dot(h, tl)
+
+    def six(name, h, m, l):
+        return dot(table(name), below(h, m, l, h)) + dot(table(name, part=1), below(m, h))
 
     def beside(*blocks):
         return jnp.concatenate(blocks, axis=1)
@@ -195,11 +220,19 @@
     def below(*blocks):
         return jnp.concatenate(blocks, axis=0)
 
+    low = lax.broadcasted_iota(jnp.int32, (1, LANES), 1) < LANES // 2
+
     def padded(index):
-        first, second = up_ref[index], down_ref[index]
-        above = jnp.where(odd_row, first, second)
-        below = jnp.where(odd_row, second, first)
-        return jnp.concatenate([above, centre_ref[index], below], axis=0)
+        wide = []
+        for own_ref, margin_ref in ((up_ref, up_margin_ref), (down_ref, down_margin_ref)):
+            turned, margin = pltpu.roll(own_ref[index], HALO, 1), margin_ref[index]
+            wide.append(beside(jnp.where(low, margin, turned), jnp.where(low, turned, margin)))
+        first, second = wide
+        return below(
+            jnp.where(odd_row, first, second),
+            centre_ref[index],
+            jnp.where(odd_row, second, first),
+        )
 
     cell_row = lax.broadcasted_iota(jnp.int32, (centre_ref.shape[1] + 2 * HALO, 1), 0)
     first_row = jnp.where(at_top, HALO, 0)
@@ -246,17 +279,16 @@
     both = dot(table("analyse_rows", 0, 2 * grid), beside(h, m))
     rest = dot(table("analyse_rows", 2 * grid), h) + dot(table("analyse_rows", 0, grid), l)
     both = both[:grid, :LANES] + (both[:grid, LANES:] + both[grid:, :LANES]) + (both[grid:, LANES:] + rest)
-    low = lax.broadcasted_iota(jnp.int32, (1, LANES), 1) < LANES // 2
     turned = pltpu.roll(both[BAND:], LANES // 2, 1)
     spectrum = both[:BAND] + jnp.where(low, turned, -turned)
 
     products = below(*[s * spectrum for s in spectra])
     h, m, l = split(products, 3)
-    size = 2 * LANES
+    th, tm, tl = [table("field_cols", LANES * index, LANES) for index in range(3)]
     halves = (
-        dot(beside(h, m), table("field_cols", 0, size))
-        + dot(beside(h, m), table("field_cols", size, size))
-        + dot(beside(l, h), table("field_cols", 2 * size, size))
+        dot(beside(h, m), below(th, th))
+        + dot(beside(h, m), below(tm, tm))
+        + dot(beside(l, h), below(th, tl))
     )
     halves = split(halves, 3)
     fields = []
@@ -270,8 +302,7 @@
                 rows = part[first : first + BAND]
                 stacked.append(below(rows[:, :LANES], rows[:, LANES:]))
             parts.append(beside(*stacked))
-        h, m, l = parts
-        field = dot(table("field_rows"), below(h, m, l, h, m, h))
+        field = six("field_rows", *parts)
         fields.append(field)
         square = square + field * field
 
@@ -279,14 +310,16 @@
     square = square + pltpu.roll(square, LANES // 2, 1)
     h, m, l = [part.astype(jnp.float32) for part in split(square, 3)]
     mixed = [jnp.where(low, h, m), jnp.where(low, l, h), jnp.where(low, m, h)]
-    tall = dot(beside(*[part.astype(jnp.bfloat16) for part in mixed]), table("up_cols"))
+    th, tm, tl = [table("up_cols", grid * index, grid) for index in range(3)]
+    mixed = beside(*[part.astype(jnp.bfloat16) for part in mixed])
+    tall = dot(mixed, below(th, th, th, tm, tm, tl))
     tall = split(tall, 3)
 
     slopes = []
     loss = 0.0
     for condition, dose in enumerate(DOSES):
-        h, m, l = [part[condition * grid : (condition + 1) * grid] for part in tall]
-        intensity = dot(table("up_rows"), below(h, m, l, h, m, h))
+        parts = [part[condition * grid : (condition + 1) * grid] for part in tall]
+        intensity = six("up_rows", *parts)
         resist = jax.nn.sigmoid(SHARPNESS * (dose * intensity - THRESHOLD))
         error = resist - target
         scaled = weight * error
@@ -309,17 +342,13 @@
             turned = pltpu.roll(block[BAND:], LANES // 2, 1)
             backs[condition].append(block[:BAND] + jnp.where(low, -turned, turned))
     h, l = split(below(*backs[0], *backs[1]), 2)
-    backs = dot(beside(h, l), table("back_cols", 0, 2 * LANES)) + dot(
-        h, table("back_cols", 2 * LANES)
-    )
+    backs = three("back_cols", h, l)
     total = 0.0
     for index, spectrum in enumerate(spectra):
         total = total + spectrum * backs[index * BAND : (index + 1) * BAND]
 
     h, l = split(total, 2)
-    across = dot(beside(h, l), table("core_cols", 0, 2 * LANES)) + dot(
-        h, table("core_cols", 2 * LANES)
-    )
+    across = three("core_cols", h, l)
     core_width = across.shape[1] // 2
     h, l = split(below(across[:, :core_width], across[:, core_width:]), 2)
     gradient = dot(table("core_rows"), below(h, l, h))
@@ -368,24 +397,34 @@
 
     packed = struct(core_width * 3 // 2, core_width)
     own = jnp.stack([mask_logits, target, weight])
-    slab_a, slab_b = pl.pallas_call(
-        pack_columns,
-        out_shape=(packed, packed),
+    slab = struct(3, HALO, core_width)
+    slab_a, slab_b, up, down = pl.pallas_call(
+        pack,
+        out_shape=(packed, packed, slab, slab),
         in_specs=[VMEM],
-        out_specs=(VMEM,) * 2,
+        out_specs=(VMEM,) * 4,
         compiler_params=small(4),
     )(own)
-    bank = jnp.broadcast_to(kernels[None], (rows * cols,) + kernels.shape)
-    got_a, got_b = pair_swap(slab_a, "col", 0), pair_swap(slab_b, "col", 1)
-    slab = struct(3, HALO, pad_width)
-    centre, up, down, bank = pl.pallas_call(
+    bank = pl.pallas_call(
+        spread,
+        out_shape=struct(rows * cols, *kernels.shape),
+        in_specs=[VMEM],
+        out_specs=VMEM,
+        compiler_params=small(4),
+    )(kernels)
+    got_a, got_b = pair_swap(slab_a, "col", 0), pair_swap(slab_b, "col", 1, wrap=True)
+    up, down = pair_swap(up, "row", 0), pair_swap(down, "row", 1, wrap=True)
+    centre, up_margin, down_margin = pl.pallas_call(
         widen,
-        out_shape=(struct(3, core_width, pad_width), slab, slab, struct(*bank.shape)),
-        in_specs=[VMEM] * 4,
-        out_specs=(VMEM,) * 4,
+        out_shape=(struct(3, core_width, pad_width), slab, slab),
+        in_specs=[VMEM] * 3 + [pl.BlockSpec(memory_space=pl.ANY)] * 2,
+        out_specs=(VMEM,) * 3,
         compiler_params=small(8),
-    )(own, got_a, got_b, bank)
-    up, down = pair_swap(up, "row", 0), pair_swap(down, "row", 1, wrap=True)
+    )(own, got_a, got_b, up, down)
+    up_margin, down_margin = (
+        pair_swap(up_margin, "row", 0),
+        pair_swap(down_margin, "row", 1, wrap=True),
+    )
     bank = to_all(bank)
     pieces = kernels.shape[1] // LANES
     if kernels.shape[1] % LANES:
@@ -400,11 +439,11 @@
             struct(core_width, core_width),
             struct(rows * cols, 2, LANES),
         ),
-        in_specs=[VMEM] * 6,
+        in_specs=[VMEM] * 7,
         out_specs=(VMEM,) * 2,
         scratch_shapes=[pltpu.VMEM((CONDITIONS, len(order), LANES), f32)],
         compiler_params=pltpu.CompilerParams(vmem_limit_bytes=16 * 1024 * 1024),
-    )(bank, centre, up, down, *consts)
+    )(bank, centre, up, down, up_margin, down_margin, consts)
 
     sums = to_all(sums)
     cell_count = rows * cols * core_width * core_width

time: 40.2 us -> 36.4 us (0.905)
  blocking collectives: 23.1 us -> 10.3 us
  starting transfers between devices: 6.61 us -> 13.3 us
  waiting for transfers between devices: 2.14 us -> 5.08 us
  local copies, waits for them, and re-layouts: 2.1 us -> 0.69 us
  Pallas kernels: 4.35 us -> 4.98 us
    all_to_all x2 -> x1, blocking collectives: 23.1 us -> 10.3 us  [to_all(): return lax.all_to_all(value, ('row', 'col'), 0, 0)]
    all_to_all x0 -> x1, waiting for transfers between devices: none -> 4.96 us  [to_all(): return lax.all_to_all(value, ('row', 'col'), 0, 0)]
    ppermute x4 -> x6, starting transfers between devices: 6.61 us -> 10.8 us  [pair_swap(): return lax.ppermute(value, axis, pairs)]
    all_to_all x0 -> x1, starting transfers between devices: none -> 2.56 us  [to_all(): return lax.all_to_all(value, ('row', 'col'), 0, 0)]
    ppermute x4 -> x6, waiting for transfers between devices: 2.14 us -> 0.12 us  [pair_swap(): return lax.ppermute(value, axis, pairs)]
    broadcast_in_dim x1 -> x0, local copies, waits for them, and re-layouts: 0.71 us -> none  [shards(): bank = jnp.broadcast_to(kernels[None], (rows * cols,) + kernels.shape)]
    unnamed x4, local copies, waits for them, and re-layouts: 1.39 us -> 0.69 us
    pallas_call x1 -> x2, Pallas kernels: 0.12 us -> 0.75 us  [the longest x1 0.63 us: shards(): pl.pallas_call(spread, out_shape=struct(rows * cols, *kernels.shape), in_...]
  transfers between devices with their start and end apart: 4 -> 7, of which waited for: 1 -> 2; matrix products, arithmetic and copies ran while one was open for 0% -> 0% of each run, Pallas kernels for 0% -> 2%
where the time goes in v4:
time: 36.4 us; the launch traced here: 36.1 us
  starting transfers between devices  13.3 us (37%)
  blocking collectives  10.3 us (28%)
  waiting for transfers between devices  5.08 us (14%)
  Pallas kernels  4.98 us (14%)
  other arithmetic  1.02 us (3%)
  between operations  0.7 us (2%)
  local copies, waits for them, and re-layouts  0.69 us (2%)
    ppermute x6, starting transfers between devices, pair_swap(): return lax.ppermute(value, axis, pairs)  10.8 us
    all_to_all x1, blocking collectives, to_all(): return lax.all_to_all(value, ('row', 'col'), 0, 0)  10.3 us
    all_to_all x1, waiting for transfers between devices, to_all(): return lax.all_to_all(value, ('row', 'col'), 0, 0)  4.96 us
    pallas_call x1, Pallas kernels, shards(): pl.pallas_call(functools.partial(step_kernel, order, place), out_shape=(s...  3.37 us
    all_to_all x1, starting transfers between devices, to_all(): return lax.all_to_all(value, ('row', 'col'), 0, 0)  2.56 us
    another operation x1, other arithmetic, shards(): own = jnp.stack([mask_logits, target, weight])  1.02 us
  transfers between devices with their start and end apart: 7, of which 2 were waited for; matrix products, arithmetic and copies ran while one was open for 0% of the time, Pallas kernels for 2%

profile of v4, /device:TPU:0, one launch (start us, length us, event | category | flops | bytes accessed | tf_op | source)
XLA Modules:
  0.0 36.1 jit_solution(6097840494637749845)
XLA Ops:
  0.6 0.0 copy-start
  0.6 1.0 %pad_maximum_fusion.own_ref = f32[3,128,128]{2,1,0:T(8,128)S(1)} fusion(f32[1,128,128]{2,1,0:T(8,128)} %bitcast.4, f32[1,128,128]{2,1,0:T(8,128)} %bitcast.5, f32[1,128,128]{2,1,0:T(8,128)} %bitcast.6), kind=kLoop, calls=%fused_computation | loop fusion | flops 98304 | bytes 393216 | tf_op jit(solution)/shard_map/stack | solution.py:399
  1.7 0.1 shard_map.69
  1.8 0.5 %collective-permute-start.2 = (f32[3,64,128]{2,1,0:T(8,128)S(1)}, f32[3,64,128]{2,1,0:T(8,128)S(1)}, u32[]{:S(2)}, u32[]{:S(2)}) collective-permute-start(f32[3,64,128]{2,1,0:T(8,128)S(1)} %get-tuple-element.15), channel_id=1, source_target_pairs={{0,4},{4,0},{8,12},{12,8},{16,20},{20,16},{24,28},{28,24},{1,5},{5... | collective-permute-start | bytes 294920 | tf_op jit(solution)/shard_map/ppermute | solution.py:379
  2.3 3.6 %collective-permute-start.3 = (f32[3,64,128]{2,1,0:T(8,128)S(1)}, f32[3,64,128]{2,1,0:T(8,128)S(1)}, u32[]{:S(2)}, u32[]{:S(2)}) collective-permute-start(f32[3,64,128]{2,1,0:T(8,128)S(1)} %get-tuple-element.16), channel_id=1, source_target_pairs={{4,8},{8,4},{12,16},{16,12},{20,24},{24,20},{0,28},{28,0},{5,9},{9... | collective-permute-start | bytes 294920 | tf_op jit(solution)/shard_map/ppermute | solution.py:379
  5.9 1.6 %collective-permute-start = (f32[192,128]{1,0:T(8,128)S(1)}, f32[192,128]{1,0:T(8,128)S(1)}, u32[]{:S(2)}, u32[]{:S(2)}) collective-permute-start(f32[192,128]{1,0:T(8,128)S(1)} %get-tuple-element.13), channel_id=1, source_target_pairs={{0,1},{1,0},{2,3},{3,2},{4,5},{5,4},{6,7},{7,6},{8,9},{9,8},{10,11... | collective-permute-start | bytes 294920 | tf_op jit(solution)/shard_map/ppermute | solution.py:379
  7.4 2.5 %collective-permute-start.1 = (f32[192,128]{1,0:T(8,128)S(1)}, f32[192,128]{1,0:T(8,128)S(1)}, u32[]{:S(2)}, u32[]{:S(2)}) collective-permute-start(f32[192,128]{1,0:T(8,128)S(1)} %get-tuple-element.14), channel_id=1, source_target_pairs={{1,2},{2,1},{0,3},{3,0},{5,6},{6,5},{4,7},{7,4},{9,10},{10,9},{8,1... | collective-permute-start | bytes 294920 | tf_op jit(solution)/shard_map/ppermute | solution.py:379
  9.9 0.0 copy-start.1
  9.9 0.7 %copy-done.1 = f32[2,384]{1,0:T(2,128)S(1)} copy-done((f32[2,384]{1,0:T(2,128)S(1)}, f32[2,384]{1,0:T(2,128)}, u32[]{:S(2)}) %copy-start.1) | copy-done | bytes 3096
  10.6 0.6 %shard_map.68 = f32[32,2,384]{2,1,0:T(2,128)} custom-call(f32[2,384]{1,0:T(2,128)S(1)} %copy-done.1), custom_call_target="tpu_custom_call" | custom-call | tf_op jit(solution)/shard_map/pallas_call | solution.py:408
  11.2 2.6 %all-to-all-start = ((f32[32,2,384]{2,1,0:T(2,128)}), f32[32,2,384]{2,1,0:T(2,128)S(1)}, u32[]{:S(2)}, u32[]{:S(2)}) async-start(f32[32,2,384]{2,1,0:T(2,128)} %shard_map.68), calls=%async_computation | async-start | bytes 196608 | tf_op jit(solution)/shard_map/all_to_all | solution.py:369
  13.8 0.0 collective-permute-done.2._.up_ref
  13.8 0.0 collective-permute-done.3.__.down_ref
  13.8 0.0 collective-permute-done.a_ref
  13.8 0.1 collective-permute-done.1.b_ref
  13.9 0.2 shard_map.70
  14.1 0.1 collective-permute-start.4
  14.2 2.6 %collective-permute-start.5 = (f32[3,64,128]{2,1,0:T(8,128)S(1)}, f32[3,64,128]{2,1,0:T(8,128)S(1)}, u32[]{:S(2)}, u32[]{:S(2)}) collective-permute-start(f32[3,64,128]{2,1,0:T(8,128)S(1)} %get-tuple-element.19), channel_id=1, source_target_pairs={{4,8},{8,4},{12,16},{16,12},{20,24},{24,20},{0,28},{28,0},{5,9},{9... | collective-permute-start | bytes 294920 | tf_op jit(solution)/shard_map/ppermute | solution.py:379
  16.8 5.0 %all-to-all-done.bank_ref = f32[32,2,384]{2,1,0:T(2,128)S(1)} async-done(((f32[32,2,384]{2,1,0:T(2,128)}), f32[32,2,384]{2,1,0:T(2,128)S(1)}, u32[]{:S(2)}, u32[]{:S(2)}) %all-to-all-start) | async-done | bytes 98336 | tf_op jit(solution)/shard_map/all_to_all | solution.py:369
  21.7 0.0 collective-permute-done.4.up_margin_ref
  21.7 0.0 collective-permute-done.5.down_margin_ref
  21.7 0.0 copy-done
  21.8 3.4 %shard_map.71 = (f32[128,128]{1,0:T(8,128)S(1)}, f32[32,2,128]{2,1,0:T(2,128)S(1)}) custom-call(f32[32,2,384]{2,1,0:T(2,128)S(1)} %all-to-all-done.bank_ref, f32[3,128,256]{2,1,0:T(8,128)S(1)} %get-tuple-element.17.centre_ref, f32[3,64,128]{2,1,0:T(8,128)S(1)} %collective-permute-done.2._.up_ref, f32[3,64,128]{2,1,0:T(8,128)S(1)} %collective-permute-done.3.__.down_ref, ...), custom_call_target="tpu_custom_call" | custom-call | tf_op jit(solution)/shard_map/pallas_call | solution.py:436
  25.1 10.3 %all_to_all.10.sums_ref = f32[32,2,128]{2,1,0:T(2,128)S(1)} all-to-all(f32[32,2,128]{2,1,0:T(2,128)S(1)} %get-tuple-element.21), channel_id=1, replica_groups=mesh['row'=8,'col'=4] {'row','col'}, dimensions={0} | all-to-all | bytes 65536 | tf_op jit(solution)/shard_map/all_to_all | solution.py:369
  35.4 0.7 %shard_map.72 = (f32[128,128]{1,0:T(8,128)}, f32[1,1]{1,0:T(1,128)}) custom-call(f32[3,128,128]{2,1,0:T(8,128)S(1)} %pad_maximum_fusion.own_ref, f32[128,128]{1,0:T(8,128)S(1)} %get-tuple-element.20.cells_ref, f32[32,2,128]{2,1,0:T(2,128)S(1)} %all_to_all.10.sums_ref), custom_call_target="tpu_custom_call" | custom-call | tf_op jit(solution)/shard_map/pallas_call | solution.py:450
Async XLA Ops:
  0.6 21.1 %copy-start = (bf16[2496,256]{1,0:T(8,128)(2,1)S(1)}, bf16[2496,256]{1,0:T(8,128)(2,1)}, u32[]{:S(2)}) copy-start(bf16[2496,256]{1,0:T(8,128)(2,1)} %constant.2.clone.table_ref) | copy-start | bytes 3833860
  1.8 12.0 %collective-permute-start.2 = (f32[3,64,128]{2,1,0:T(8,128)S(1)}, f32[3,64,128]{2,1,0:T(8,128)S(1)}, u32[]{:S(2)}, u32[]{:S(2)}) collective-permute-start(f32[3,64,128]{2,1,0:T(8,128)S(1)} %get-tuple-element.15), channel_id=1, source_target_pairs={{0,4},{4,0},{8,12},{12,8},{16,20},{20,16},{24,28},{28,24},{1,5},{5... | collective-permute-start | bytes 294920 | tf_op jit(solution)/shard_map/ppermute | solution.py:379
  2.3 11.5 %collective-permute-start.3 = (f32[3,64,128]{2,1,0:T(8,128)S(1)}, f32[3,64,128]{2,1,0:T(8,128)S(1)}, u32[]{:S(2)}, u32[]{:S(2)}) collective-permute-start(f32[3,64,128]{2,1,0:T(8,128)S(1)} %get-tuple-element.16), channel_id=1, source_target_pairs={{4,8},{8,4},{12,16},{16,12},{20,24},{24,20},{0,28},{28,0},{5,9},{9... | collective-permute-start | bytes 294920 | tf_op jit(solution)/shard_map/ppermute | solution.py:379
  5.9 8.0 %collective-permute-start = (f32[192,128]{1,0:T(8,128)S(1)}, f32[192,128]{1,0:T(8,128)S(1)}, u32[]{:S(2)}, u32[]{:S(2)}) collective-permute-start(f32[192,128]{1,0:T(8,128)S(1)} %get-tuple-element.13), channel_id=1, source_target_pairs={{0,1},{1,0},{2,3},{3,2},{4,5},{5,4},{6,7},{7,6},{8,9},{9,8},{10,11... | collective-permute-start | bytes 294920 | tf_op jit(solution)/shard_map/ppermute | solution.py:379
  7.4 6.5 %collective-permute-start.1 = (f32[192,128]{1,0:T(8,128)S(1)}, f32[192,128]{1,0:T(8,128)S(1)}, u32[]{:S(2)}, u32[]{:S(2)}) collective-permute-start(f32[192,128]{1,0:T(8,128)S(1)} %get-tuple-element.14), channel_id=1, source_target_pairs={{1,2},{2,1},{0,3},{3,0},{5,6},{6,5},{4,7},{7,4},{9,10},{10,9},{8,1... | collective-permute-start | bytes 294920 | tf_op jit(solution)/shard_map/ppermute | solution.py:379
  9.9 0.7 %copy-start.1 = (f32[2,384]{1,0:T(2,128)S(1)}, f32[2,384]{1,0:T(2,128)}, u32[]{:S(2)}) copy-start(f32[2,384]{1,0:T(2,128)} %shard_ref.1) | copy-start | bytes 9220
  11.2 10.5 %all-to-all-start = ((f32[32,2,384]{2,1,0:T(2,128)}), f32[32,2,384]{2,1,0:T(2,128)S(1)}, u32[]{:S(2)}, u32[]{:S(2)}) async-start(f32[32,2,384]{2,1,0:T(2,128)} %shard_map.68), calls=%async_computation | async-start | bytes 196608 | tf_op jit(solution)/shard_map/all_to_all | solution.py:369
  14.1 7.6 %collective-permute-start.4 = (f32[3,64,128]{2,1,0:T(8,128)S(1)}, f32[3,64,128]{2,1,0:T(8,128)S(1)}, u32[]{:S(2)}, u32[]{:S(2)}) collective-permute-start(f32[3,64,128]{2,1,0:T(8,128)S(1)} %get-tuple-element.18), channel_id=1, source_target_pairs={{0,4},{4,0},{8,12},{12,8},{16,20},{20,16},{24,28},{28,24},{1,5},{5... | collective-permute-start | bytes 294920 | tf_op jit(solution)/shard_map/ppermute | solution.py:379
  14.2 7.5 %collective-permute-start.5 = (f32[3,64,128]{2,1,0:T(8,128)S(1)}, f32[3,64,128]{2,1,0:T(8,128)S(1)}, u32[]{:S(2)}, u32[]{:S(2)}) collective-permute-start(f32[3,64,128]{2,1,0:T(8,128)S(1)} %get-tuple-element.19), channel_id=1, source_target_pairs={{4,8},{8,4},{12,16},{16,12},{20,24},{24,20},{0,28},{28,0},{5,9},{9... | collective-permute-start | bytes 294920 | tf_op jit(solution)/shard_map/ppermute | solution.py:379

commit v5 on v4

--- a/solution.py
+++ b/solution.py
@@ -122,7 +122,12 @@
     return jnp.asarray(whole), where
 
 
-def pack(own_ref, a_ref, b_ref, up_ref, down_ref):
+def pack(held_ref, own_ref, a_ref, b_ref, up_ref, down_ref, bank_ref):
+    cells, width = own_ref.shape[1:]
+    for index in range(3):
+        own_ref[index] = held_ref[:cells, index * width : (index + 1) * width]
+    shard = held_ref[cells : cells + CONDITIONS, : bank_ref.shape[2]]
+    bank_ref[...] = jnp.broadcast_to(shard[None], bank_ref.shape)
     odd_row = lax.rem(lax.axis_index("row"), 2) == 1
     for index in range(3):
         first, second = own_ref[index, :HALO], own_ref[index, HALO:]
@@ -148,10 +153,6 @@
     b_ref[rows:] = jnp.where(odd, to_right[1], to_left[1])
 
 
-def spread(shard_ref, out_ref):
-    out_ref[...] = jnp.broadcast_to(shard_ref[...][None], out_ref.shape)
-
-
 def widen(own_ref, a_ref, b_ref, _, __, centre_ref, up_ref, down_ref):
     half = HALO
     odd = lax.rem(lax.axis_index("col"), 2) == 1
@@ -369,14 +370,29 @@
     return lax.all_to_all(value, ("row", "col"), 0, 0)
 
 
-def pair_swap(value, axis, first, wrap=False):
-    count = lax.axis_size(axis)
+def pair_swap(value, axis, first):
+    if axis == "row":
+        count = lax.axis_size(axis)
+        pairs = []
+        for low in range(first, count - 1, 2):
+            pairs += [(low, low + 1), (low + 1, low)]
+        if first and count % 2 == 0:
+            pairs += [(0, count - 1), (count - 1, 0)]
+        return lax.ppermute(value, axis, pairs)
+    sizes = lax.axis_size("row"), lax.axis_size("col")
+    along = ("row", "col").index(axis)
     pairs = []
-    for low in range(first, count - 1, 2):
-        pairs += [(low, low + 1), (low + 1, low)]
-    if wrap and first and count % 2 == 0:
-        pairs += [(0, count - 1), (count - 1, 0)]
-    return lax.ppermute(value, axis, pairs)
+    for place in np.ndindex(*sizes):
+        other = list(place)
+        step = 1 if (place[along] - first) % 2 == 0 else -1
+        if 0 <= place[along] + step < sizes[along]:
+            other[along] += step
+        elif 0 <= place[1 - along] ^ 1 < sizes[1 - along]:
+            other[1 - along] ^= 1
+        else:
+            continue
+        pairs.append(tuple(int(r) * sizes[1] + int(c) for r, c in (place, other)))
+    return lax.ppermute(value, ("row", "col"), pairs)
 
 
 def finish(cell_count, own_ref, cells_ref, sums_ref, logits_ref, loss_ref):
@@ -396,24 +412,19 @@
         return jax.ShapeDtypeStruct(shape, f32)
 
     packed = struct(core_width * 3 // 2, core_width)
-    own = jnp.stack([mask_logits, target, weight])
     slab = struct(3, HALO, core_width)
-    slab_a, slab_b, up, down = pl.pallas_call(
+    cells = jnp.concatenate([mask_logits, target, weight], axis=1)
+    shard = jnp.pad(kernels, ((0, 0), (0, cells.shape[1] - kernels.shape[1])))
+    own, slab_a, slab_b, up, down, bank = pl.pallas_call(
         pack,
-        out_shape=(packed, packed, slab, slab),
+        out_shape=(struct(3, core_width, core_width), packed, packed, slab, slab)
+        + (struct(rows * cols, *kernels.shape),),
         in_specs=[VMEM],
-        out_specs=(VMEM,) * 4,
+        out_specs=(VMEM,) * 6,
         compiler_params=small(4),
-    )(own)
-    bank = pl.pallas_call(
-        spread,
-        out_shape=struct(rows * cols, *kernels.shape),
-        in_specs=[VMEM],
-        out_specs=VMEM,
-        compiler_params=small(4),
-    )(kernels)
-    got_a, got_b = pair_swap(slab_a, "col", 0), pair_swap(slab_b, "col", 1, wrap=True)
-    up, down = pair_swap(up, "row", 0), pair_swap(down, "row", 1, wrap=True)
+    )(jnp.concatenate([cells, shard], axis=0))
+    got_a, got_b = pair_swap(slab_a, "col", 0), pair_swap(slab_b, "col", 1)
+    up, down = pair_swap(up, "row", 0), pair_swap(down, "row", 1)
     centre, up_margin, down_margin = pl.pallas_call(
         widen,
         out_shape=(struct(3, core_width, pad_width), slab, slab),
@@ -423,7 +434,7 @@
     )(own, got_a, got_b, up, down)
     up_margin, down_margin = (
         pair_swap(up_margin, "row", 0),
-        pair_swap(down_margin, "row", 1, wrap=True),
+        pair_swap(down_margin, "row", 1),
     )
     bank = to_all(bank)
     pieces = kernels.shape[1] // LANES

time: 36.4 us -> 34 us (0.934)
  starting transfers between devices: 13.3 us -> 11.8 us
  local copies, waits for them, and re-layouts: 0.69 us -> 0.01 us
    ppermute x6 -> x4, starting transfers between devices: 10.8 us -> 5.28 us  [pair_swap(): return lax.ppermute(value, axis, pairs)]
    ppermute x0 -> x2, starting transfers between devices: none -> 3.03 us  [pair_swap(): return lax.ppermute(value, ('row', 'col'), pairs)]
    concatenate x0 -> x1, other arithmetic: none -> 1.04 us  [shards(): jnp.concatenate([cells, shard], axis=0)]
    another operation x1 -> x0, other arithmetic: 1.02 us -> none  [shards(): own = jnp.stack([mask_logits, target, weight])]
    all_to_all x1, starting transfers between devices: 2.56 us -> 3.51 us  [to_all(): return lax.all_to_all(value, ('row', 'col'), 0, 0)]
    unnamed x4 -> x2, local copies, waits for them, and re-layouts: 0.69 us -> 0.01 us
    pallas_call x2 -> x1, Pallas kernels: 0.75 us -> 0.68 us  [shards(): pl.pallas_call(pack, out_shape=(struct(3, core_width, core_width), packed...]
  transfers between devices with their start and end apart: 7 -> 7, of which waited for: 2 -> 2; matrix products, arithmetic and copies ran while one was open for 0% -> 0% of each run, Pallas kernels for 2% -> 1%
where the time goes in v5:
time: 34 us; the launch traced here: 33.8 us
  starting transfers between devices  11.8 us (35%)
  blocking collectives  10.3 us (30%)
  waiting for transfers between devices  5.02 us (15%)
  Pallas kernels  4.91 us (14%)
  other arithmetic  1.04 us (3%)
  between operations  0.69 us (2%)
    all_to_all x1, blocking collectives, to_all(): return lax.all_to_all(value, ('row', 'col'), 0, 0)  10.3 us
    ppermute x4, starting transfers between devices, pair_swap(): return lax.ppermute(value, axis, pairs)  5.28 us
    all_to_all x1, waiting for transfers between devices, to_all(): return lax.all_to_all(value, ('row', 'col'), 0, 0)  4.86 us
    all_to_all x1, starting transfers between devices, to_all(): return lax.all_to_all(value, ('row', 'col'), 0, 0)  3.51 us
    pallas_call x1, Pallas kernels, shards(): pl.pallas_call(functools.partial(step_kernel, order, place), out_shape=(s...  3.37 us
    ppermute x2, starting transfers between devices, pair_swap(): return lax.ppermute(value, ('row', 'col'), pairs)  3.03 us
    concatenate x1, other arithmetic, shards(): jnp.concatenate([cells, shard], axis=0)  1.04 us
    pallas_call x1, Pallas kernels, shards(): pl.pallas_call(functools.partial(finish, cell_count), out_shape=(struct(c...  0.69 us
  transfers between devices with their start and end apart: 7, of which 2 were waited for; matrix products, arithmetic and copies ran while one was open for 0% of the time, Pallas kernels for 1%

profile of v5, /device:TPU:0, one launch (start us, length us, event | category | flops | bytes accessed | tf_op | source)
XLA Modules:
  0.0 33.8 jit_solution(831880159239606791)
XLA Ops:
  0.6 0.0 copy-start
  0.6 1.0 %pad_maximum_fusion.held_ref = f32[130,384]{1,0:T(8,128)S(1)} fusion(f32[2,384]{1,0:T(2,128)} %param.8, f32[128,128]{1,0:T(8,128)} %param.7, f32[128,128]{1,0:T(8,128)} %param.6, f32[128,128]{1,0:T(8,128)} %param.5), kind=kLoop, calls=%fused_computation | loop fusion | flops 149760 | bytes 399360 | tf_op jit(solution)/shard_map/concatenate | solution.py:425
  1.7 0.7 %shard_map.68 = (f32[3,128,128]{2,1,0:T(8,128)S(1)}, f32[192,128]{1,0:T(8,128)S(1)}, f32[192,128]{1,0:T(8,128)S(1)}, f32[3,64,128]{2,1,0:T(8,128)S(1)}, f32[3,64...) custom-call(f32[130,384]{1,0:T(8,128)S(1)} %pad_maximum_fusion.held_ref), custom_call_target="tpu_custom_call" | custom-call | tf_op jit(solution)/shard_map/pallas_call | solution.py:418
  2.4 3.0 %collective-permute-start = (f32[192,128]{1,0:T(8,128)S(1)}, f32[192,128]{1,0:T(8,128)S(1)}, u32[]{:S(2)}, u32[]{:S(2)}) collective-permute-start(f32[192,128]{1,0:T(8,128)S(1)} %get-tuple-element.17), channel_id=1, source_target_pairs={{0,1},{1,0},{2,3},{3,2},{4,5},{5,4},{6,7},{7,6},{8,9},{9,8},{10,11... | collective-permute-start | bytes 294920 | tf_op jit(solution)/shard_map/ppermute | solution.py:395
  5.4 0.0 collective-permute-start.1
  5.4 0.5 %collective-permute-start.2 = (f32[3,64,128]{2,1,0:T(8,128)S(1)}, f32[3,64,128]{2,1,0:T(8,128)S(1)}, u32[]{:S(2)}, u32[]{:S(2)}) collective-permute-start(f32[3,64,128]{2,1,0:T(8,128)S(1)} %get-tuple-element.19), channel_id=1, source_target_pairs={{0,4},{4,0},{8,12},{12,8},{16,20},{20,16},{24,28},{28,24},{1,5},{5... | collective-permute-start | bytes 294920 | tf_op jit(solution)/shard_map/ppermute | solution.py:381
  5.9 2.1 %collective-permute-start.3 = (f32[3,64,128]{2,1,0:T(8,128)S(1)}, f32[3,64,128]{2,1,0:T(8,128)S(1)}, u32[]{:S(2)}, u32[]{:S(2)}) collective-permute-start(f32[3,64,128]{2,1,0:T(8,128)S(1)} %get-tuple-element.20), channel_id=1, source_target_pairs={{4,8},{8,4},{12,16},{16,12},{20,24},{24,20},{0,28},{28,0},{5,9},{9... | collective-permute-start | bytes 294920 | tf_op jit(solution)/shard_map/ppermute | solution.py:381
  8.0 3.5 %all-to-all-start = ((f32[32,2,384]{2,1,0:T(2,128)}), f32[32,2,384]{2,1,0:T(2,128)S(1)}, u32[]{:S(2)}, u32[]{:S(2)}) async-start(f32[32,2,384]{2,1,0:T(2,128)} %get-tuple-element.16), calls=%async_computation | async-start | bytes 196608 | tf_op jit(solution)/shard_map/all_to_all | solution.py:370
  11.5 0.0 collective-permute-done.a_ref
  11.5 0.0 collective-permute-done.1.b_ref
  11.5 0.0 collective-permute-done.2._.up_ref
  11.5 0.1 collective-permute-done.3.__.down_ref
  11.7 0.2 shard_map.69
  11.8 0.2 collective-permute-start.4
  12.0 2.5 %collective-permute-start.5 = (f32[3,64,128]{2,1,0:T(8,128)S(1)}, f32[3,64,128]{2,1,0:T(8,128)S(1)}, u32[]{:S(2)}, u32[]{:S(2)}) collective-permute-start(f32[3,64,128]{2,1,0:T(8,128)S(1)} %get-tuple-element.23), channel_id=1, source_target_pairs={{4,8},{8,4},{12,16},{16,12},{20,24},{24,20},{0,28},{28,0},{5,9},{9... | collective-permute-start | bytes 294920 | tf_op jit(solution)/shard_map/ppermute | solution.py:381
  14.6 4.9 %all-to-all-done.bank_ref = f32[32,2,384]{2,1,0:T(2,128)S(1)} async-done(((f32[32,2,384]{2,1,0:T(2,128)}), f32[32,2,384]{2,1,0:T(2,128)S(1)}, u32[]{:S(2)}, u32[]{:S(2)}) %all-to-all-start) | async-done | bytes 98336 | tf_op jit(solution)/shard_map/all_to_all | solution.py:370
  19.4 0.0 collective-permute-done.4.up_margin_ref
  19.4 0.0 collective-permute-done.5.down_margin_ref
  19.4 0.0 copy-done
  19.4 3.4 %shard_map.70 = (f32[128,128]{1,0:T(8,128)S(1)}, f32[32,2,128]{2,1,0:T(2,128)S(1)}) custom-call(f32[32,2,384]{2,1,0:T(2,128)S(1)} %all-to-all-done.bank_ref, f32[3,128,256]{2,1,0:T(8,128)S(1)} %get-tuple-element.21.centre_ref, f32[3,64,128]{2,1,0:T(8,128)S(1)} %collective-permute-done.2._.up_ref, f32[3,64,128]{2,1,0:T(8,128)S(1)} %collective-permute-done.3.__.down_ref, ...), custom_call_target="tpu_custom_call" | custom-call | tf_op jit(solution)/shard_map/pallas_call | solution.py:447
  22.8 10.3 %all_to_all.10.sums_ref = f32[32,2,128]{2,1,0:T(2,128)S(1)} all-to-all(f32[32,2,128]{2,1,0:T(2,128)S(1)} %get-tuple-element.25), channel_id=1, replica_groups=mesh['row'=8,'col'=4] {'row','col'}, dimensions={0} | all-to-all | bytes 65536 | tf_op jit(solution)/shard_map/all_to_all | solution.py:370
  33.1 0.7 %shard_map.71 = (f32[128,128]{1,0:T(8,128)}, f32[1,1]{1,0:T(1,128)}) custom-call(f32[3,128,128]{2,1,0:T(8,128)S(1)} %get-tuple-element.15.own_ref, f32[128,128]{1,0:T(8,128)S(1)} %get-tuple-element.24.cells_ref, f32[32,2,128]{2,1,0:T(2,128)S(1)} %all_to_all.10.sums_ref), custom_call_target="tpu_custom_call" | custom-call | tf_op jit(solution)/shard_map/pallas_call | solution.py:461
Async XLA Ops:
  0.6 18.8 %copy-start = (bf16[2496,256]{1,0:T(8,128)(2,1)S(1)}, bf16[2496,256]{1,0:T(8,128)(2,1)}, u32[]{:S(2)}) copy-start(bf16[2496,256]{1,0:T(8,128)(2,1)} %constant.1.clone.table_ref) | copy-start | bytes 3833860
  2.4 9.1 %collective-permute-start = (f32[192,128]{1,0:T(8,128)S(1)}, f32[192,128]{1,0:T(8,128)S(1)}, u32[]{:S(2)}, u32[]{:S(2)}) collective-permute-start(f32[192,128]{1,0:T(8,128)S(1)} %get-tuple-element.17), channel_id=1, source_target_pairs={{0,1},{1,0},{2,3},{3,2},{4,5},{5,4},{6,7},{7,6},{8,9},{9,8},{10,11... | collective-permute-start | bytes 294920 | tf_op jit(solution)/shard_map/ppermute | solution.py:395
  5.4 6.1 %collective-permute-start.1 = (f32[192,128]{1,0:T(8,128)S(1)}, f32[192,128]{1,0:T(8,128)S(1)}, u32[]{:S(2)}, u32[]{:S(2)}) collective-permute-start(f32[192,128]{1,0:T(8,128)S(1)} %get-tuple-element.18), channel_id=1, source_target_pairs={{0,4},{1,2},{2,1},{3,7},{4,0},{5,6},{6,5},{7,3},{8,12},{9,10},{10,... | collective-permute-start | bytes 294920 | tf_op jit(solution)/shard_map/ppermute | solution.py:395
  5.4 6.1 %collective-permute-start.2 = (f32[3,64,128]{2,1,0:T(8,128)S(1)}, f32[3,64,128]{2,1,0:T(8,128)S(1)}, u32[]{:S(2)}, u32[]{:S(2)}) collective-permute-start(f32[3,64,128]{2,1,0:T(8,128)S(1)} %get-tuple-element.19), channel_id=1, source_target_pairs={{0,4},{4,0},{8,12},{12,8},{16,20},{20,16},{24,28},{28,24},{1,5},{5... | collective-permute-start | bytes 294920 | tf_op jit(solution)/shard_map/ppermute | solution.py:381
  5.9 5.8 %collective-permute-start.3 = (f32[3,64,128]{2,1,0:T(8,128)S(1)}, f32[3,64,128]{2,1,0:T(8,128)S(1)}, u32[]{:S(2)}, u32[]{:S(2)}) collective-permute-start(f32[3,64,128]{2,1,0:T(8,128)S(1)} %get-tuple-element.20), channel_id=1, source_target_pairs={{4,8},{8,4},{12,16},{16,12},{20,24},{24,20},{0,28},{28,0},{5,9},{9... | collective-permute-start | bytes 294920 | tf_op jit(solution)/shard_map/ppermute | solution.py:381
  8.0 11.5 %all-to-all-start = ((f32[32,2,384]{2,1,0:T(2,128)}), f32[32,2,384]{2,1,0:T(2,128)S(1)}, u32[]{:S(2)}, u32[]{:S(2)}) async-start(f32[32,2,384]{2,1,0:T(2,128)} %get-tuple-element.16), calls=%async_computation | async-start | bytes 196608 | tf_op jit(solution)/shard_map/all_to_all | solution.py:370
  11.8 7.6 %collective-permute-start.4 = (f32[3,64,128]{2,1,0:T(8,128)S(1)}, f32[3,64,128]{2,1,0:T(8,128)S(1)}, u32[]{:S(2)}, u32[]{:S(2)}) collective-permute-start(f32[3,64,128]{2,1,0:T(8,128)S(1)} %get-tuple-element.22), channel_id=1, source_target_pairs={{0,4},{4,0},{8,12},{12,8},{16,20},{20,16},{24,28},{28,24},{1,5},{5... | collective-permute-start | bytes 294920 | tf_op jit(solution)/shard_map/ppermute | solution.py:381
  12.0 7.4 %collective-permute-start.5 = (f32[3,64,128]{2,1,0:T(8,128)S(1)}, f32[3,64,128]{2,1,0:T(8,128)S(1)}, u32[]{:S(2)}, u32[]{:S(2)}) collective-permute-start(f32[3,64,128]{2,1,0:T(8,128)S(1)} %get-tuple-element.23), channel_id=1, source_target_pairs={{4,8},{8,4},{12,16},{16,12},{20,24},{24,20},{0,28},{28,0},{5,9},{9... | collective-permute-start | bytes 294920 | tf_op jit(solution)/shard_map/ppermute | solution.py:381

commit v6 on v5

--- a/solution.py
+++ b/solution.py
@@ -153,7 +153,9 @@
     b_ref[rows:] = jnp.where(odd, to_right[1], to_left[1])
 
 
-def widen(own_ref, a_ref, b_ref, _, __, centre_ref, up_ref, down_ref):
+def widen(
+    own_ref, a_ref, b_ref, _, __, centre_ref, up_ref, *down_refs
+):
     half = HALO
     odd = lax.rem(lax.axis_index("col"), 2) == 1
     odd_row = lax.rem(lax.axis_index("row"), 2) == 1
@@ -171,79 +173,120 @@
 
     lefts = [left[:rows], left_turned[:rows], two(left[rows:], left_turned[rows:])]
     rights = [right_turned[:rows], right[:rows], two(right_turned[rows:], right[rows:])]
+    margins = []
     for index, value in enumerate(values):
         turned = pltpu.roll(value, half, 1)
         wide = jnp.concatenate(
             [jnp.where(low, lefts[index], turned), jnp.where(low, turned, rights[index])], axis=1
         )
         centre_ref[index] = wide
-        margin = jnp.where(low, wide[:, :LANES], wide[:, LANES:])
-        up_ref[index] = jnp.where(odd_row, margin[:half], margin[half:])
-        down_ref[index] = jnp.where(odd_row, margin[half:], margin[:half])
-
-
-def step_kernel(
+        margins.append(jnp.where(low, wide[:, :LANES], wide[:, LANES:]))
+    margins[0] = mask_of(margins[0], margins[2])
+    for margin, first_ref, second_ref in zip(
+        margins,
+        (up_ref.at[0], up_ref.at[1], up_ref.at[2]),
+        down_refs,
+        strict=True,
+    ):
+        first_ref[...] = jnp.where(odd_row, margin[:half], margin[half:])
+        second_ref[...] = jnp.where(odd_row, margin[half:], margin[:half])
+
+
+def beside(*blocks):
+    return jnp.concatenate(blocks, axis=1)
+
+
+def below(*blocks):
+    return jnp.concatenate(blocks, axis=0)
+
+
+class Tables:
+    def __init__(self, ref, place):
+        self.ref, self.place = ref, place
+
+    def __call__(self, name, first=0, count=None, part=0):
+        top, left, shape = self.place[name, part]
+        top, count = top + first, shape[0] - first if count is None else count
+        return self.ref[top : top + count, left : left + shape[1]]
+
+    def three(self, name, h, l):
+        th, tl = self(name, 0, LANES), self(name, LANES)
+        return dot(beside(h, l), below(th, th)) + dot(h, tl)
+
+    def six(self, name, h, m, l):
+        first = dot(self(name), below(h, m, l, h))
+        return first + dot(self(name, part=1), below(m, h))
+
+
+def above_below(first, second):
+    row = lax.axis_index("row")
+    odd = lax.rem(row, 2) == 1
+    above = jnp.where(row == 0, 0.0, jnp.where(odd, first, second))
+    last = row == lax.axis_size("row") - 1
+    return above, jnp.where(last, 0.0, jnp.where(odd, second, first))
+
+
+def spectrum_of(mask, cols, rows):
+    grid = 2 * BAND
+    low = lax.broadcasted_iota(jnp.int32, (1, LANES), 1) < LANES // 2
+    h, l = split(mask, 2)
+    both = dot(h, cols)
+    half = both[:, :LANES] + both[:, LANES:] + dot(l, cols[:, :LANES])
+    h, m, l = split(half, 3)
+    both = dot(rows[: 2 * grid], beside(h, m))
+    rest = dot(rows[2 * grid :], h) + dot(rows[:grid], l)
+    middle = both[:grid, LANES:] + both[grid:, :LANES]
+    both = both[:grid, :LANES] + middle + (both[grid:, LANES:] + rest)
+    turned = pltpu.roll(both[BAND:], LANES // 2, 1)
+    return both[:BAND] + jnp.where(low, turned, -turned)
+
+
+def mask_of(logits, weight):
+    return jnp.where(weight > 0.0, jax.nn.sigmoid(logits), 0.0)
+
+
+def before_margins(
+    place, centre_ref, up_ref, down_ref, table_ref, spectrum_ref, cells_ref, factor_ref
+):
+    table = Tables(table_ref, place)
+    low = lax.broadcasted_iota(jnp.int32, (1, LANES), 1) < LANES // 2
+
+    def padded(index):
+        ends = []
+        for own in above_below(up_ref[index], down_ref[index]):
+            turned = pltpu.roll(own, HALO, 1)
+            ends.append(beside(jnp.where(low, 0.0, turned), jnp.where(low, turned, 0.0)))
+        return below(ends[0], centre_ref[index], ends[1])
+
+    weight = padded(2)
+    mask = mask_of(padded(0), weight)
+    cells_ref[0] = padded(1)
+    cells_ref[1] = weight
+    core = slice(HALO, mask.shape[0] - HALO)
+    own = mask[core, core]
+    factor_ref[...] = own * (1.0 - own)
+    spectrum_ref[...] = spectrum_of(mask, table("analyse_cols"), table("analyse_rows"))
+
+
+def forward_kernel(
     order,
     place,
     bank_ref,
-    centre_ref,
-    up_ref,
-    down_ref,
+    spectrum_ref,
     up_margin_ref,
     down_margin_ref,
     table_ref,
-    grad_ref,
-    sums_ref,
+    spectra_ref,
+    fields_ref,
+    tall_ref,
     flat_ref,
 ):
-    row_place = lax.axis_index("row")
-    odd_row = lax.rem(row_place, 2) == 1
-    at_top, at_bottom = row_place == 0, row_place == lax.axis_size("row") - 1
     grid = 2 * BAND
     fold = LANES // BAND
     per = BAND // fold
-
-    def table(name, first=0, count=None, part=0):
-        top, left, shape = place[name, part]
-        top, count = top + first, shape[0] - first if count is None else count
-        return table_ref[top : top + count, left : left + shape[1]]
-
-    def three(name, h, l):
-        th, tl = table(name, 0, LANES), table(name, LANES)
-        return dot(beside(h, l), below(th, th)) + dot(h, tl)
-
-    def six(name, h, m, l):
-        return dot(table(name), below(h, m, l, h)) + dot(table(name, part=1), below(m, h))
-
-    def beside(*blocks):
-        return jnp.concatenate(blocks, axis=1)
-
-    def below(*blocks):
-        return jnp.concatenate(blocks, axis=0)
-
+    table = Tables(table_ref, place)
     low = lax.broadcasted_iota(jnp.int32, (1, LANES), 1) < LANES // 2
-
-    def padded(index):
-        wide = []
-        for own_ref, margin_ref in ((up_ref, up_margin_ref), (down_ref, down_margin_ref)):
-            turned, margin = pltpu.roll(own_ref[index], HALO, 1), margin_ref[index]
-            wide.append(beside(jnp.where(low, margin, turned), jnp.where(low, turned, margin)))
-        first, second = wide
-        return below(
-            jnp.where(odd_row, first, second),
-            centre_ref[index],
-            jnp.where(odd_row, second, first),
-        )
-
-    cell_row = lax.broadcasted_iota(jnp.int32, (centre_ref.shape[1] + 2 * HALO, 1), 0)
-    first_row = jnp.where(at_top, HALO, 0)
-    last_row = jnp.where(at_bottom, cell_row.shape[0] - HALO, cell_row.shape[0])
-    inside = jnp.logical_and(cell_row >= first_row, cell_row < last_row)
-    weight = jnp.where(inside, padded(2), 0.0)
-    mask = jnp.where(weight > 0.0, jax.nn.sigmoid(padded(0)), 0.0)
-    target = jnp.where(inside, padded(1), 0.0)
-    pad_width = mask.shape[0]
-    core = slice(HALO, pad_width - HALO)
+    corner_mask = below(*above_below(up_margin_ref[0], down_margin_ref[...]))
 
     for row, (device, piece) in enumerate(order):
         both = bank_ref[device, :, piece * LANES : (piece + 1) * LANES]
@@ -273,15 +316,11 @@
     pairs = [(c, k) for c in range(CONDITIONS) for k in range(KERNELS)]
     spectra = [spread(c, k) for c, k in pairs]
 
-    h, l = split(mask, 2)
-    both = dot(h, table("analyse_cols"))
-    half = both[:, :LANES] + both[:, LANES:] + dot(l, table("analyse_cols")[:, :LANES])
-    h, m, l = split(half, 3)
-    both = dot(table("analyse_rows", 0, 2 * grid), beside(h, m))
-    rest = dot(table("analyse_rows", 2 * grid), h) + dot(table("analyse_rows", 0, grid), l)
-    both = both[:grid, :LANES] + (both[:grid, LANES:] + both[grid:, :LANES]) + (both[grid:, LANES:] + rest)
-    turned = pltpu.roll(both[BAND:], LANES // 2, 1)
-    spectrum = both[:BAND] + jnp.where(low, turned, -turned)
+    cols = table("analyse_cols")
+    cols = below(cols[:HALO], cols[-HALO:])
+    rows = table("analyse_rows").astype(jnp.float32)
+    rows = jnp.where(low, rows[:, :LANES], rows[:, LANES:]).astype(jnp.bfloat16)
+    spectrum = spectrum_ref[...] + spectrum_of(corner_mask, cols, rows)
 
     products = below(*[s * spectrum for s in spectra])
     h, m, l = split(products, 3)
@@ -303,7 +342,7 @@
                 rows = part[first : first + BAND]
                 stacked.append(below(rows[:, :LANES], rows[:, LANES:]))
             parts.append(beside(*stacked))
-        field = six("field_rows", *parts)
+        field = table.six("field_rows", *parts)
         fields.append(field)
         square = square + field * field
 
@@ -314,13 +353,52 @@
     th, tm, tl = [table("up_cols", grid * index, grid) for index in range(3)]
     mixed = beside(*[part.astype(jnp.bfloat16) for part in mixed])
     tall = dot(mixed, below(th, th, th, tm, tm, tl))
-    tall = split(tall, 3)
-
+    tall_ref[...] = tall
+    for index, value in enumerate(spectra):
+        spectra_ref[index] = value
+    for index, value in enumerate(fields):
+        fields_ref[index] = value
+
+
+def backward_kernel(
+    place,
+    spectra_ref,
+    fields_ref,
+    tall_ref,
+    cells_ref,
+    factor_ref,
+    up_margin_ref,
+    down_margin_ref,
+    down_weight_ref,
+    table_ref,
+    grad_ref,
+    sums_ref,
+):
+    grid = 2 * BAND
+    table = Tables(table_ref, place)
+    low = lax.broadcasted_iota(jnp.int32, (1, LANES), 1) < LANES // 2
+    pad_width = cells_ref.shape[1]
+    core = slice(HALO, pad_width - HALO)
+
+    def filled(index):
+        cells = cells_ref[index]
+        other = (down_margin_ref, down_weight_ref)[index][...]
+        corners = above_below(up_margin_ref[index + 1], other)
+        ends = []
+        for corner, rows in zip(corners, (cells[:HALO], cells[-HALO:]), strict=True):
+            left, right = rows[:, :LANES], rows[:, LANES:]
+            ends.append(beside(jnp.where(low, corner, left), jnp.where(low, right, corner)))
+        return below(ends[0], cells[core], ends[1])
+
+    target, weight = filled(0), filled(1)
+    spectra = [spectra_ref[index] for index in range(CONDITIONS * KERNELS)]
+    fields = [fields_ref[index] for index in range(KERNELS)]
+    tall = split(tall_ref[...], 3)
     slopes = []
     loss = 0.0
     for condition, dose in enumerate(DOSES):
         parts = [part[condition * grid : (condition + 1) * grid] for part in tall]
-        intensity = six("up_rows", *parts)
+        intensity = table.six("up_rows", *parts)
         resist = jax.nn.sigmoid(SHARPNESS * (dose * intensity - THRESHOLD))
         error = resist - target
         scaled = weight * error
@@ -343,18 +421,17 @@
             turned = pltpu.roll(block[BAND:], LANES // 2, 1)
             backs[condition].append(block[:BAND] + jnp.where(low, -turned, turned))
     h, l = split(below(*backs[0], *backs[1]), 2)
-    backs = three("back_cols", h, l)
+    backs = table.three("back_cols", h, l)
     total = 0.0
     for index, spectrum in enumerate(spectra):
         total = total + spectrum * backs[index * BAND : (index + 1) * BAND]
 
     h, l = split(total, 2)
-    across = three("core_cols", h, l)
+    across = table.three("core_cols", h, l)
     core_width = across.shape[1] // 2
     h, l = split(below(across[:, :core_width], across[:, core_width:]), 2)
     gradient = dot(table("core_rows"), below(h, l, h))
-    own = mask[core, core]
-    cells = gradient * own * (1.0 - own)
+    cells = gradient * factor_ref[...]
     grad_ref[...] = cells
     square = jnp.sum(jnp.sum(cells * cells, axis=0, keepdims=True), axis=1, keepdims=True)
     loss = jnp.sum(jnp.sum(loss, axis=0, keepdims=True), axis=1, keepdims=True)
@@ -371,14 +448,6 @@
 
 
 def pair_swap(value, axis, first):
-    if axis == "row":
-        count = lax.axis_size(axis)
-        pairs = []
-        for low in range(first, count - 1, 2):
-            pairs += [(low, low + 1), (low + 1, low)]
-        if first and count % 2 == 0:
-            pairs += [(0, count - 1), (count - 1, 0)]
-        return lax.ppermute(value, axis, pairs)
     sizes = lax.axis_size("row"), lax.axis_size("col")
     along = ("row", "col").index(axis)
     pairs = []
@@ -425,17 +494,27 @@
     )(jnp.concatenate([cells, shard], axis=0))
     got_a, got_b = pair_swap(slab_a, "col", 0), pair_swap(slab_b, "col", 1)
     up, down = pair_swap(up, "row", 0), pair_swap(down, "row", 1)
-    centre, up_margin, down_margin = pl.pallas_call(
+    centre, up_margin, *down_margins = pl.pallas_call(
         widen,
-        out_shape=(struct(3, core_width, pad_width), slab, slab),
+        out_shape=(struct(3, core_width, pad_width), slab) + (struct(HALO, core_width),) * 3,
         in_specs=[VMEM] * 3 + [pl.BlockSpec(memory_space=pl.ANY)] * 2,
-        out_specs=(VMEM,) * 3,
+        out_specs=(VMEM,) * 5,
         compiler_params=small(8),
     )(own, got_a, got_b, up, down)
-    up_margin, down_margin = (
-        pair_swap(up_margin, "row", 0),
-        pair_swap(down_margin, "row", 1),
-    )
+    up_margin = pair_swap(up_margin, "row", 0)
+    down_margins = [pair_swap(margin, "row", 1) for margin in down_margins]
+    consts, place = tables(pad_width, HALO)
+    spectrum, cells, factor = pl.pallas_call(
+        functools.partial(before_margins, place),
+        out_shape=(
+            struct(BAND, LANES),
+            struct(2, pad_width, pad_width),
+            struct(core_width, core_width),
+        ),
+        in_specs=[VMEM] * 4,
+        out_specs=(VMEM,) * 3,
+        compiler_params=small(16),
+    )(centre, up, down, consts)
     bank = to_all(bank)
     pieces = kernels.shape[1] // LANES
     if kernels.shape[1] % LANES:
@@ -443,18 +522,25 @@
         pieces = bank.shape[2] // LANES
     order = [(device, piece) for device in range(bank.shape[0]) for piece in range(pieces)]
 
-    consts, place = tables(pad_width, HALO)
+    spectra, fields, tall = pl.pallas_call(
+        functools.partial(forward_kernel, order, place),
+        out_shape=(
+            struct(CONDITIONS * KERNELS, BAND, LANES),
+            struct(KERNELS, 2 * BAND, 2 * LANES),
+            struct(CONDITIONS * 2 * BAND, pad_width),
+        ),
+        in_specs=[VMEM] * 5,
+        out_specs=(VMEM,) * 3,
+        scratch_shapes=[pltpu.VMEM((CONDITIONS, len(order), LANES), f32)],
+        compiler_params=small(16),
+    )(bank, spectrum, up_margin, down_margins[0], consts)
     grad_cells, sums = pl.pallas_call(
-        functools.partial(step_kernel, order, place),
-        out_shape=(
-            struct(core_width, core_width),
-            struct(rows * cols, 2, LANES),
-        ),
-        in_specs=[VMEM] * 7,
+        functools.partial(backward_kernel, place),
+        out_shape=(struct(core_width, core_width), struct(rows * cols, 2, LANES)),
+        in_specs=[VMEM] * 9,
         out_specs=(VMEM,) * 2,
-        scratch_shapes=[pltpu.VMEM((CONDITIONS, len(order), LANES), f32)],
-        compiler_params=pltpu.CompilerParams(vmem_limit_bytes=16 * 1024 * 1024),
-    )(bank, centre, up, down, up_margin, down_margin, consts)
+        compiler_params=small(16),
+    )(spectra, fields, tall, cells, factor, up_margin, *down_margins[1:], consts)
 
     sums = to_all(sums)
     cell_count = rows * cols * core_width * core_width

time: 34 us -> 33.6 us (0.988)
  waiting for transfers between devices: 5.02 us -> 3.05 us
  starting transfers between devices: 11.8 us -> 13.5 us
  blocking collectives: 10.3 us -> 9.63 us
  Pallas kernels: 4.91 us -> 5.38 us
    ppermute x2 -> x8, starting transfers between devices: 3.03 us -> 10.6 us  [pair_swap(): return lax.ppermute(value, ('row', 'col'), pairs)]
    ppermute x4 -> x0, starting transfers between devices: 5.28 us -> none  [pair_swap(): return lax.ppermute(value, axis, pairs)]
    all_to_all x1, waiting for transfers between devices: 4.86 us -> 3.03 us  [to_all(): return lax.all_to_all(value, ('row', 'col'), 0, 0)]
    all_to_all x1, blocking collectives: 10.3 us -> 9.63 us  [to_all(): return lax.all_to_all(value, ('row', 'col'), 0, 0)]
    all_to_all x1, starting transfers between devices: 3.51 us -> 2.98 us  [to_all(): return lax.all_to_all(value, ('row', 'col'), 0, 0)]
    pallas_call x2 -> x4, Pallas kernels: 3.54 us -> 4 us  [the longest x1 1.79 us: shards(): pl.pallas_call(functools.partial(backward_kernel, place), out_shape=(stru...]
  transfers between devices with their start and end apart: 7 -> 9, of which waited for: 2 -> 1; matrix products, arithmetic and copies ran while one was open for 0% -> 0% of each run, Pallas kernels for 1% -> 7%
where the time goes in v6:
time: 33.6 us; the launch traced here: 33.4 us
  starting transfers between devices  13.5 us (40%)
  blocking collectives  9.63 us (29%)
  Pallas kernels  5.38 us (16%)
  waiting for transfers between devices  3.05 us (9%)
  other arithmetic  1.04 us (3%)
  between operations  0.72 us (2%)
    ppermute x8, starting transfers between devices, pair_swap(): return lax.ppermute(value, ('row', 'col'), pairs)  10.6 us
    all_to_all x1, blocking collectives, to_all(): return lax.all_to_all(value, ('row', 'col'), 0, 0)  9.63 us
    all_to_all x1, waiting for transfers between devices, to_all(): return lax.all_to_all(value, ('row', 'col'), 0, 0)  3.03 us
    all_to_all x1, starting transfers between devices, to_all(): return lax.all_to_all(value, ('row', 'col'), 0, 0)  2.98 us
    pallas_call x1, Pallas kernels, shards(): pl.pallas_call(functools.partial(backward_kernel, place), out_shape=(stru...  1.79 us
    pallas_call x1, Pallas kernels, shards(): pl.pallas_call(functools.partial(forward_kernel, order, place), out_shape...  1.48 us
    concatenate x1, other arithmetic, shards(): jnp.concatenate([cells, shard], axis=0)  1.04 us
    pallas_call x1, Pallas kernels, shards(): pl.pallas_call(functools.partial(finish, cell_count), out_shape=(struct(c...  0.69 us
  transfers between devices with their start and end apart: 9, of which 1 were waited for; matrix products, arithmetic and copies ran while one was open for 0% of the time, Pallas kernels for 7%

profile of v6, /device:TPU:0, one launch (start us, length us, event | category | flops | bytes accessed | tf_op | source)
XLA Modules:
  0.0 33.4 jit_solution(2637122612090160282)
XLA Ops:
  0.6 0.0 copy-start
  0.6 1.0 %pad_maximum_fusion.held_ref = f32[130,384]{1,0:T(8,128)S(1)} fusion(f32[2,384]{1,0:T(2,128)} %param.8, f32[128,128]{1,0:T(8,128)} %param.7, f32[128,128]{1,0:T(8,128)} %param.6, f32[128,128]{1,0:T(8,128)} %param.5), kind=kLoop, calls=%fused_computation | loop fusion | flops 149760 | bytes 399360 | tf_op jit(solution)/shard_map/concatenate | solution.py:494
  1.7 0.7 %shard_map.68 = (f32[3,128,128]{2,1,0:T(8,128)S(1)}, f32[192,128]{1,0:T(8,128)S(1)}, f32[192,128]{1,0:T(8,128)S(1)}, f32[3,64,128]{2,1,0:T(8,128)S(1)}, f32[3,64...) custom-call(f32[130,384]{1,0:T(8,128)S(1)} %pad_maximum_fusion.held_ref), custom_call_target="tpu_custom_call" | custom-call | tf_op jit(solution)/shard_map/pallas_call | solution.py:487
  2.4 3.0 %collective-permute-start = (f32[192,128]{1,0:T(8,128)S(1)}, f32[192,128]{1,0:T(8,128)S(1)}, u32[]{:S(2)}, u32[]{:S(2)}) collective-permute-start(f32[192,128]{1,0:T(8,128)S(1)} %get-tuple-element.25), channel_id=1, source_target_pairs={{0,1},{1,0},{2,3},{3,2},{4,5},{5,4},{6,7},{7,6},{8,9},{9,8},{10,11... | collective-permute-start | bytes 294920 | tf_op jit(solution)/shard_map/ppermute | solution.py:464
  5.4 0.0 collective-permute-start.1
  5.4 0.5 %collective-permute-start.2 = (f32[3,64,128]{2,1,0:T(8,128)S(1)}, f32[3,64,128]{2,1,0:T(8,128)S(1)}, u32[]{:S(2)}, u32[]{:S(2)}) collective-permute-start(f32[3,64,128]{2,1,0:T(8,128)S(1)} %get-tuple-element.27), channel_id=1, source_target_pairs={{0,4},{1,5},{2,6},{3,7},{4,0},{5,1},{6,2},{7,3},{8,12},{9,13},{10,... | collective-permute-start | bytes 294920 | tf_op jit(solution)/shard_map/ppermute | solution.py:464
  5.9 2.6 %collective-permute-start.3 = (f32[3,64,128]{2,1,0:T(8,128)S(1)}, f32[3,64,128]{2,1,0:T(8,128)S(1)}, u32[]{:S(2)}, u32[]{:S(2)}) collective-permute-start(f32[3,64,128]{2,1,0:T(8,128)S(1)} %get-tuple-element.28), channel_id=1, source_target_pairs={{0,1},{1,0},{2,3},{3,2},{4,8},{5,9},{6,10},{7,11},{8,4},{9,5},{10,... | collective-permute-start | bytes 294920 | tf_op jit(solution)/shard_map/ppermute | solution.py:464
  8.6 3.0 %all-to-all-start = ((f32[32,2,384]{2,1,0:T(2,128)}), f32[32,2,384]{2,1,0:T(2,128)S(1)}, u32[]{:S(2)}, u32[]{:S(2)}) async-start(f32[32,2,384]{2,1,0:T(2,128)} %get-tuple-element.24), calls=%async_computation | async-start | bytes 196608 | tf_op jit(solution)/shard_map/all_to_all | solution.py:447
  11.5 0.0 collective-permute-done.a_ref
  11.6 0.0 collective-permute-done.1.b_ref
  11.6 0.0 collective-permute-done.2._.up_ref
  11.6 0.0 collective-permute-done.3.__.down_ref
  11.6 0.2 shard_map.69
  11.8 0.3 collective-permute-start.4
  12.1 2.0 %collective-permute-start.5 = (f32[64,128]{1,0:T(8,128)S(1)}, f32[64,128]{1,0:T(8,128)S(1)}, u32[]{:S(2)}, u32[]{:S(2)}) collective-permute-start(f32[64,128]{1,0:T(8,128)S(1)} %get-tuple-element.32), channel_id=1, source_target_pairs={{0,1},{1,0},{2,3},{3,2},{4,8},{5,9},{6,10},{7,11},{8,4},{9,5},{10,... | collective-permute-start | bytes 98312 | tf_op jit(solution)/shard_map/ppermute | solution.py:464
  14.1 0.0 collective-permute-start.6
  14.2 2.0 %collective-permute-start.7 = (f32[64,128]{1,0:T(8,128)S(1)}, f32[64,128]{1,0:T(8,128)S(1)}, u32[]{:S(2)}, u32[]{:S(2)}) collective-permute-start(f32[64,128]{1,0:T(8,128)S(1)} %get-tuple-element.39), channel_id=1, source_target_pairs={{0,1},{1,0},{2,3},{3,2},{4,8},{5,9},{6,10},{7,11},{8,4},{9,5},{10,... | collective-permute-start | bytes 98312 | tf_op jit(solution)/shard_map/ppermute | solution.py:464
  16.2 0.0 copy-done
  16.2 0.6 %shard_map.70 = (f32[32,128]{1,0:T(8,128)S(1)}, f32[2,256,256]{2,1,0:T(8,128)S(1)}, f32[128,128]{1,0:T(8,128)S(1)}) custom-call(f32[3,128,256]{2,1,0:T(8,128)S(1)} %get-tuple-element.29.centre_ref, f32[3,64,128]{2,1,0:T(8,128)S(1)} %collective-permute-done.2._.up_ref, f32[3,64,128]{2,1,0:T(8,128)S(1)} %collective-permute-done.3.__.down_ref, ...), custom_call_target="tpu_custom_call" | custom-call | tf_op jit(solution)/shard_map/pallas_call | solution.py:507
  16.7 0.0 collective-permute-done.5.down_margin_ref
  16.7 3.0 %all-to-all-done.bank_ref = f32[32,2,384]{2,1,0:T(2,128)S(1)} async-done(((f32[32,2,384]{2,1,0:T(2,128)}), f32[32,2,384]{2,1,0:T(2,128)S(1)}, u32[]{:S(2)}, u32[]{:S(2)}) %all-to-all-start) | async-done | bytes 98336 | tf_op jit(solution)/shard_map/all_to_all | solution.py:447
  19.8 0.0 collective-permute-done.4.up_margin_ref
  19.8 1.5 %shard_map.71 = (f32[12,32,128]{2,1,0:T(8,128)S(1)}, f32[6,64,256]{2,1,0:T(8,128)S(1)}, f32[128,256]{1,0:T(8,128)S(1)}) custom-call(f32[32,2,384]{2,1,0:T(2,128)S(1)} %all-to-all-done.bank_ref, f32[32,128]{1,0:T(8,128)S(1)} %get-tuple-element.30.spectrum_ref, f32[3,64,128]{2,1,0:T(8,128)S(1)} %collective-permute-done.4.up_margin_ref, ...), custom_call_target="tpu_custom_call" | custom-call | tf_op jit(solution)/shard_map/pallas_call | solution.py:525
  21.2 0.0 collective-permute-done.6.down_margin_ref
  21.2 0.0 collective-permute-done.7.down_weight_ref
  21.3 1.8 %shard_map.72 = (f32[128,128]{1,0:T(8,128)S(1)}, f32[32,2,128]{2,1,0:T(2,128)S(1)}) custom-call(f32[12,32,128]{2,1,0:T(8,128)S(1)} %get-tuple-element.33.spectra_ref, f32[6,64,256]{2,1,0:T(8,128)S(1)} %get-tuple-element.34.fields_ref, f32[128,256]{1,0:T(8,128)S(1)} %get-tuple-element.35.tall_ref, f32[2,256,256]{2,1,0:T(8,128)S(1)} %get-tuple-element.36.cells_ref, ...), custom_call_target="tpu_custom_call" | custom-call | tf_op jit(solution)/shard_map/pallas_call | solution.py:537
  23.0 9.6 %all_to_all.10.sums_ref = f32[32,2,128]{2,1,0:T(2,128)S(1)} all-to-all(f32[32,2,128]{2,1,0:T(2,128)S(1)} %get-tuple-element.41), channel_id=1, replica_groups=mesh['row'=8,'col'=4] {'row','col'}, dimensions={0} | all-to-all | bytes 65536 | tf_op jit(solution)/shard_map/all_to_all | solution.py:447
  32.7 0.7 %shard_map.73 = (f32[128,128]{1,0:T(8,128)}, f32[1,1]{1,0:T(1,128)}) custom-call(f32[3,128,128]{2,1,0:T(8,128)S(1)} %get-tuple-element.23.own_ref, f32[128,128]{1,0:T(8,128)S(1)} %get-tuple-element.40.cells_ref, f32[32,2,128]{2,1,0:T(2,128)S(1)} %all_to_all.10.sums_ref), custom_call_target="tpu_custom_call" | custom-call | tf_op jit(solution)/shard_map/pallas_call | solution.py:547
Async XLA Ops:
  0.6 15.5 %copy-start = (bf16[2496,256]{1,0:T(8,128)(2,1)S(1)}, bf16[2496,256]{1,0:T(8,128)(2,1)}, u32[]{:S(2)}) copy-start(bf16[2496,256]{1,0:T(8,128)(2,1)} %constant.1.clone.table_ref) | copy-start | bytes 3833860
  2.4 9.2 %collective-permute-start = (f32[192,128]{1,0:T(8,128)S(1)}, f32[192,128]{1,0:T(8,128)S(1)}, u32[]{:S(2)}, u32[]{:S(2)}) collective-permute-start(f32[192,128]{1,0:T(8,128)S(1)} %get-tuple-element.25), channel_id=1, source_target_pairs={{0,1},{1,0},{2,3},{3,2},{4,5},{5,4},{6,7},{7,6},{8,9},{9,8},{10,11... | collective-permute-start | bytes 294920 | tf_op jit(solution)/shard_map/ppermute | solution.py:464
  5.4 6.2 %collective-permute-start.1 = (f32[192,128]{1,0:T(8,128)S(1)}, f32[192,128]{1,0:T(8,128)S(1)}, u32[]{:S(2)}, u32[]{:S(2)}) collective-permute-start(f32[192,128]{1,0:T(8,128)S(1)} %get-tuple-element.26), channel_id=1, source_target_pairs={{0,4},{1,2},{2,1},{3,7},{4,0},{5,6},{6,5},{7,3},{8,12},{9,10},{10,... | collective-permute-start | bytes 294920 | tf_op jit(solution)/shard_map/ppermute | solution.py:464
  5.4 6.2 %collective-permute-start.2 = (f32[3,64,128]{2,1,0:T(8,128)S(1)}, f32[3,64,128]{2,1,0:T(8,128)S(1)}, u32[]{:S(2)}, u32[]{:S(2)}) collective-permute-start(f32[3,64,128]{2,1,0:T(8,128)S(1)} %get-tuple-element.27), channel_id=1, source_target_pairs={{0,4},{1,5},{2,6},{3,7},{4,0},{5,1},{6,2},{7,3},{8,12},{9,13},{10,... | collective-permute-start | bytes 294920 | tf_op jit(solution)/shard_map/ppermute | solution.py:464
  5.9 5.7 %collective-permute-start.3 = (f32[3,64,128]{2,1,0:T(8,128)S(1)}, f32[3,64,128]{2,1,0:T(8,128)S(1)}, u32[]{:S(2)}, u32[]{:S(2)}) collective-permute-start(f32[3,64,128]{2,1,0:T(8,128)S(1)} %get-tuple-element.28), channel_id=1, source_target_pairs={{0,1},{1,0},{2,3},{3,2},{4,8},{5,9},{6,10},{7,11},{8,4},{9,5},{10,... | collective-permute-start | bytes 294920 | tf_op jit(solution)/shard_map/ppermute | solution.py:464
  8.6 11.2 %all-to-all-start = ((f32[32,2,384]{2,1,0:T(2,128)}), f32[32,2,384]{2,1,0:T(2,128)S(1)}, u32[]{:S(2)}, u32[]{:S(2)}) async-start(f32[32,2,384]{2,1,0:T(2,128)} %get-tuple-element.24), calls=%async_computation | async-start | bytes 196608 | tf_op jit(solution)/shard_map/all_to_all | solution.py:447
  11.8 8.0 %collective-permute-start.4 = (f32[3,64,128]{2,1,0:T(8,128)S(1)}, f32[3,64,128]{2,1,0:T(8,128)S(1)}, u32[]{:S(2)}, u32[]{:S(2)}) collective-permute-start(f32[3,64,128]{2,1,0:T(8,128)S(1)} %get-tuple-element.31), channel_id=1, source_target_pairs={{0,4},{1,5},{2,6},{3,7},{4,0},{5,1},{6,2},{7,3},{8,12},{9,13},{10,... | collective-permute-start | bytes 294920 | tf_op jit(solution)/shard_map/ppermute | solution.py:464
  12.1 4.6 %collective-permute-start.5 = (f32[64,128]{1,0:T(8,128)S(1)}, f32[64,128]{1,0:T(8,128)S(1)}, u32[]{:S(2)}, u32[]{:S(2)}) collective-permute-start(f32[64,128]{1,0:T(8,128)S(1)} %get-tuple-element.32), channel_id=1, source_target_pairs={{0,1},{1,0},{2,3},{3,2},{4,8},{5,9},{6,10},{7,11},{8,4},{9,5},{10,... | collective-permute-start | bytes 98312 | tf_op jit(solution)/shard_map/ppermute | solution.py:464
  14.1 7.1 %collective-permute-start.6 = (f32[64,128]{1,0:T(8,128)S(1)}, f32[64,128]{1,0:T(8,128)S(1)}, u32[]{:S(2)}, u32[]{:S(2)}) collective-permute-start(f32[64,128]{1,0:T(8,128)S(1)} %get-tuple-element.38), channel_id=1, source_target_pairs={{0,1},{1,0},{2,3},{3,2},{4,8},{5,9},{6,10},{7,11},{8,4},{9,5},{10,... | collective-permute-start | bytes 98312 | tf_op jit(solution)/shard_map/ppermute | solution.py:464
  14.2 7.1 %collective-permute-start.7 = (f32[64,128]{1,0:T(8,128)S(1)}, f32[64,128]{1,0:T(8,128)S(1)}, u32[]{:S(2)}, u32[]{:S(2)}) collective-permute-start(f32[64,128]{1,0:T(8,128)S(1)} %get-tuple-element.39), channel_id=1, source_target_pairs={{0,1},{1,0},{2,3},{3,2},{4,8},{5,9},{6,10},{7,11},{8,4},{9,5},{10,... | collective-permute-start | bytes 98312 | tf_op jit(solution)/shard_map/ppermute | solution.py:464

commit v7 on v6

--- a/solution.py
+++ b/solution.py
@@ -154,7 +154,7 @@
 
 
 def widen(
-    own_ref, a_ref, b_ref, _, __, centre_ref, up_ref, *down_refs
+    own_ref, a_ref, b_ref, _, centre_ref, up_ref, down_ref, down_weight_ref
 ):
     half = HALO
     odd = lax.rem(lax.axis_index("col"), 2) == 1
@@ -185,7 +185,7 @@
     for margin, first_ref, second_ref in zip(
         margins,
         (up_ref.at[0], up_ref.at[1], up_ref.at[2]),
-        down_refs,
+        (down_ref.at[0], down_ref.at[1], down_weight_ref),
         strict=True,
     ):
         first_ref[...] = jnp.where(odd_row, margin[:half], margin[half:])
@@ -286,7 +286,7 @@
     per = BAND // fold
     table = Tables(table_ref, place)
     low = lax.broadcasted_iota(jnp.int32, (1, LANES), 1) < LANES // 2
-    corner_mask = below(*above_below(up_margin_ref[0], down_margin_ref[...]))
+    corner_mask = below(*above_below(up_margin_ref[0], down_margin_ref[0]))
 
     for row, (device, piece) in enumerate(order):
         both = bank_ref[device, :, piece * LANES : (piece + 1) * LANES]
@@ -382,7 +382,7 @@
 
     def filled(index):
         cells = cells_ref[index]
-        other = (down_margin_ref, down_weight_ref)[index][...]
+        other = (down_margin_ref[1], down_weight_ref[...])[index]
         corners = above_below(up_margin_ref[index + 1], other)
         ends = []
         for corner, rows in zip(corners, (cells[:HALO], cells[-HALO:]), strict=True):
@@ -494,15 +494,17 @@
     )(jnp.concatenate([cells, shard], axis=0))
     got_a, got_b = pair_swap(slab_a, "col", 0), pair_swap(slab_b, "col", 1)
     up, down = pair_swap(up, "row", 0), pair_swap(down, "row", 1)
-    centre, up_margin, *down_margins = pl.pallas_call(
+    margin = struct(2, HALO, core_width)
+    centre, up_margin, down_margin, down_weight = pl.pallas_call(
         widen,
-        out_shape=(struct(3, core_width, pad_width), slab) + (struct(HALO, core_width),) * 3,
-        in_specs=[VMEM] * 3 + [pl.BlockSpec(memory_space=pl.ANY)] * 2,
-        out_specs=(VMEM,) * 5,
+        out_shape=(struct(3, core_width, pad_width), slab, margin, struct(HALO, core_width)),
+        in_specs=[VMEM] * 3 + [pl.BlockSpec(memory_space=pl.ANY)],
+        out_specs=(VMEM,) * 4,
         compiler_params=small(8),
-    )(own, got_a, got_b, up, down)
+    )(own, got_a, got_b, down)
     up_margin = pair_swap(up_margin, "row", 0)
-    down_margins = [pair_swap(margin, "row", 1) for margin in down_margins]
+    down_margin = pair_swap(down_margin, "row", 1)
+    down_weight = pair_swap(down_weight, "row", 1)
     consts, place = tables(pad_width, HALO)
     spectrum, cells, factor = pl.pallas_call(
         functools.partial(before_margins, place),
@@ -533,14 +535,14 @@
         out_specs=(VMEM,) * 3,
         scratch_shapes=[pltpu.VMEM((CONDITIONS, len(order), LANES), f32)],
         compiler_params=small(16),
-    )(bank, spectrum, up_margin, down_margins[0], consts)
+    )(bank, spectrum, up_margin, down_margin, consts)
     grad_cells, sums = pl.pallas_call(
         functools.partial(backward_kernel, place),
         out_shape=(struct(core_width, core_width), struct(rows * cols, 2, LANES)),
         in_specs=[VMEM] * 9,
         out_specs=(VMEM,) * 2,
         compiler_params=small(16),
-    )(spectra, fields, tall, cells, factor, up_margin, *down_margins[1:], consts)
+    )(spectra, fields, tall, cells, factor, up_margin, down_margin, down_weight, consts)
 
     sums = to_all(sums)
     cell_count = rows * cols * core_width * core_width

time: 33.6 us -> 33.2 us (0.988)
  starting transfers between devices: 13.5 us -> 11.4 us
  waiting for transfers between devices: 3.05 us -> 4.8 us
    ppermute x8 -> x7, waiting for transfers between devices: 0.02 us -> 2.18 us  [pair_swap(): return lax.ppermute(value, ('row', 'col'), pairs)]
    ppermute x8 -> x7, starting transfers between devices: 10.6 us -> 8.84 us  [pair_swap(): return lax.ppermute(value, ('row', 'col'), pairs)]
    all_to_all x1, starting transfers between devices: 2.98 us -> 2.55 us  [to_all(): return lax.all_to_all(value, ('row', 'col'), 0, 0)]
    all_to_all x1, waiting for transfers between devices: 3.03 us -> 2.61 us  [to_all(): return lax.all_to_all(value, ('row', 'col'), 0, 0)]
  transfers between devices with their start and end apart: 9 -> 8, of which waited for: 1 -> 2; matrix products, arithmetic and copies ran while one was open for 0% -> 0% of each run, Pallas kernels for 7% -> 7%
where the time goes in v7:
time: 33.2 us; the launch traced here: 33 us
  starting transfers between devices  11.4 us (34%)
  blocking collectives  9.67 us (29%)
  Pallas kernels  5.38 us (16%)
  waiting for transfers between devices  4.8 us (14%)
  other arithmetic  1.04 us (3%)
  between operations  0.67 us (2%)
    all_to_all x1, blocking collectives, to_all(): return lax.all_to_all(value, ('row', 'col'), 0, 0)  9.67 us
    ppermute x7, starting transfers between devices, pair_swap(): return lax.ppermute(value, ('row', 'col'), pairs)  8.84 us
    all_to_all x1, waiting for transfers between devices, to_all(): return lax.all_to_all(value, ('row', 'col'), 0, 0)  2.61 us
    all_to_all x1, starting transfers between devices, to_all(): return lax.all_to_all(value, ('row', 'col'), 0, 0)  2.55 us
    ppermute x7, waiting for transfers between devices, pair_swap(): return lax.ppermute(value, ('row', 'col'), pairs)  2.18 us
    pallas_call x1, Pallas kernels, shards(): pl.pallas_call(functools.partial(backward_kernel, place), out_shape=(stru...  1.79 us
    pallas_call x1, Pallas kernels, shards(): pl.pallas_call(functools.partial(forward_kernel, order, place), out_shape...  1.48 us
    concatenate x1, other arithmetic, shards(): jnp.concatenate([cells, shard], axis=0)  1.04 us
  transfers between devices with their start and end apart: 8, of which 2 were waited for; matrix products, arithmetic and copies ran while one was open for 0% of the time, Pallas kernels for 7%

profile of v7, /device:TPU:0, one launch (start us, length us, event | category | flops | bytes accessed | tf_op | source)
XLA Modules:
  0.0 33.0 jit_solution(12462131423944943583)
XLA Ops:
  0.6 0.0 copy-start
  0.6 1.0 %pad_maximum_fusion.held_ref = f32[130,384]{1,0:T(8,128)S(1)} fusion(f32[2,384]{1,0:T(2,128)} %param.8, f32[128,128]{1,0:T(8,128)} %param.7, f32[128,128]{1,0:T(8,128)} %param.6, f32[128,128]{1,0:T(8,128)} %param.5), kind=kLoop, calls=%fused_computation | loop fusion | flops 149760 | bytes 399360 | tf_op jit(solution)/shard_map/concatenate | solution.py:494
  1.7 0.7 %shard_map.68 = (f32[3,128,128]{2,1,0:T(8,128)S(1)}, f32[192,128]{1,0:T(8,128)S(1)}, f32[192,128]{1,0:T(8,128)S(1)}, f32[3,64,128]{2,1,0:T(8,128)S(1)}, f32[3,64...) custom-call(f32[130,384]{1,0:T(8,128)S(1)} %pad_maximum_fusion.held_ref), custom_call_target="tpu_custom_call" | custom-call | tf_op jit(solution)/shard_map/pallas_call | solution.py:487
  2.4 3.0 %collective-permute-start = (f32[192,128]{1,0:T(8,128)S(1)}, f32[192,128]{1,0:T(8,128)S(1)}, u32[]{:S(2)}, u32[]{:S(2)}) collective-permute-start(f32[192,128]{1,0:T(8,128)S(1)} %get-tuple-element.24), channel_id=1, source_target_pairs={{0,1},{1,0},{2,3},{3,2},{4,5},{5,4},{6,7},{7,6},{8,9},{9,8},{10,11... | collective-permute-start | bytes 294920 | tf_op jit(solution)/shard_map/ppermute | solution.py:464
  5.4 0.0 collective-permute-start.1
  5.4 3.1 %collective-permute-start.2 = (f32[3,64,128]{2,1,0:T(8,128)S(1)}, f32[3,64,128]{2,1,0:T(8,128)S(1)}, u32[]{:S(2)}, u32[]{:S(2)}) collective-permute-start(f32[3,64,128]{2,1,0:T(8,128)S(1)} %get-tuple-element.26), channel_id=1, source_target_pairs={{0,1},{1,0},{2,3},{3,2},{4,8},{5,9},{6,10},{7,11},{8,4},{9,5},{10,... | collective-permute-start | bytes 294920 | tf_op jit(solution)/shard_map/ppermute | solution.py:464
  8.5 2.6 %all-to-all-start = ((f32[32,2,384]{2,1,0:T(2,128)}), f32[32,2,384]{2,1,0:T(2,128)S(1)}, u32[]{:S(2)}, u32[]{:S(2)}) async-start(f32[32,2,384]{2,1,0:T(2,128)} %get-tuple-element.23), calls=%async_computation | async-start | bytes 196608 | tf_op jit(solution)/shard_map/all_to_all | solution.py:447
  11.1 0.3 collective-permute-start.3
  11.4 0.0 collective-permute-done.a_ref
  11.4 0.0 collective-permute-done.1.b_ref
  11.4 0.0 collective-permute-done.2._.down_ref
  11.4 0.2 shard_map.69
  11.6 0.3 %collective-permute-start.4 = (f32[3,64,128]{2,1,0:T(8,128)S(1)}, f32[3,64,128]{2,1,0:T(8,128)S(1)}, u32[]{:S(2)}, u32[]{:S(2)}) collective-permute-start(f32[3,64,128]{2,1,0:T(8,128)S(1)} %get-tuple-element.30), channel_id=1, source_target_pairs={{0,4},{1,5},{2,6},{3,7},{4,0},{5,1},{6,2},{7,3},{8,12},{9,13},{10,... | collective-permute-start | bytes 294920 | tf_op jit(solution)/shard_map/ppermute | solution.py:464
  11.9 1.8 %collective-permute-start.5 = (f32[2,64,128]{2,1,0:T(8,128)S(1)}, f32[2,64,128]{2,1,0:T(8,128)S(1)}, u32[]{:S(2)}, u32[]{:S(2)}) collective-permute-start(f32[2,64,128]{2,1,0:T(8,128)S(1)} %get-tuple-element.31), channel_id=1, source_target_pairs={{0,1},{1,0},{2,3},{3,2},{4,8},{5,9},{6,10},{7,11},{8,4},{9,5},{10,... | collective-permute-start | bytes 196616 | tf_op jit(solution)/shard_map/ppermute | solution.py:464
  13.7 0.3 collective-permute-start.6
  14.0 0.0 collective-permute-done.3.up_ref
  14.0 0.0 copy-done
  14.0 0.6 %shard_map.70 = (f32[32,128]{1,0:T(8,128)S(1)}, f32[2,256,256]{2,1,0:T(8,128)S(1)}, f32[128,128]{1,0:T(8,128)S(1)}) custom-call(f32[3,128,256]{2,1,0:T(8,128)S(1)} %get-tuple-element.27.centre_ref, f32[3,64,128]{2,1,0:T(8,128)S(1)} %collective-permute-done.3.up_ref, f32[3,64,128]{2,1,0:T(8,128)S(1)} %collective-permute-done.2._.down_ref, ...), custom_call_target="tpu_custom_call" | custom-call | tf_op jit(solution)/shard_map/pallas_call | solution.py:509
  14.5 2.2 %collective-permute-done.5.down_margin_ref = f32[2,64,128]{2,1,0:T(8,128)S(1)} collective-permute-done((f32[2,64,128]{2,1,0:T(8,128)S(1)}, f32[2,64,128]{2,1,0:T(8,128)S(1)}, u32[]{:S(2)}, u32[]{:S(2)}) %collective-permute-start.5) | collective-permute-done | bytes 65568 | tf_op jit(solution)/shard_map/ppermute | solution.py:464
  16.7 2.6 %all-to-all-done.bank_ref = f32[32,2,384]{2,1,0:T(2,128)S(1)} async-done(((f32[32,2,384]{2,1,0:T(2,128)}), f32[32,2,384]{2,1,0:T(2,128)S(1)}, u32[]{:S(2)}, u32[]{:S(2)}) %all-to-all-start) | async-done | bytes 98336 | tf_op jit(solution)/shard_map/all_to_all | solution.py:447
  19.3 0.0 collective-permute-done.4.up_margin_ref
  19.3 1.5 %shard_map.71 = (f32[12,32,128]{2,1,0:T(8,128)S(1)}, f32[6,64,256]{2,1,0:T(8,128)S(1)}, f32[128,256]{1,0:T(8,128)S(1)}) custom-call(f32[32,2,384]{2,1,0:T(2,128)S(1)} %all-to-all-done.bank_ref, f32[32,128]{1,0:T(8,128)S(1)} %get-tuple-element.29.spectrum_ref, f32[3,64,128]{2,1,0:T(8,128)S(1)} %collective-permute-done.4.up_margin_ref, ...), custom_call_target="tpu_custom_call" | custom-call | tf_op jit(solution)/shard_map/pallas_call | solution.py:527
  20.8 0.0 collective-permute-done.6.down_weight_ref
  20.8 1.8 %shard_map.72 = (f32[128,128]{1,0:T(8,128)S(1)}, f32[32,2,128]{2,1,0:T(2,128)S(1)}) custom-call(f32[12,32,128]{2,1,0:T(8,128)S(1)} %get-tuple-element.32.spectra_ref, f32[6,64,256]{2,1,0:T(8,128)S(1)} %get-tuple-element.33.fields_ref, f32[128,256]{1,0:T(8,128)S(1)} %get-tuple-element.34.tall_ref, f32[2,256,256]{2,1,0:T(8,128)S(1)} %get-tuple-element.35.cells_ref, ...), custom_call_target="tpu_custom_call" | custom-call | tf_op jit(solution)/shard_map/pallas_call | solution.py:539
  22.6 9.7 %all_to_all.10.sums_ref = f32[32,2,128]{2,1,0:T(2,128)S(1)} all-to-all(f32[32,2,128]{2,1,0:T(2,128)S(1)} %get-tuple-element.39), channel_id=1, replica_groups=mesh['row'=8,'col'=4] {'row','col'}, dimensions={0} | all-to-all | bytes 65536 | tf_op jit(solution)/shard_map/all_to_all | solution.py:447
  32.3 0.7 %shard_map.73 = (f32[128,128]{1,0:T(8,128)}, f32[1,1]{1,0:T(1,128)}) custom-call(f32[3,128,128]{2,1,0:T(8,128)S(1)} %get-tuple-element.22.own_ref, f32[128,128]{1,0:T(8,128)S(1)} %get-tuple-element.38.cells_ref, f32[32,2,128]{2,1,0:T(2,128)S(1)} %all_to_all.10.sums_ref), custom_call_target="tpu_custom_call" | custom-call | tf_op jit(solution)/shard_map/pallas_call | solution.py:549
Async XLA Ops:
  0.6 13.4 %copy-start = (bf16[2496,256]{1,0:T(8,128)(2,1)S(1)}, bf16[2496,256]{1,0:T(8,128)(2,1)}, u32[]{:S(2)}) copy-start(bf16[2496,256]{1,0:T(8,128)(2,1)} %constant.1.clone.table_ref) | copy-start | bytes 3833860
  2.4 9.0 %collective-permute-start = (f32[192,128]{1,0:T(8,128)S(1)}, f32[192,128]{1,0:T(8,128)S(1)}, u32[]{:S(2)}, u32[]{:S(2)}) collective-permute-start(f32[192,128]{1,0:T(8,128)S(1)} %get-tuple-element.24), channel_id=1, source_target_pairs={{0,1},{1,0},{2,3},{3,2},{4,5},{5,4},{6,7},{7,6},{8,9},{9,8},{10,11... | collective-permute-start | bytes 294920 | tf_op jit(solution)/shard_map/ppermute | solution.py:464
  5.4 6.0 %collective-permute-start.1 = (f32[192,128]{1,0:T(8,128)S(1)}, f32[192,128]{1,0:T(8,128)S(1)}, u32[]{:S(2)}, u32[]{:S(2)}) collective-permute-start(f32[192,128]{1,0:T(8,128)S(1)} %get-tuple-element.25), channel_id=1, source_target_pairs={{0,4},{1,2},{2,1},{3,7},{4,0},{5,6},{6,5},{7,3},{8,12},{9,10},{10,... | collective-permute-start | bytes 294920 | tf_op jit(solution)/shard_map/ppermute | solution.py:464
  5.4 6.0 %collective-permute-start.2 = (f32[3,64,128]{2,1,0:T(8,128)S(1)}, f32[3,64,128]{2,1,0:T(8,128)S(1)}, u32[]{:S(2)}, u32[]{:S(2)}) collective-permute-start(f32[3,64,128]{2,1,0:T(8,128)S(1)} %get-tuple-element.26), channel_id=1, source_target_pairs={{0,1},{1,0},{2,3},{3,2},{4,8},{5,9},{6,10},{7,11},{8,4},{9,5},{10,... | collective-permute-start | bytes 294920 | tf_op jit(solution)/shard_map/ppermute | solution.py:464
  8.5 10.8 %all-to-all-start = ((f32[32,2,384]{2,1,0:T(2,128)}), f32[32,2,384]{2,1,0:T(2,128)S(1)}, u32[]{:S(2)}, u32[]{:S(2)}) async-start(f32[32,2,384]{2,1,0:T(2,128)} %get-tuple-element.23), calls=%async_computation | async-start | bytes 196608 | tf_op jit(solution)/shard_map/all_to_all | solution.py:447
  11.1 2.9 %collective-permute-start.3 = (f32[3,64,128]{2,1,0:T(8,128)S(1)}, f32[3,64,128]{2,1,0:T(8,128)S(1)}, u32[]{:S(2)}, u32[]{:S(2)}) collective-permute-start(f32[3,64,128]{2,1,0:T(8,128)S(1)} %get-tuple-element.28), channel_id=1, source_target_pairs={{0,4},{1,5},{2,6},{3,7},{4,0},{5,1},{6,2},{7,3},{8,12},{9,13},{10,... | collective-permute-start | bytes 294920 | tf_op jit(solution)/shard_map/ppermute | solution.py:464
  11.6 7.7 %collective-permute-start.4 = (f32[3,64,128]{2,1,0:T(8,128)S(1)}, f32[3,64,128]{2,1,0:T(8,128)S(1)}, u32[]{:S(2)}, u32[]{:S(2)}) collective-permute-start(f32[3,64,128]{2,1,0:T(8,128)S(1)} %get-tuple-element.30), channel_id=1, source_target_pairs={{0,4},{1,5},{2,6},{3,7},{4,0},{5,1},{6,2},{7,3},{8,12},{9,13},{10,... | collective-permute-start | bytes 294920 | tf_op jit(solution)/shard_map/ppermute | solution.py:464
  11.9 4.8 %collective-permute-start.5 = (f32[2,64,128]{2,1,0:T(8,128)S(1)}, f32[2,64,128]{2,1,0:T(8,128)S(1)}, u32[]{:S(2)}, u32[]{:S(2)}) collective-permute-start(f32[2,64,128]{2,1,0:T(8,128)S(1)} %get-tuple-element.31), channel_id=1, source_target_pairs={{0,1},{1,0},{2,3},{3,2},{4,8},{5,9},{6,10},{7,11},{8,4},{9,5},{10,... | collective-permute-start | bytes 196616 | tf_op jit(solution)/shard_map/ppermute | solution.py:464
  13.7 7.1 %collective-permute-start.6 = (f32[64,128]{1,0:T(8,128)S(1)}, f32[64,128]{1,0:T(8,128)S(1)}, u32[]{:S(2)}, u32[]{:S(2)}) collective-permute-start(f32[64,128]{1,0:T(8,128)S(1)} %get-tuple-element.37), channel_id=1, source_target_pairs={{0,1},{1,0},{2,3},{3,2},{4,8},{5,9},{6,10},{7,11},{8,4},{9,5},{10,... | collective-permute-start | bytes 98312 | tf_op jit(solution)/shard_map/ppermute | solution.py:464

commit v8 on v7

--- a/solution.py
+++ b/solution.py
@@ -154,7 +154,7 @@
 
 
 def widen(
-    own_ref, a_ref, b_ref, _, centre_ref, up_ref, down_ref, down_weight_ref
+    own_ref, a_ref, b_ref, _, centre_ref, up_ref, first_ref, second_ref
 ):
     half = HALO
     odd = lax.rem(lax.axis_index("col"), 2) == 1
@@ -182,14 +182,17 @@
         centre_ref[index] = wide
         margins.append(jnp.where(low, wide[:, :LANES], wide[:, LANES:]))
     margins[0] = mask_of(margins[0], margins[2])
-    for margin, first_ref, second_ref in zip(
-        margins,
-        (up_ref.at[0], up_ref.at[1], up_ref.at[2]),
-        (down_ref.at[0], down_ref.at[1], down_weight_ref),
-        strict=True,
-    ):
-        first_ref[...] = jnp.where(odd_row, margin[:half], margin[half:])
-        second_ref[...] = jnp.where(odd_row, margin[half:], margin[:half])
+    ups, downs = [], []
+    for margin in margins:
+        ups.append(jnp.where(odd_row, margin[:half], margin[half:]))
+        downs.append(jnp.where(odd_row, margin[half:], margin[:half]))
+    for index, value in enumerate(ups):
+        up_ref[index] = value
+    middle = half // 2
+    first_ref[:half] = downs[0]
+    first_ref[half:] = downs[1][:middle]
+    second_ref[:middle] = downs[1][middle:]
+    second_ref[middle:] = downs[2]
 
 
 def beside(*blocks):
@@ -274,7 +277,7 @@
     bank_ref,
     spectrum_ref,
     up_margin_ref,
-    down_margin_ref,
+    first_ref,
     table_ref,
     spectra_ref,
     fields_ref,
@@ -286,7 +289,7 @@
     per = BAND // fold
     table = Tables(table_ref, place)
     low = lax.broadcasted_iota(jnp.int32, (1, LANES), 1) < LANES // 2
-    corner_mask = below(*above_below(up_margin_ref[0], down_margin_ref[0]))
+    corner_mask = below(*above_below(up_margin_ref[0], first_ref[:HALO]))
 
     for row, (device, piece) in enumerate(order):
         both = bank_ref[device, :, piece * LANES : (piece + 1) * LANES]
@@ -368,8 +371,8 @@
     cells_ref,
     factor_ref,
     up_margin_ref,
-    down_margin_ref,
-    down_weight_ref,
+    first_ref,
+    second_ref,
     table_ref,
     grad_ref,
     sums_ref,
@@ -382,7 +385,7 @@
 
     def filled(index):
         cells = cells_ref[index]
-        other = (down_margin_ref[1], down_weight_ref[...])[index]
+        other = (below(first_ref[HALO:], second_ref[: HALO // 2]), second_ref[HALO // 2 :])[index]
         corners = above_below(up_margin_ref[index + 1], other)
         ends = []
         for corner, rows in zip(corners, (cells[:HALO], cells[-HALO:]), strict=True):
@@ -494,17 +497,17 @@
     )(jnp.concatenate([cells, shard], axis=0))
     got_a, got_b = pair_swap(slab_a, "col", 0), pair_swap(slab_b, "col", 1)
     up, down = pair_swap(up, "row", 0), pair_swap(down, "row", 1)
-    margin = struct(2, HALO, core_width)
-    centre, up_margin, down_margin, down_weight = pl.pallas_call(
+    margin = struct(HALO * 3 // 2, core_width)
+    centre, up_margin, first_margin, second_margin = pl.pallas_call(
         widen,
-        out_shape=(struct(3, core_width, pad_width), slab, margin, struct(HALO, core_width)),
+        out_shape=(struct(3, core_width, pad_width), slab, margin, margin),
         in_specs=[VMEM] * 3 + [pl.BlockSpec(memory_space=pl.ANY)],
         out_specs=(VMEM,) * 4,
         compiler_params=small(8),
     )(own, got_a, got_b, down)
     up_margin = pair_swap(up_margin, "row", 0)
-    down_margin = pair_swap(down_margin, "row", 1)
-    down_weight = pair_swap(down_weight, "row", 1)
+    first_margin = pair_swap(first_margin, "row", 1)
+    second_margin = pair_swap(second_margin, "row", 1)
     consts, place = tables(pad_width, HALO)
     spectrum, cells, factor = pl.pallas_call(
         functools.partial(before_margins, place),
@@ -535,14 +538,14 @@
         out_specs=(VMEM,) * 3,
         scratch_shapes=[pltpu.VMEM((CONDITIONS, len(order), LANES), f32)],
         compiler_params=small(16),
-    )(bank, spectrum, up_margin, down_margin, consts)
+    )(bank, spectrum, up_margin, first_margin, consts)
     grad_cells, sums = pl.pallas_call(
         functools.partial(backward_kernel, place),
         out_shape=(struct(core_width, core_width), struct(rows * cols, 2, LANES)),
         in_specs=[VMEM] * 9,
         out_specs=(VMEM,) * 2,
         compiler_params=small(16),
-    )(spectra, fields, tall, cells, factor, up_margin, down_margin, down_weight, consts)
+    )(spectra, fields, tall, cells, factor, up_margin, first_margin, second_margin, consts)
 
     sums = to_all(sums)
     cell_count = rows * cols * core_width * core_width

time: 33.2 us -> 32.8 us (0.988)
  blocking collectives: 9.67 us -> 9.32 us
    all_to_all x1, blocking collectives: 9.67 us -> 9.32 us  [to_all(): return lax.all_to_all(value, ('row', 'col'), 0, 0)]
where the time goes in v8:
time: 32.8 us; the launch traced here: 32.6 us
  starting transfers between devices  11.4 us (35%)
  blocking collectives  9.32 us (28%)
  Pallas kernels  5.38 us (16%)
  waiting for transfers between devices  4.8 us (15%)
  other arithmetic  1.04 us (3%)
  between operations  0.67 us (2%)
    all_to_all x1, blocking collectives, to_all(): return lax.all_to_all(value, ('row', 'col'), 0, 0)  9.32 us
    ppermute x7, starting transfers between devices, pair_swap(): return lax.ppermute(value, ('row', 'col'), pairs)  8.84 us
    all_to_all x1, waiting for transfers between devices, to_all(): return lax.all_to_all(value, ('row', 'col'), 0, 0)  2.88 us
    all_to_all x1, starting transfers between devices, to_all(): return lax.all_to_all(value, ('row', 'col'), 0, 0)  2.55 us
    ppermute x7, waiting for transfers between devices, pair_swap(): return lax.ppermute(value, ('row', 'col'), pairs)  1.92 us
    pallas_call x1, Pallas kernels, shards(): pl.pallas_call(functools.partial(backward_kernel, place), out_shape=(stru...  1.79 us
    pallas_call x1, Pallas kernels, shards(): pl.pallas_call(functools.partial(forward_kernel, order, place), out_shape...  1.48 us
    concatenate x1, other arithmetic, shards(): jnp.concatenate([cells, shard], axis=0)  1.04 us
  transfers between devices with their start and end apart: 8, of which 2 were waited for; matrix products, arithmetic and copies ran while one was open for 0% of the time, Pallas kernels for 7%

profile of v8, /device:TPU:0, one launch (start us, length us, event | category | flops | bytes accessed | tf_op | source)
XLA Modules:
  0.0 32.6 jit_solution(5702263665988998874)
XLA Ops:
  0.6 0.0 copy-start
  0.6 1.0 %pad_maximum_fusion.held_ref = f32[130,384]{1,0:T(8,128)S(1)} fusion(f32[2,384]{1,0:T(2,128)} %param.8, f32[128,128]{1,0:T(8,128)} %param.7, f32[128,128]{1,0:T(8,128)} %param.6, f32[128,128]{1,0:T(8,128)} %param.5), kind=kLoop, calls=%fused_computation | loop fusion | flops 149760 | bytes 399360 | tf_op jit(solution)/shard_map/concatenate | solution.py:497
  1.7 0.7 %shard_map.68 = (f32[3,128,128]{2,1,0:T(8,128)S(1)}, f32[192,128]{1,0:T(8,128)S(1)}, f32[192,128]{1,0:T(8,128)S(1)}, f32[3,64,128]{2,1,0:T(8,128)S(1)}, f32[3,64...) custom-call(f32[130,384]{1,0:T(8,128)S(1)} %pad_maximum_fusion.held_ref), custom_call_target="tpu_custom_call" | custom-call | tf_op jit(solution)/shard_map/pallas_call | solution.py:490
  2.4 3.0 %collective-permute-start = (f32[192,128]{1,0:T(8,128)S(1)}, f32[192,128]{1,0:T(8,128)S(1)}, u32[]{:S(2)}, u32[]{:S(2)}) collective-permute-start(f32[192,128]{1,0:T(8,128)S(1)} %get-tuple-element.24), channel_id=1, source_target_pairs={{0,1},{1,0},{2,3},{3,2},{4,5},{5,4},{6,7},{7,6},{8,9},{9,8},{10,11... | collective-permute-start | bytes 294920 | tf_op jit(solution)/shard_map/ppermute | solution.py:467
  5.4 0.0 collective-permute-start.1
  5.4 3.1 %collective-permute-start.2 = (f32[3,64,128]{2,1,0:T(8,128)S(1)}, f32[3,64,128]{2,1,0:T(8,128)S(1)}, u32[]{:S(2)}, u32[]{:S(2)}) collective-permute-start(f32[3,64,128]{2,1,0:T(8,128)S(1)} %get-tuple-element.26), channel_id=1, source_target_pairs={{0,1},{1,0},{2,3},{3,2},{4,8},{5,9},{6,10},{7,11},{8,4},{9,5},{10,... | collective-permute-start | bytes 294920 | tf_op jit(solution)/shard_map/ppermute | solution.py:467
  8.5 2.6 %all-to-all-start = ((f32[32,2,384]{2,1,0:T(2,128)}), f32[32,2,384]{2,1,0:T(2,128)S(1)}, u32[]{:S(2)}, u32[]{:S(2)}) async-start(f32[32,2,384]{2,1,0:T(2,128)} %get-tuple-element.23), calls=%async_computation | async-start | bytes 196608 | tf_op jit(solution)/shard_map/all_to_all | solution.py:450
  11.1 0.3 collective-permute-start.3
  11.4 0.0 collective-permute-done.a_ref
  11.4 0.0 collective-permute-done.1.b_ref
  11.4 0.0 collective-permute-done.2._.down_ref
  11.4 0.2 shard_map.69
  11.6 0.3 %collective-permute-start.4 = (f32[3,64,128]{2,1,0:T(8,128)S(1)}, f32[3,64,128]{2,1,0:T(8,128)S(1)}, u32[]{:S(2)}, u32[]{:S(2)}) collective-permute-start(f32[3,64,128]{2,1,0:T(8,128)S(1)} %get-tuple-element.30), channel_id=1, source_target_pairs={{0,4},{1,5},{2,6},{3,7},{4,0},{5,1},{6,2},{7,3},{8,12},{9,13},{10,... | collective-permute-start | bytes 294920 | tf_op jit(solution)/shard_map/ppermute | solution.py:467
  11.9 1.8 %collective-permute-start.5 = (f32[96,128]{1,0:T(8,128)S(1)}, f32[96,128]{1,0:T(8,128)S(1)}, u32[]{:S(2)}, u32[]{:S(2)}) collective-permute-start(f32[96,128]{1,0:T(8,128)S(1)} %get-tuple-element.31), channel_id=1, source_target_pairs={{0,1},{1,0},{2,3},{3,2},{4,8},{5,9},{6,10},{7,11},{8,4},{9,5},{10,... | collective-permute-start | bytes 147464 | tf_op jit(solution)/shard_map/ppermute | solution.py:467
  13.7 0.3 collective-permute-start.6
  14.0 0.0 collective-permute-done.3.up_ref
  14.0 0.0 copy-done
  14.0 0.6 %shard_map.70 = (f32[32,128]{1,0:T(8,128)S(1)}, f32[2,256,256]{2,1,0:T(8,128)S(1)}, f32[128,128]{1,0:T(8,128)S(1)}) custom-call(f32[3,128,256]{2,1,0:T(8,128)S(1)} %get-tuple-element.27.centre_ref, f32[3,64,128]{2,1,0:T(8,128)S(1)} %collective-permute-done.3.up_ref, f32[3,64,128]{2,1,0:T(8,128)S(1)} %collective-permute-done.2._.down_ref, ...), custom_call_target="tpu_custom_call" | custom-call | tf_op jit(solution)/shard_map/pallas_call | solution.py:512
  14.5 1.9 %collective-permute-done.5.first_ref = f32[96,128]{1,0:T(8,128)S(1)} collective-permute-done((f32[96,128]{1,0:T(8,128)S(1)}, f32[96,128]{1,0:T(8,128)S(1)}, u32[]{:S(2)}, u32[]{:S(2)}) %collective-permute-start.5) | collective-permute-done | bytes 49184 | tf_op jit(solution)/shard_map/ppermute | solution.py:467
  16.4 2.9 %all-to-all-done.bank_ref = f32[32,2,384]{2,1,0:T(2,128)S(1)} async-done(((f32[32,2,384]{2,1,0:T(2,128)}), f32[32,2,384]{2,1,0:T(2,128)S(1)}, u32[]{:S(2)}, u32[]{:S(2)}) %all-to-all-start) | async-done | bytes 98336 | tf_op jit(solution)/shard_map/all_to_all | solution.py:450
  19.3 0.0 collective-permute-done.4.up_margin_ref
  19.3 1.5 %shard_map.71 = (f32[12,32,128]{2,1,0:T(8,128)S(1)}, f32[6,64,256]{2,1,0:T(8,128)S(1)}, f32[128,256]{1,0:T(8,128)S(1)}) custom-call(f32[32,2,384]{2,1,0:T(2,128)S(1)} %all-to-all-done.bank_ref, f32[32,128]{1,0:T(8,128)S(1)} %get-tuple-element.29.spectrum_ref, f32[3,64,128]{2,1,0:T(8,128)S(1)} %collective-permute-done.4.up_margin_ref, ...), custom_call_target="tpu_custom_call" | custom-call | tf_op jit(solution)/shard_map/pallas_call | solution.py:530
  20.8 0.0 collective-permute-done.6.second_ref
  20.8 1.8 %shard_map.72 = (f32[128,128]{1,0:T(8,128)S(1)}, f32[32,2,128]{2,1,0:T(2,128)S(1)}) custom-call(f32[12,32,128]{2,1,0:T(8,128)S(1)} %get-tuple-element.32.spectra_ref, f32[6,64,256]{2,1,0:T(8,128)S(1)} %get-tuple-element.33.fields_ref, f32[128,256]{1,0:T(8,128)S(1)} %get-tuple-element.34.tall_ref, f32[2,256,256]{2,1,0:T(8,128)S(1)} %get-tuple-element.35.cells_ref, ...), custom_call_target="tpu_custom_call" | custom-call | tf_op jit(solution)/shard_map/pallas_call | solution.py:542
  22.6 9.3 %all_to_all.10.sums_ref = f32[32,2,128]{2,1,0:T(2,128)S(1)} all-to-all(f32[32,2,128]{2,1,0:T(2,128)S(1)} %get-tuple-element.39), channel_id=1, replica_groups=mesh['row'=8,'col'=4] {'row','col'}, dimensions={0} | all-to-all | bytes 65536 | tf_op jit(solution)/shard_map/all_to_all | solution.py:450
  31.9 0.7 %shard_map.73 = (f32[128,128]{1,0:T(8,128)}, f32[1,1]{1,0:T(1,128)}) custom-call(f32[3,128,128]{2,1,0:T(8,128)S(1)} %get-tuple-element.22.own_ref, f32[128,128]{1,0:T(8,128)S(1)} %get-tuple-element.38.cells_ref, f32[32,2,128]{2,1,0:T(2,128)S(1)} %all_to_all.10.sums_ref), custom_call_target="tpu_custom_call" | custom-call | tf_op jit(solution)/shard_map/pallas_call | solution.py:552
Async XLA Ops:
  0.6 13.4 %copy-start = (bf16[2496,256]{1,0:T(8,128)(2,1)S(1)}, bf16[2496,256]{1,0:T(8,128)(2,1)}, u32[]{:S(2)}) copy-start(bf16[2496,256]{1,0:T(8,128)(2,1)} %constant.1.clone.table_ref) | copy-start | bytes 3833860
  2.4 9.0 %collective-permute-start = (f32[192,128]{1,0:T(8,128)S(1)}, f32[192,128]{1,0:T(8,128)S(1)}, u32[]{:S(2)}, u32[]{:S(2)}) collective-permute-start(f32[192,128]{1,0:T(8,128)S(1)} %get-tuple-element.24), channel_id=1, source_target_pairs={{0,1},{1,0},{2,3},{3,2},{4,5},{5,4},{6,7},{7,6},{8,9},{9,8},{10,11... | collective-permute-start | bytes 294920 | tf_op jit(solution)/shard_map/ppermute | solution.py:467
  5.4 6.0 %collective-permute-start.1 = (f32[192,128]{1,0:T(8,128)S(1)}, f32[192,128]{1,0:T(8,128)S(1)}, u32[]{:S(2)}, u32[]{:S(2)}) collective-permute-start(f32[192,128]{1,0:T(8,128)S(1)} %get-tuple-element.25), channel_id=1, source_target_pairs={{0,4},{1,2},{2,1},{3,7},{4,0},{5,6},{6,5},{7,3},{8,12},{9,10},{10,... | collective-permute-start | bytes 294920 | tf_op jit(solution)/shard_map/ppermute | solution.py:467
  5.4 6.0 %collective-permute-start.2 = (f32[3,64,128]{2,1,0:T(8,128)S(1)}, f32[3,64,128]{2,1,0:T(8,128)S(1)}, u32[]{:S(2)}, u32[]{:S(2)}) collective-permute-start(f32[3,64,128]{2,1,0:T(8,128)S(1)} %get-tuple-element.26), channel_id=1, source_target_pairs={{0,1},{1,0},{2,3},{3,2},{4,8},{5,9},{6,10},{7,11},{8,4},{9,5},{10,... | collective-permute-start | bytes 294920 | tf_op jit(solution)/shard_map/ppermute | solution.py:467
  8.5 10.8 %all-to-all-start = ((f32[32,2,384]{2,1,0:T(2,128)}), f32[32,2,384]{2,1,0:T(2,128)S(1)}, u32[]{:S(2)}, u32[]{:S(2)}) async-start(f32[32,2,384]{2,1,0:T(2,128)} %get-tuple-element.23), calls=%async_computation | async-start | bytes 196608 | tf_op jit(solution)/shard_map/all_to_all | solution.py:450
  11.1 2.9 %collective-permute-start.3 = (f32[3,64,128]{2,1,0:T(8,128)S(1)}, f32[3,64,128]{2,1,0:T(8,128)S(1)}, u32[]{:S(2)}, u32[]{:S(2)}) collective-permute-start(f32[3,64,128]{2,1,0:T(8,128)S(1)} %get-tuple-element.28), channel_id=1, source_target_pairs={{0,4},{1,5},{2,6},{3,7},{4,0},{5,1},{6,2},{7,3},{8,12},{9,13},{10,... | collective-permute-start | bytes 294920 | tf_op jit(solution)/shard_map/ppermute | solution.py:467
  11.6 7.7 %collective-permute-start.4 = (f32[3,64,128]{2,1,0:T(8,128)S(1)}, f32[3,64,128]{2,1,0:T(8,128)S(1)}, u32[]{:S(2)}, u32[]{:S(2)}) collective-permute-start(f32[3,64,128]{2,1,0:T(8,128)S(1)} %get-tuple-element.30), channel_id=1, source_target_pairs={{0,4},{1,5},{2,6},{3,7},{4,0},{5,1},{6,2},{7,3},{8,12},{9,13},{10,... | collective-permute-start | bytes 294920 | tf_op jit(solution)/shard_map/ppermute | solution.py:467
  11.9 4.5 %collective-permute-start.5 = (f32[96,128]{1,0:T(8,128)S(1)}, f32[96,128]{1,0:T(8,128)S(1)}, u32[]{:S(2)}, u32[]{:S(2)}) collective-permute-start(f32[96,128]{1,0:T(8,128)S(1)} %get-tuple-element.31), channel_id=1, source_target_pairs={{0,1},{1,0},{2,3},{3,2},{4,8},{5,9},{6,10},{7,11},{8,4},{9,5},{10,... | collective-permute-start | bytes 147464 | tf_op jit(solution)/shard_map/ppermute | solution.py:467
  13.7 7.1 %collective-permute-start.6 = (f32[96,128]{1,0:T(8,128)S(1)}, f32[96,128]{1,0:T(8,128)S(1)}, u32[]{:S(2)}, u32[]{:S(2)}) collective-permute-start(f32[96,128]{1,0:T(8,128)S(1)} %get-tuple-element.37), channel_id=1, source_target_pairs={{0,1},{1,0},{2,3},{3,2},{4,8},{5,9},{6,10},{7,11},{8,4},{9,5},{10,... | collective-permute-start | bytes 147464 | tf_op jit(solution)/shard_map/ppermute | solution.py:467

commit v9 on v8

--- a/solution.py
+++ b/solution.py
@@ -153,9 +153,7 @@
     b_ref[rows:] = jnp.where(odd, to_right[1], to_left[1])
 
 
-def widen(
-    own_ref, a_ref, b_ref, _, centre_ref, up_ref, first_ref, second_ref
-):
+def widen(own_ref, a_ref, b_ref, _, centre_ref, up_ref, first_ref, second_ref):
     half = HALO
     odd = lax.rem(lax.axis_index("col"), 2) == 1
     odd_row = lax.rem(lax.axis_index("row"), 2) == 1
@@ -486,7 +484,8 @@
     packed = struct(core_width * 3 // 2, core_width)
     slab = struct(3, HALO, core_width)
     cells = jnp.concatenate([mask_logits, target, weight], axis=1)
-    shard = jnp.pad(kernels, ((0, 0), (0, cells.shape[1] - kernels.shape[1])))
+    width = max(cells.shape[1], kernels.shape[1])
+    cells, shard = [jnp.pad(a, ((0, 0), (0, width - a.shape[1]))) for a in (cells, kernels)]
     own, slab_a, slab_b, up, down, bank = pl.pallas_call(
         pack,
         out_shape=(struct(3, core_width, core_width), packed, packed, slab, slab)

time: 32.8 us -> 32.8 us (level)
  no operation moved by 1% of the time
where the time goes in v9:
time: 32.8 us; the launch traced here: 32.6 us
  starting transfers between devices  11.4 us (35%)
  blocking collectives  9.32 us (28%)
  Pallas kernels  5.38 us (16%)
  waiting for transfers between devices  4.8 us (15%)
  other arithmetic  1.04 us (3%)
  between operations  0.67 us (2%)
    all_to_all x1, blocking collectives, to_all(): return lax.all_to_all(value, ('row', 'col'), 0, 0)  9.32 us
    ppermute x7, starting transfers between devices, pair_swap(): return lax.ppermute(value, ('row', 'col'), pairs)  8.84 us
    all_to_all x1, waiting for transfers between devices, to_all(): return lax.all_to_all(value, ('row', 'col'), 0, 0)  2.88 us
    all_to_all x1, starting transfers between devices, to_all(): return lax.all_to_all(value, ('row', 'col'), 0, 0)  2.55 us
    ppermute x7, waiting for transfers between devices, pair_swap(): return lax.ppermute(value, ('row', 'col'), pairs)  1.92 us
    pallas_call x1, Pallas kernels, shards(): pl.pallas_call(functools.partial(backward_kernel, place), out_shape=(stru...  1.79 us
    pallas_call x1, Pallas kernels, shards(): pl.pallas_call(functools.partial(forward_kernel, order, place), out_shape...  1.48 us
    concatenate x1, other arithmetic, shards(): jnp.concatenate([cells, shard], axis=0)  1.04 us
  transfers between devices with their start and end apart: 8, of which 2 were waited for; matrix products, arithmetic and copies ran while one was open for 0% of the time, Pallas kernels for 7%

profile of v9, /device:TPU:0, one launch (start us, length us, event | category | flops | bytes accessed | tf_op | source)
XLA Modules:
  0.0 32.6 jit_solution(5702263665988998874)
XLA Ops:
  0.6 0.0 copy-start
  0.6 1.0 %pad_maximum_fusion.held_ref = f32[130,384]{1,0:T(8,128)S(1)} fusion(f32[2,384]{1,0:T(2,128)} %param.8, f32[128,128]{1,0:T(8,128)} %param.7, f32[128,128]{1,0:T(8,128)} %param.6, f32[128,128]{1,0:T(8,128)} %param.5), kind=kLoop, calls=%fused_computation | loop fusion | flops 149760 | bytes 399360 | tf_op jit(solution)/shard_map/concatenate | solution.py:496
  1.7 0.7 %shard_map.68 = (f32[3,128,128]{2,1,0:T(8,128)S(1)}, f32[192,128]{1,0:T(8,128)S(1)}, f32[192,128]{1,0:T(8,128)S(1)}, f32[3,64,128]{2,1,0:T(8,128)S(1)}, f32[3,64...) custom-call(f32[130,384]{1,0:T(8,128)S(1)} %pad_maximum_fusion.held_ref), custom_call_target="tpu_custom_call" | custom-call | tf_op jit(solution)/shard_map/pallas_call | solution.py:489
  2.4 3.0 %collective-permute-start = (f32[192,128]{1,0:T(8,128)S(1)}, f32[192,128]{1,0:T(8,128)S(1)}, u32[]{:S(2)}, u32[]{:S(2)}) collective-permute-start(f32[192,128]{1,0:T(8,128)S(1)} %get-tuple-element.24), channel_id=1, source_target_pairs={{0,1},{1,0},{2,3},{3,2},{4,5},{5,4},{6,7},{7,6},{8,9},{9,8},{10,11... | collective-permute-start | bytes 294920 | tf_op jit(solution)/shard_map/ppermute | solution.py:465
  5.4 0.0 collective-permute-start.1
  5.4 3.1 %collective-permute-start.2 = (f32[3,64,128]{2,1,0:T(8,128)S(1)}, f32[3,64,128]{2,1,0:T(8,128)S(1)}, u32[]{:S(2)}, u32[]{:S(2)}) collective-permute-start(f32[3,64,128]{2,1,0:T(8,128)S(1)} %get-tuple-element.26), channel_id=1, source_target_pairs={{0,1},{1,0},{2,3},{3,2},{4,8},{5,9},{6,10},{7,11},{8,4},{9,5},{10,... | collective-permute-start | bytes 294920 | tf_op jit(solution)/shard_map/ppermute | solution.py:465
  8.5 2.6 %all-to-all-start = ((f32[32,2,384]{2,1,0:T(2,128)}), f32[32,2,384]{2,1,0:T(2,128)S(1)}, u32[]{:S(2)}, u32[]{:S(2)}) async-start(f32[32,2,384]{2,1,0:T(2,128)} %get-tuple-element.23), calls=%async_computation | async-start | bytes 196608 | tf_op jit(solution)/shard_map/all_to_all | solution.py:448
  11.1 0.3 collective-permute-start.3
  11.4 0.0 collective-permute-done.a_ref
  11.4 0.0 collective-permute-done.1.b_ref
  11.4 0.0 collective-permute-done.2._.down_ref
  11.4 0.2 shard_map.69
  11.6 0.3 %collective-permute-start.4 = (f32[3,64,128]{2,1,0:T(8,128)S(1)}, f32[3,64,128]{2,1,0:T(8,128)S(1)}, u32[]{:S(2)}, u32[]{:S(2)}) collective-permute-start(f32[3,64,128]{2,1,0:T(8,128)S(1)} %get-tuple-element.30), channel_id=1, source_target_pairs={{0,4},{1,5},{2,6},{3,7},{4,0},{5,1},{6,2},{7,3},{8,12},{9,13},{10,... | collective-permute-start | bytes 294920 | tf_op jit(solution)/shard_map/ppermute | solution.py:465
  11.9 1.8 %collective-permute-start.5 = (f32[96,128]{1,0:T(8,128)S(1)}, f32[96,128]{1,0:T(8,128)S(1)}, u32[]{:S(2)}, u32[]{:S(2)}) collective-permute-start(f32[96,128]{1,0:T(8,128)S(1)} %get-tuple-element.31), channel_id=1, source_target_pairs={{0,1},{1,0},{2,3},{3,2},{4,8},{5,9},{6,10},{7,11},{8,4},{9,5},{10,... | collective-permute-start | bytes 147464 | tf_op jit(solution)/shard_map/ppermute | solution.py:465
  13.7 0.3 collective-permute-start.6
  14.0 0.0 collective-permute-done.3.up_ref
  14.0 0.0 copy-done
  14.0 0.6 %shard_map.70 = (f32[32,128]{1,0:T(8,128)S(1)}, f32[2,256,256]{2,1,0:T(8,128)S(1)}, f32[128,128]{1,0:T(8,128)S(1)}) custom-call(f32[3,128,256]{2,1,0:T(8,128)S(1)} %get-tuple-element.27.centre_ref, f32[3,64,128]{2,1,0:T(8,128)S(1)} %collective-permute-done.3.up_ref, f32[3,64,128]{2,1,0:T(8,128)S(1)} %collective-permute-done.2._.down_ref, ...), custom_call_target="tpu_custom_call" | custom-call | tf_op jit(solution)/shard_map/pallas_call | solution.py:511
  14.5 1.9 %collective-permute-done.5.first_ref = f32[96,128]{1,0:T(8,128)S(1)} collective-permute-done((f32[96,128]{1,0:T(8,128)S(1)}, f32[96,128]{1,0:T(8,128)S(1)}, u32[]{:S(2)}, u32[]{:S(2)}) %collective-permute-start.5) | collective-permute-done | bytes 49184 | tf_op jit(solution)/shard_map/ppermute | solution.py:465
  16.4 2.9 %all-to-all-done.bank_ref = f32[32,2,384]{2,1,0:T(2,128)S(1)} async-done(((f32[32,2,384]{2,1,0:T(2,128)}), f32[32,2,384]{2,1,0:T(2,128)S(1)}, u32[]{:S(2)}, u32[]{:S(2)}) %all-to-all-start) | async-done | bytes 98336 | tf_op jit(solution)/shard_map/all_to_all | solution.py:448
  19.3 0.0 collective-permute-done.4.up_margin_ref
  19.3 1.5 %shard_map.71 = (f32[12,32,128]{2,1,0:T(8,128)S(1)}, f32[6,64,256]{2,1,0:T(8,128)S(1)}, f32[128,256]{1,0:T(8,128)S(1)}) custom-call(f32[32,2,384]{2,1,0:T(2,128)S(1)} %all-to-all-done.bank_ref, f32[32,128]{1,0:T(8,128)S(1)} %get-tuple-element.29.spectrum_ref, f32[3,64,128]{2,1,0:T(8,128)S(1)} %collective-permute-done.4.up_margin_ref, ...), custom_call_target="tpu_custom_call" | custom-call | tf_op jit(solution)/shard_map/pallas_call | solution.py:529
  20.8 0.0 collective-permute-done.6.second_ref
  20.8 1.8 %shard_map.72 = (f32[128,128]{1,0:T(8,128)S(1)}, f32[32,2,128]{2,1,0:T(2,128)S(1)}) custom-call(f32[12,32,128]{2,1,0:T(8,128)S(1)} %get-tuple-element.32.spectra_ref, f32[6,64,256]{2,1,0:T(8,128)S(1)} %get-tuple-element.33.fields_ref, f32[128,256]{1,0:T(8,128)S(1)} %get-tuple-element.34.tall_ref, f32[2,256,256]{2,1,0:T(8,128)S(1)} %get-tuple-element.35.cells_ref, ...), custom_call_target="tpu_custom_call" | custom-call | tf_op jit(solution)/shard_map/pallas_call | solution.py:541
  22.6 9.3 %all_to_all.10.sums_ref = f32[32,2,128]{2,1,0:T(2,128)S(1)} all-to-all(f32[32,2,128]{2,1,0:T(2,128)S(1)} %get-tuple-element.39), channel_id=1, replica_groups=mesh['row'=8,'col'=4] {'row','col'}, dimensions={0} | all-to-all | bytes 65536 | tf_op jit(solution)/shard_map/all_to_all | solution.py:448
  31.9 0.7 %shard_map.73 = (f32[128,128]{1,0:T(8,128)}, f32[1,1]{1,0:T(1,128)}) custom-call(f32[3,128,128]{2,1,0:T(8,128)S(1)} %get-tuple-element.22.own_ref, f32[128,128]{1,0:T(8,128)S(1)} %get-tuple-element.38.cells_ref, f32[32,2,128]{2,1,0:T(2,128)S(1)} %all_to_all.10.sums_ref), custom_call_target="tpu_custom_call" | custom-call | tf_op jit(solution)/shard_map/pallas_call | solution.py:551
Async XLA Ops:
  0.6 13.4 %copy-start = (bf16[2496,256]{1,0:T(8,128)(2,1)S(1)}, bf16[2496,256]{1,0:T(8,128)(2,1)}, u32[]{:S(2)}) copy-start(bf16[2496,256]{1,0:T(8,128)(2,1)} %constant.1.clone.table_ref) | copy-start | bytes 3833860
  2.4 9.0 %collective-permute-start = (f32[192,128]{1,0:T(8,128)S(1)}, f32[192,128]{1,0:T(8,128)S(1)}, u32[]{:S(2)}, u32[]{:S(2)}) collective-permute-start(f32[192,128]{1,0:T(8,128)S(1)} %get-tuple-element.24), channel_id=1, source_target_pairs={{0,1},{1,0},{2,3},{3,2},{4,5},{5,4},{6,7},{7,6},{8,9},{9,8},{10,11... | collective-permute-start | bytes 294920 | tf_op jit(solution)/shard_map/ppermute | solution.py:465
  5.4 6.0 %collective-permute-start.1 = (f32[192,128]{1,0:T(8,128)S(1)}, f32[192,128]{1,0:T(8,128)S(1)}, u32[]{:S(2)}, u32[]{:S(2)}) collective-permute-start(f32[192,128]{1,0:T(8,128)S(1)} %get-tuple-element.25), channel_id=1, source_target_pairs={{0,4},{1,2},{2,1},{3,7},{4,0},{5,6},{6,5},{7,3},{8,12},{9,10},{10,... | collective-permute-start | bytes 294920 | tf_op jit(solution)/shard_map/ppermute | solution.py:465
  5.4 6.0 %collective-permute-start.2 = (f32[3,64,128]{2,1,0:T(8,128)S(1)}, f32[3,64,128]{2,1,0:T(8,128)S(1)}, u32[]{:S(2)}, u32[]{:S(2)}) collective-permute-start(f32[3,64,128]{2,1,0:T(8,128)S(1)} %get-tuple-element.26), channel_id=1, source_target_pairs={{0,1},{1,0},{2,3},{3,2},{4,8},{5,9},{6,10},{7,11},{8,4},{9,5},{10,... | collective-permute-start | bytes 294920 | tf_op jit(solution)/shard_map/ppermute | solution.py:465
  8.5 10.8 %all-to-all-start = ((f32[32,2,384]{2,1,0:T(2,128)}), f32[32,2,384]{2,1,0:T(2,128)S(1)}, u32[]{:S(2)}, u32[]{:S(2)}) async-start(f32[32,2,384]{2,1,0:T(2,128)} %get-tuple-element.23), calls=%async_computation | async-start | bytes 196608 | tf_op jit(solution)/shard_map/all_to_all | solution.py:448
  11.1 2.9 %collective-permute-start.3 = (f32[3,64,128]{2,1,0:T(8,128)S(1)}, f32[3,64,128]{2,1,0:T(8,128)S(1)}, u32[]{:S(2)}, u32[]{:S(2)}) collective-permute-start(f32[3,64,128]{2,1,0:T(8,128)S(1)} %get-tuple-element.28), channel_id=1, source_target_pairs={{0,4},{1,5},{2,6},{3,7},{4,0},{5,1},{6,2},{7,3},{8,12},{9,13},{10,... | collective-permute-start | bytes 294920 | tf_op jit(solution)/shard_map/ppermute | solution.py:465
  11.6 7.7 %collective-permute-start.4 = (f32[3,64,128]{2,1,0:T(8,128)S(1)}, f32[3,64,128]{2,1,0:T(8,128)S(1)}, u32[]{:S(2)}, u32[]{:S(2)}) collective-permute-start(f32[3,64,128]{2,1,0:T(8,128)S(1)} %get-tuple-element.30), channel_id=1, source_target_pairs={{0,4},{1,5},{2,6},{3,7},{4,0},{5,1},{6,2},{7,3},{8,12},{9,13},{10,... | collective-permute-start | bytes 294920 | tf_op jit(solution)/shard_map/ppermute | solution.py:465
  11.9 4.5 %collective-permute-start.5 = (f32[96,128]{1,0:T(8,128)S(1)}, f32[96,128]{1,0:T(8,128)S(1)}, u32[]{:S(2)}, u32[]{:S(2)}) collective-permute-start(f32[96,128]{1,0:T(8,128)S(1)} %get-tuple-element.31), channel_id=1, source_target_pairs={{0,1},{1,0},{2,3},{3,2},{4,8},{5,9},{6,10},{7,11},{8,4},{9,5},{10,... | collective-permute-start | bytes 147464 | tf_op jit(solution)/shard_map/ppermute | solution.py:465
  13.7 7.1 %collective-permute-start.6 = (f32[96,128]{1,0:T(8,128)S(1)}, f32[96,128]{1,0:T(8,128)S(1)}, u32[]{:S(2)}, u32[]{:S(2)}) collective-permute-start(f32[96,128]{1,0:T(8,128)S(1)} %get-tuple-element.37), channel_id=1, source_target_pairs={{0,1},{1,0},{2,3},{3,2},{4,8},{5,9},{6,10},{7,11},{8,4},{9,5},{10,... | collective-permute-start | bytes 147464 | tf_op jit(solution)/shard_map/ppermute | solution.py:465

commit v10 on v9

--- a/solution.py
+++ b/solution.py
@@ -405,13 +405,14 @@
         scaled = weight * error
         loss = loss + (scaled * error)[core, core]
         slopes.append((2.0 * SHARPNESS * dose) * scaled * (resist * (1.0 - resist)))
-    h, l = split(below(*slopes), 2)
+    h, l = split(beside(*slopes), 2)
+    both = dot(table("down_rows"), h)
+    narrow = both[:grid] + (both[grid:] + dot(table("down_rows", 0, grid), l))
+    narrow = below(*[narrow[:, c * pad_width : (c + 1) * pad_width] for c in range(CONDITIONS)])
+    h, l = split(narrow, 2)
     both = dot(h, table("down_cols"))
-    narrow = both[:, :LANES] + (both[:, LANES:] + dot(l, table("down_cols")[:, :LANES]))
-    narrow = beside(*[narrow[c * pad_width : (c + 1) * pad_width] for c in range(CONDITIONS)])
-    h, l = split(narrow, 2)
-    both = dot(table("down_rows"), h)
-    coarse = both[:grid] + (both[grid:] + dot(table("down_rows", 0, grid), l))
+    coarse = both[:, :LANES] + (both[:, LANES:] + dot(l, table("down_cols")[:, :LANES]))
+    coarse = beside(*[coarse[c * grid : (c + 1) * grid] for c in range(CONDITIONS)])
 
     backs = [[], []]
     for field in fields:

time: 32.8 us -> 32.8 us (level)
  no operation moved by 1% of the time
where the time goes in v10:
time: 32.8 us; the launch traced here: 32.6 us
  starting transfers between devices  11.4 us (35%)
  blocking collectives  9.32 us (28%)
  Pallas kernels  5.37 us (16%)
  waiting for transfers between devices  4.8 us (15%)
  other arithmetic  1.04 us (3%)
  between operations  0.67 us (2%)
    all_to_all x1, blocking collectives, to_all(): return lax.all_to_all(value, ('row', 'col'), 0, 0)  9.32 us
    ppermute x7, starting transfers between devices, pair_swap(): return lax.ppermute(value, ('row', 'col'), pairs)  8.84 us
    all_to_all x1, waiting for transfers between devices, to_all(): return lax.all_to_all(value, ('row', 'col'), 0, 0)  2.88 us
    all_to_all x1, starting transfers between devices, to_all(): return lax.all_to_all(value, ('row', 'col'), 0, 0)  2.55 us
    ppermute x7, waiting for transfers between devices, pair_swap(): return lax.ppermute(value, ('row', 'col'), pairs)  1.92 us
    pallas_call x1, Pallas kernels, shards(): pl.pallas_call(functools.partial(backward_kernel, place), out_shape=(stru...  1.77 us
    pallas_call x1, Pallas kernels, shards(): pl.pallas_call(functools.partial(forward_kernel, order, place), out_shape...  1.48 us
    concatenate x1, other arithmetic, shards(): jnp.concatenate([cells, shard], axis=0)  1.04 us
  transfers between devices with their start and end apart: 8, of which 2 were waited for; matrix products, arithmetic and copies ran while one was open for 0% of the time, Pallas kernels for 7%

profile of v10, /device:TPU:0, one launch (start us, length us, event | category | flops | bytes accessed | tf_op | source)
XLA Modules:
  0.0 32.6 jit_solution(7950718149522788337)
XLA Ops:
  0.6 0.0 copy-start
  0.6 1.0 %pad_maximum_fusion.held_ref = f32[130,384]{1,0:T(8,128)S(1)} fusion(f32[2,384]{1,0:T(2,128)} %param.8, f32[128,128]{1,0:T(8,128)} %param.7, f32[128,128]{1,0:T(8,128)} %param.6, f32[128,128]{1,0:T(8,128)} %param.5), kind=kLoop, calls=%fused_computation | loop fusion | flops 149760 | bytes 399360 | tf_op jit(solution)/shard_map/concatenate | solution.py:497
  1.7 0.7 %shard_map.68 = (f32[3,128,128]{2,1,0:T(8,128)S(1)}, f32[192,128]{1,0:T(8,128)S(1)}, f32[192,128]{1,0:T(8,128)S(1)}, f32[3,64,128]{2,1,0:T(8,128)S(1)}, f32[3,64...) custom-call(f32[130,384]{1,0:T(8,128)S(1)} %pad_maximum_fusion.held_ref), custom_call_target="tpu_custom_call" | custom-call | tf_op jit(solution)/shard_map/pallas_call | solution.py:490
  2.4 3.0 %collective-permute-start = (f32[192,128]{1,0:T(8,128)S(1)}, f32[192,128]{1,0:T(8,128)S(1)}, u32[]{:S(2)}, u32[]{:S(2)}) collective-permute-start(f32[192,128]{1,0:T(8,128)S(1)} %get-tuple-element.24), channel_id=1, source_target_pairs={{0,1},{1,0},{2,3},{3,2},{4,5},{5,4},{6,7},{7,6},{8,9},{9,8},{10,11... | collective-permute-start | bytes 294920 | tf_op jit(solution)/shard_map/ppermute | solution.py:466
  5.4 0.0 collective-permute-start.1
  5.4 3.1 %collective-permute-start.2 = (f32[3,64,128]{2,1,0:T(8,128)S(1)}, f32[3,64,128]{2,1,0:T(8,128)S(1)}, u32[]{:S(2)}, u32[]{:S(2)}) collective-permute-start(f32[3,64,128]{2,1,0:T(8,128)S(1)} %get-tuple-element.26), channel_id=1, source_target_pairs={{0,1},{1,0},{2,3},{3,2},{4,8},{5,9},{6,10},{7,11},{8,4},{9,5},{10,... | collective-permute-start | bytes 294920 | tf_op jit(solution)/shard_map/ppermute | solution.py:466
  8.5 2.6 %all-to-all-start = ((f32[32,2,384]{2,1,0:T(2,128)}), f32[32,2,384]{2,1,0:T(2,128)S(1)}, u32[]{:S(2)}, u32[]{:S(2)}) async-start(f32[32,2,384]{2,1,0:T(2,128)} %get-tuple-element.23), calls=%async_computation | async-start | bytes 196608 | tf_op jit(solution)/shard_map/all_to_all | solution.py:449
  11.1 0.3 collective-permute-start.3
  11.4 0.0 collective-permute-done.a_ref
  11.4 0.0 collective-permute-done.1.b_ref
  11.4 0.0 collective-permute-done.2._.down_ref
  11.4 0.2 shard_map.69
  11.6 0.3 %collective-permute-start.4 = (f32[3,64,128]{2,1,0:T(8,128)S(1)}, f32[3,64,128]{2,1,0:T(8,128)S(1)}, u32[]{:S(2)}, u32[]{:S(2)}) collective-permute-start(f32[3,64,128]{2,1,0:T(8,128)S(1)} %get-tuple-element.30), channel_id=1, source_target_pairs={{0,4},{1,5},{2,6},{3,7},{4,0},{5,1},{6,2},{7,3},{8,12},{9,13},{10,... | collective-permute-start | bytes 294920 | tf_op jit(solution)/shard_map/ppermute | solution.py:466
  11.9 1.8 %collective-permute-start.5 = (f32[96,128]{1,0:T(8,128)S(1)}, f32[96,128]{1,0:T(8,128)S(1)}, u32[]{:S(2)}, u32[]{:S(2)}) collective-permute-start(f32[96,128]{1,0:T(8,128)S(1)} %get-tuple-element.31), channel_id=1, source_target_pairs={{0,1},{1,0},{2,3},{3,2},{4,8},{5,9},{6,10},{7,11},{8,4},{9,5},{10,... | collective-permute-start | bytes 147464 | tf_op jit(solution)/shard_map/ppermute | solution.py:466
  13.7 0.3 collective-permute-start.6
  14.0 0.0 collective-permute-done.3.up_ref
  14.0 0.0 copy-done
  14.0 0.6 %shard_map.70 = (f32[32,128]{1,0:T(8,128)S(1)}, f32[2,256,256]{2,1,0:T(8,128)S(1)}, f32[128,128]{1,0:T(8,128)S(1)}) custom-call(f32[3,128,256]{2,1,0:T(8,128)S(1)} %get-tuple-element.27.centre_ref, f32[3,64,128]{2,1,0:T(8,128)S(1)} %collective-permute-done.3.up_ref, f32[3,64,128]{2,1,0:T(8,128)S(1)} %collective-permute-done.2._.down_ref, ...), custom_call_target="tpu_custom_call" | custom-call | tf_op jit(solution)/shard_map/pallas_call | solution.py:512
  14.5 1.9 %collective-permute-done.5.first_ref = f32[96,128]{1,0:T(8,128)S(1)} collective-permute-done((f32[96,128]{1,0:T(8,128)S(1)}, f32[96,128]{1,0:T(8,128)S(1)}, u32[]{:S(2)}, u32[]{:S(2)}) %collective-permute-start.5) | collective-permute-done | bytes 49184 | tf_op jit(solution)/shard_map/ppermute | solution.py:466
  16.4 2.9 %all-to-all-done.bank_ref = f32[32,2,384]{2,1,0:T(2,128)S(1)} async-done(((f32[32,2,384]{2,1,0:T(2,128)}), f32[32,2,384]{2,1,0:T(2,128)S(1)}, u32[]{:S(2)}, u32[]{:S(2)}) %all-to-all-start) | async-done | bytes 98336 | tf_op jit(solution)/shard_map/all_to_all | solution.py:449
  19.3 0.0 collective-permute-done.4.up_margin_ref
  19.3 1.5 %shard_map.71 = (f32[12,32,128]{2,1,0:T(8,128)S(1)}, f32[6,64,256]{2,1,0:T(8,128)S(1)}, f32[128,256]{1,0:T(8,128)S(1)}) custom-call(f32[32,2,384]{2,1,0:T(2,128)S(1)} %all-to-all-done.bank_ref, f32[32,128]{1,0:T(8,128)S(1)} %get-tuple-element.29.spectrum_ref, f32[3,64,128]{2,1,0:T(8,128)S(1)} %collective-permute-done.4.up_margin_ref, ...), custom_call_target="tpu_custom_call" | custom-call | tf_op jit(solution)/shard_map/pallas_call | solution.py:530
  20.8 0.0 collective-permute-done.6.second_ref
  20.8 1.8 %shard_map.72 = (f32[128,128]{1,0:T(8,128)S(1)}, f32[32,2,128]{2,1,0:T(2,128)S(1)}) custom-call(f32[12,32,128]{2,1,0:T(8,128)S(1)} %get-tuple-element.32.spectra_ref, f32[6,64,256]{2,1,0:T(8,128)S(1)} %get-tuple-element.33.fields_ref, f32[128,256]{1,0:T(8,128)S(1)} %get-tuple-element.34.tall_ref, f32[2,256,256]{2,1,0:T(8,128)S(1)} %get-tuple-element.35.cells_ref, ...), custom_call_target="tpu_custom_call" | custom-call | tf_op jit(solution)/shard_map/pallas_call | solution.py:542
  22.6 9.3 %all_to_all.10.sums_ref = f32[32,2,128]{2,1,0:T(2,128)S(1)} all-to-all(f32[32,2,128]{2,1,0:T(2,128)S(1)} %get-tuple-element.39), channel_id=1, replica_groups=mesh['row'=8,'col'=4] {'row','col'}, dimensions={0} | all-to-all | bytes 65536 | tf_op jit(solution)/shard_map/all_to_all | solution.py:449
  31.9 0.7 %shard_map.73 = (f32[128,128]{1,0:T(8,128)}, f32[1,1]{1,0:T(1,128)}) custom-call(f32[3,128,128]{2,1,0:T(8,128)S(1)} %get-tuple-element.22.own_ref, f32[128,128]{1,0:T(8,128)S(1)} %get-tuple-element.38.cells_ref, f32[32,2,128]{2,1,0:T(2,128)S(1)} %all_to_all.10.sums_ref), custom_call_target="tpu_custom_call" | custom-call | tf_op jit(solution)/shard_map/pallas_call | solution.py:552
Async XLA Ops:
  0.6 13.4 %copy-start = (bf16[2496,256]{1,0:T(8,128)(2,1)S(1)}, bf16[2496,256]{1,0:T(8,128)(2,1)}, u32[]{:S(2)}) copy-start(bf16[2496,256]{1,0:T(8,128)(2,1)} %constant.1.clone.table_ref) | copy-start | bytes 3833860
  2.4 9.0 %collective-permute-start = (f32[192,128]{1,0:T(8,128)S(1)}, f32[192,128]{1,0:T(8,128)S(1)}, u32[]{:S(2)}, u32[]{:S(2)}) collective-permute-start(f32[192,128]{1,0:T(8,128)S(1)} %get-tuple-element.24), channel_id=1, source_target_pairs={{0,1},{1,0},{2,3},{3,2},{4,5},{5,4},{6,7},{7,6},{8,9},{9,8},{10,11... | collective-permute-start | bytes 294920 | tf_op jit(solution)/shard_map/ppermute | solution.py:466
  5.4 6.0 %collective-permute-start.1 = (f32[192,128]{1,0:T(8,128)S(1)}, f32[192,128]{1,0:T(8,128)S(1)}, u32[]{:S(2)}, u32[]{:S(2)}) collective-permute-start(f32[192,128]{1,0:T(8,128)S(1)} %get-tuple-element.25), channel_id=1, source_target_pairs={{0,4},{1,2},{2,1},{3,7},{4,0},{5,6},{6,5},{7,3},{8,12},{9,10},{10,... | collective-permute-start | bytes 294920 | tf_op jit(solution)/shard_map/ppermute | solution.py:466
  5.4 6.0 %collective-permute-start.2 = (f32[3,64,128]{2,1,0:T(8,128)S(1)}, f32[3,64,128]{2,1,0:T(8,128)S(1)}, u32[]{:S(2)}, u32[]{:S(2)}) collective-permute-start(f32[3,64,128]{2,1,0:T(8,128)S(1)} %get-tuple-element.26), channel_id=1, source_target_pairs={{0,1},{1,0},{2,3},{3,2},{4,8},{5,9},{6,10},{7,11},{8,4},{9,5},{10,... | collective-permute-start | bytes 294920 | tf_op jit(solution)/shard_map/ppermute | solution.py:466
  8.5 10.8 %all-to-all-start = ((f32[32,2,384]{2,1,0:T(2,128)}), f32[32,2,384]{2,1,0:T(2,128)S(1)}, u32[]{:S(2)}, u32[]{:S(2)}) async-start(f32[32,2,384]{2,1,0:T(2,128)} %get-tuple-element.23), calls=%async_computation | async-start | bytes 196608 | tf_op jit(solution)/shard_map/all_to_all | solution.py:449
  11.1 2.9 %collective-permute-start.3 = (f32[3,64,128]{2,1,0:T(8,128)S(1)}, f32[3,64,128]{2,1,0:T(8,128)S(1)}, u32[]{:S(2)}, u32[]{:S(2)}) collective-permute-start(f32[3,64,128]{2,1,0:T(8,128)S(1)} %get-tuple-element.28), channel_id=1, source_target_pairs={{0,4},{1,5},{2,6},{3,7},{4,0},{5,1},{6,2},{7,3},{8,12},{9,13},{10,... | collective-permute-start | bytes 294920 | tf_op jit(solution)/shard_map/ppermute | solution.py:466
  11.6 7.7 %collective-permute-start.4 = (f32[3,64,128]{2,1,0:T(8,128)S(1)}, f32[3,64,128]{2,1,0:T(8,128)S(1)}, u32[]{:S(2)}, u32[]{:S(2)}) collective-permute-start(f32[3,64,128]{2,1,0:T(8,128)S(1)} %get-tuple-element.30), channel_id=1, source_target_pairs={{0,4},{1,5},{2,6},{3,7},{4,0},{5,1},{6,2},{7,3},{8,12},{9,13},{10,... | collective-permute-start | bytes 294920 | tf_op jit(solution)/shard_map/ppermute | solution.py:466
  11.9 4.5 %collective-permute-start.5 = (f32[96,128]{1,0:T(8,128)S(1)}, f32[96,128]{1,0:T(8,128)S(1)}, u32[]{:S(2)}, u32[]{:S(2)}) collective-permute-start(f32[96,128]{1,0:T(8,128)S(1)} %get-tuple-element.31), channel_id=1, source_target_pairs={{0,1},{1,0},{2,3},{3,2},{4,8},{5,9},{6,10},{7,11},{8,4},{9,5},{10,... | collective-permute-start | bytes 147464 | tf_op jit(solution)/shard_map/ppermute | solution.py:466
  13.7 7.1 %collective-permute-start.6 = (f32[96,128]{1,0:T(8,128)S(1)}, f32[96,128]{1,0:T(8,128)S(1)}, u32[]{:S(2)}, u32[]{:S(2)}) collective-permute-start(f32[96,128]{1,0:T(8,128)S(1)} %get-tuple-element.37), channel_id=1, source_target_pairs={{0,1},{1,0},{2,3},{3,2},{4,8},{5,9},{6,10},{7,11},{8,4},{9,5},{10,... | collective-permute-start | bytes 147464 | tf_op jit(solution)/shard_map/ppermute | solution.py:466

commit v11 on v10

--- a/solution.py
+++ b/solution.py
@@ -437,8 +437,7 @@
     grad_ref[...] = cells
     square = jnp.sum(jnp.sum(cells * cells, axis=0, keepdims=True), axis=1, keepdims=True)
     loss = jnp.sum(jnp.sum(loss, axis=0, keepdims=True), axis=1, keepdims=True)
-    sums = jnp.concatenate([square, loss], axis=0)
-    sums_ref[...] = jnp.broadcast_to(sums[None], sums_ref.shape)
+    sums_ref[...] = jnp.broadcast_to(jnp.where(low, square, loss)[None], sums_ref.shape)
 
 
 def small(megabytes):
@@ -468,9 +467,11 @@
 
 def finish(cell_count, own_ref, cells_ref, sums_ref, logits_ref, loss_ref):
     total = jnp.sum(sums_ref[...], axis=0) / cell_count
-    scale = STEP / jnp.sqrt(total[0:1] + EPSILON)
+    low = lax.broadcasted_iota(jnp.int32, total.shape, 1) < LANES // 2
+    turned = pltpu.roll(total, LANES // 2, 1)
+    scale = STEP / jnp.sqrt(jnp.where(low, total, turned) + EPSILON)
     logits_ref[...] = own_ref[0] - cells_ref[...] * scale
-    loss_ref[...] = total[1:2, 0:1]
+    loss_ref[...] = turned[:, 0:1]
 
 
 def shards(mask_logits, target, weight, kernels):
@@ -541,7 +542,7 @@
     )(bank, spectrum, up_margin, first_margin, consts)
     grad_cells, sums = pl.pallas_call(
         functools.partial(backward_kernel, place),
-        out_shape=(struct(core_width, core_width), struct(rows * cols, 2, LANES)),
+        out_shape=(struct(core_width, core_width), struct(rows * cols, 1, LANES)),
         in_specs=[VMEM] * 9,
         out_specs=(VMEM,) * 2,
         compiler_params=small(16),

time: 32.8 us -> 32.7 us (level)
  no operation moved by 1% of the time
where the time goes in v11:
time: 32.7 us; the launch traced here: 32.5 us
  starting transfers between devices  11.4 us (35%)
  blocking collectives  9.2 us (28%)
  Pallas kernels  5.37 us (16%)
  waiting for transfers between devices  4.8 us (15%)
  other arithmetic  1.04 us (3%)
  between operations  0.68 us (2%)
    all_to_all x1, blocking collectives, to_all(): return lax.all_to_all(value, ('row', 'col'), 0, 0)  9.2 us
    ppermute x7, starting transfers between devices, pair_swap(): return lax.ppermute(value, ('row', 'col'), pairs)  8.84 us
    all_to_all x1, waiting for transfers between devices, to_all(): return lax.all_to_all(value, ('row', 'col'), 0, 0)  2.88 us
    all_to_all x1, starting transfers between devices, to_all(): return lax.all_to_all(value, ('row', 'col'), 0, 0)  2.55 us
    ppermute x7, waiting for transfers between devices, pair_swap(): return lax.ppermute(value, ('row', 'col'), pairs)  1.92 us
    pallas_call x1, Pallas kernels, shards(): pl.pallas_call(functools.partial(backward_kernel, place), out_shape=(stru...  1.71 us
    pallas_call x1, Pallas kernels, shards(): pl.pallas_call(functools.partial(forward_kernel, order, place), out_shape...  1.48 us
    concatenate x1, other arithmetic, shards(): jnp.concatenate([cells, shard], axis=0)  1.04 us
  transfers between devices with their start and end apart: 8, of which 2 were waited for; matrix products, arithmetic and copies ran while one was open for 0% of the time, Pallas kernels for 7%

profile of v11, /device:TPU:0, one launch (start us, length us, event | category | flops | bytes accessed | tf_op | source)
XLA Modules:
  0.0 32.5 jit_solution(12448041102498652180)
XLA Ops:
  0.6 0.0 copy-start
  0.6 1.0 %pad_maximum_fusion.held_ref = f32[130,384]{1,0:T(8,128)S(1)} fusion(f32[2,384]{1,0:T(2,128)} %param.8, f32[128,128]{1,0:T(8,128)} %param.7, f32[128,128]{1,0:T(8,128)} %param.6, f32[128,128]{1,0:T(8,128)} %param.5), kind=kLoop, calls=%fused_computation | loop fusion | flops 149760 | bytes 399360 | tf_op jit(solution)/shard_map/concatenate | solution.py:498
  1.7 0.7 %shard_map.68 = (f32[3,128,128]{2,1,0:T(8,128)S(1)}, f32[192,128]{1,0:T(8,128)S(1)}, f32[192,128]{1,0:T(8,128)S(1)}, f32[3,64,128]{2,1,0:T(8,128)S(1)}, f32[3,64...) custom-call(f32[130,384]{1,0:T(8,128)S(1)} %pad_maximum_fusion.held_ref), custom_call_target="tpu_custom_call" | custom-call | tf_op jit(solution)/shard_map/pallas_call | solution.py:491
  2.4 3.0 %collective-permute-start = (f32[192,128]{1,0:T(8,128)S(1)}, f32[192,128]{1,0:T(8,128)S(1)}, u32[]{:S(2)}, u32[]{:S(2)}) collective-permute-start(f32[192,128]{1,0:T(8,128)S(1)} %get-tuple-element.24), channel_id=1, source_target_pairs={{0,1},{1,0},{2,3},{3,2},{4,5},{5,4},{6,7},{7,6},{8,9},{9,8},{10,11... | collective-permute-start | bytes 294920 | tf_op jit(solution)/shard_map/ppermute | solution.py:465
  5.4 0.0 collective-permute-start.1
  5.4 3.1 %collective-permute-start.2 = (f32[3,64,128]{2,1,0:T(8,128)S(1)}, f32[3,64,128]{2,1,0:T(8,128)S(1)}, u32[]{:S(2)}, u32[]{:S(2)}) collective-permute-start(f32[3,64,128]{2,1,0:T(8,128)S(1)} %get-tuple-element.26), channel_id=1, source_target_pairs={{0,1},{1,0},{2,3},{3,2},{4,8},{5,9},{6,10},{7,11},{8,4},{9,5},{10,... | collective-permute-start | bytes 294920 | tf_op jit(solution)/shard_map/ppermute | solution.py:465
  8.5 2.6 %all-to-all-start = ((f32[32,2,384]{2,1,0:T(2,128)}), f32[32,2,384]{2,1,0:T(2,128)S(1)}, u32[]{:S(2)}, u32[]{:S(2)}) async-start(f32[32,2,384]{2,1,0:T(2,128)} %get-tuple-element.23), calls=%async_computation | async-start | bytes 196608 | tf_op jit(solution)/shard_map/all_to_all | solution.py:448
  11.1 0.3 collective-permute-start.3
  11.4 0.0 collective-permute-done.a_ref
  11.4 0.0 collective-permute-done.1.b_ref
  11.4 0.0 collective-permute-done.2._.down_ref
  11.4 0.2 shard_map.69
  11.6 0.3 %collective-permute-start.4 = (f32[3,64,128]{2,1,0:T(8,128)S(1)}, f32[3,64,128]{2,1,0:T(8,128)S(1)}, u32[]{:S(2)}, u32[]{:S(2)}) collective-permute-start(f32[3,64,128]{2,1,0:T(8,128)S(1)} %get-tuple-element.30), channel_id=1, source_target_pairs={{0,4},{1,5},{2,6},{3,7},{4,0},{5,1},{6,2},{7,3},{8,12},{9,13},{10,... | collective-permute-start | bytes 294920 | tf_op jit(solution)/shard_map/ppermute | solution.py:465
  11.9 1.8 %collective-permute-start.5 = (f32[96,128]{1,0:T(8,128)S(1)}, f32[96,128]{1,0:T(8,128)S(1)}, u32[]{:S(2)}, u32[]{:S(2)}) collective-permute-start(f32[96,128]{1,0:T(8,128)S(1)} %get-tuple-element.31), channel_id=1, source_target_pairs={{0,1},{1,0},{2,3},{3,2},{4,8},{5,9},{6,10},{7,11},{8,4},{9,5},{10,... | collective-permute-start | bytes 147464 | tf_op jit(solution)/shard_map/ppermute | solution.py:465
  13.7 0.3 collective-permute-start.6
  14.0 0.0 collective-permute-done.3.up_ref
  14.0 0.0 copy-done
  14.0 0.6 %shard_map.70 = (f32[32,128]{1,0:T(8,128)S(1)}, f32[2,256,256]{2,1,0:T(8,128)S(1)}, f32[128,128]{1,0:T(8,128)S(1)}) custom-call(f32[3,128,256]{2,1,0:T(8,128)S(1)} %get-tuple-element.27.centre_ref, f32[3,64,128]{2,1,0:T(8,128)S(1)} %collective-permute-done.3.up_ref, f32[3,64,128]{2,1,0:T(8,128)S(1)} %collective-permute-done.2._.down_ref, ...), custom_call_target="tpu_custom_call" | custom-call | tf_op jit(solution)/shard_map/pallas_call | solution.py:513
  14.5 1.9 %collective-permute-done.5.first_ref = f32[96,128]{1,0:T(8,128)S(1)} collective-permute-done((f32[96,128]{1,0:T(8,128)S(1)}, f32[96,128]{1,0:T(8,128)S(1)}, u32[]{:S(2)}, u32[]{:S(2)}) %collective-permute-start.5) | collective-permute-done | bytes 49184 | tf_op jit(solution)/shard_map/ppermute | solution.py:465
  16.4 2.9 %all-to-all-done.bank_ref = f32[32,2,384]{2,1,0:T(2,128)S(1)} async-done(((f32[32,2,384]{2,1,0:T(2,128)}), f32[32,2,384]{2,1,0:T(2,128)S(1)}, u32[]{:S(2)}, u32[]{:S(2)}) %all-to-all-start) | async-done | bytes 98336 | tf_op jit(solution)/shard_map/all_to_all | solution.py:448
  19.3 0.0 collective-permute-done.4.up_margin_ref
  19.3 1.5 %shard_map.71 = (f32[12,32,128]{2,1,0:T(8,128)S(1)}, f32[6,64,256]{2,1,0:T(8,128)S(1)}, f32[128,256]{1,0:T(8,128)S(1)}) custom-call(f32[32,2,384]{2,1,0:T(2,128)S(1)} %all-to-all-done.bank_ref, f32[32,128]{1,0:T(8,128)S(1)} %get-tuple-element.29.spectrum_ref, f32[3,64,128]{2,1,0:T(8,128)S(1)} %collective-permute-done.4.up_margin_ref, ...), custom_call_target="tpu_custom_call" | custom-call | tf_op jit(solution)/shard_map/pallas_call | solution.py:531
  20.8 0.0 collective-permute-done.6.second_ref
  20.8 1.7 %shard_map.72 = (f32[128,128]{1,0:T(8,128)S(1)}, f32[32,1,128]{2,1,0:T(1,128)S(1)}) custom-call(f32[12,32,128]{2,1,0:T(8,128)S(1)} %get-tuple-element.32.spectra_ref, f32[6,64,256]{2,1,0:T(8,128)S(1)} %get-tuple-element.33.fields_ref, f32[128,256]{1,0:T(8,128)S(1)} %get-tuple-element.34.tall_ref, f32[2,256,256]{2,1,0:T(8,128)S(1)} %get-tuple-element.35.cells_ref, ...), custom_call_target="tpu_custom_call" | custom-call | tf_op jit(solution)/shard_map/pallas_call | solution.py:543
  22.5 9.2 %all_to_all.10.sums_ref = f32[32,1,128]{2,1,0:T(1,128)S(1)} all-to-all(f32[32,1,128]{2,1,0:T(1,128)S(1)} %get-tuple-element.39), channel_id=1, replica_groups=mesh['row'=8,'col'=4] {'row','col'}, dimensions={0} | all-to-all | bytes 32768 | tf_op jit(solution)/shard_map/all_to_all | solution.py:448
  31.7 0.8 %shard_map.73 = (f32[128,128]{1,0:T(8,128)}, f32[1,1]{1,0:T(1,128)}) custom-call(f32[3,128,128]{2,1,0:T(8,128)S(1)} %get-tuple-element.22.own_ref, f32[128,128]{1,0:T(8,128)S(1)} %get-tuple-element.38.cells_ref, f32[32,1,128]{2,1,0:T(1,128)S(1)} %all_to_all.10.sums_ref), custom_call_target="tpu_custom_call" | custom-call | tf_op jit(solution)/shard_map/pallas_call | solution.py:553
Async XLA Ops:
  0.6 13.4 %copy-start = (bf16[2496,256]{1,0:T(8,128)(2,1)S(1)}, bf16[2496,256]{1,0:T(8,128)(2,1)}, u32[]{:S(2)}) copy-start(bf16[2496,256]{1,0:T(8,128)(2,1)} %constant.1.clone.table_ref) | copy-start | bytes 3833860
  2.4 9.0 %collective-permute-start = (f32[192,128]{1,0:T(8,128)S(1)}, f32[192,128]{1,0:T(8,128)S(1)}, u32[]{:S(2)}, u32[]{:S(2)}) collective-permute-start(f32[192,128]{1,0:T(8,128)S(1)} %get-tuple-element.24), channel_id=1, source_target_pairs={{0,1},{1,0},{2,3},{3,2},{4,5},{5,4},{6,7},{7,6},{8,9},{9,8},{10,11... | collective-permute-start | bytes 294920 | tf_op jit(solution)/shard_map/ppermute | solution.py:465
  5.4 6.0 %collective-permute-start.1 = (f32[192,128]{1,0:T(8,128)S(1)}, f32[192,128]{1,0:T(8,128)S(1)}, u32[]{:S(2)}, u32[]{:S(2)}) collective-permute-start(f32[192,128]{1,0:T(8,128)S(1)} %get-tuple-element.25), channel_id=1, source_target_pairs={{0,4},{1,2},{2,1},{3,7},{4,0},{5,6},{6,5},{7,3},{8,12},{9,10},{10,... | collective-permute-start | bytes 294920 | tf_op jit(solution)/shard_map/ppermute | solution.py:465
  5.4 6.0 %collective-permute-start.2 = (f32[3,64,128]{2,1,0:T(8,128)S(1)}, f32[3,64,128]{2,1,0:T(8,128)S(1)}, u32[]{:S(2)}, u32[]{:S(2)}) collective-permute-start(f32[3,64,128]{2,1,0:T(8,128)S(1)} %get-tuple-element.26), channel_id=1, source_target_pairs={{0,1},{1,0},{2,3},{3,2},{4,8},{5,9},{6,10},{7,11},{8,4},{9,5},{10,... | collective-permute-start | bytes 294920 | tf_op jit(solution)/shard_map/ppermute | solution.py:465
  8.5 10.8 %all-to-all-start = ((f32[32,2,384]{2,1,0:T(2,128)}), f32[32,2,384]{2,1,0:T(2,128)S(1)}, u32[]{:S(2)}, u32[]{:S(2)}) async-start(f32[32,2,384]{2,1,0:T(2,128)} %get-tuple-element.23), calls=%async_computation | async-start | bytes 196608 | tf_op jit(solution)/shard_map/all_to_all | solution.py:448
  11.1 2.9 %collective-permute-start.3 = (f32[3,64,128]{2,1,0:T(8,128)S(1)}, f32[3,64,128]{2,1,0:T(8,128)S(1)}, u32[]{:S(2)}, u32[]{:S(2)}) collective-permute-start(f32[3,64,128]{2,1,0:T(8,128)S(1)} %get-tuple-element.28), channel_id=1, source_target_pairs={{0,4},{1,5},{2,6},{3,7},{4,0},{5,1},{6,2},{7,3},{8,12},{9,13},{10,... | collective-permute-start | bytes 294920 | tf_op jit(solution)/shard_map/ppermute | solution.py:465
  11.6 7.7 %collective-permute-start.4 = (f32[3,64,128]{2,1,0:T(8,128)S(1)}, f32[3,64,128]{2,1,0:T(8,128)S(1)}, u32[]{:S(2)}, u32[]{:S(2)}) collective-permute-start(f32[3,64,128]{2,1,0:T(8,128)S(1)} %get-tuple-element.30), channel_id=1, source_target_pairs={{0,4},{1,5},{2,6},{3,7},{4,0},{5,1},{6,2},{7,3},{8,12},{9,13},{10,... | collective-permute-start | bytes 294920 | tf_op jit(solution)/shard_map/ppermute | solution.py:465
  11.9 4.5 %collective-permute-start.5 = (f32[96,128]{1,0:T(8,128)S(1)}, f32[96,128]{1,0:T(8,128)S(1)}, u32[]{:S(2)}, u32[]{:S(2)}) collective-permute-start(f32[96,128]{1,0:T(8,128)S(1)} %get-tuple-element.31), channel_id=1, source_target_pairs={{0,1},{1,0},{2,3},{3,2},{4,8},{5,9},{6,10},{7,11},{8,4},{9,5},{10,... | collective-permute-start | bytes 147464 | tf_op jit(solution)/shard_map/ppermute | solution.py:465
  13.7 7.1 %collective-permute-start.6 = (f32[96,128]{1,0:T(8,128)S(1)}, f32[96,128]{1,0:T(8,128)S(1)}, u32[]{:S(2)}, u32[]{:S(2)}) collective-permute-start(f32[96,128]{1,0:T(8,128)S(1)} %get-tuple-element.37), channel_id=1, source_target_pairs={{0,1},{1,0},{2,3},{3,2},{4,8},{5,9},{6,10},{7,11},{8,4},{9,5},{10,... | collective-permute-start | bytes 147464 | tf_op jit(solution)/shard_map/ppermute | solution.py:465
